TPU v7x, 32 devices: a whole 2x2x4 slice. The times are simulated.
32 devices in a mesh: dp: 8 (over y, x, core), mp: 4 (over z).
Axes of the slice: x: 2, y: 2, z: 4, core: 2. Of those that a mesh axis runs over, the one named last changes fastest.
Arguments:
- block_input: float32 [16384, 1024], P(('dp', 'mp')), may hold values from -6 to 6
- lengths: int32 [8], P('dp'), may hold values from 1537 to 2048, as said below
- mixer_gain: float32 [1024], replicated, may hold values from 0.5 to 1.5
- mixer_shift: float32 [1024], replicated, may hold values from -1.25 to 1.25
- input_weight: bfloat16 [1024, 3, 1024], P(None, None, 'mp'), may hold values from -0.1875 to 0.1875
- input_bias: float32 [3, 1024], P(None, 'mp'), may hold values from -1.25 to 1.25
- conv_weight: float32 [3, 3, 1024], P(None, None, 'mp'), may hold values from -3.5 to 3.5
- conv_bias: float32 [3, 1024], P(None, 'mp'), may hold values from -1.25 to 1.25
- enter_weight: float32 [33, 64], replicated, may hold values from -3.5 to 3.5
- enter_bias: float32 [64], replicated, may hold values from -3.140625 to 3.140625
- middle_weight: float32 [64, 64], replicated, may hold values from -1.5 to 1.5
- middle_bias: float32 [64], replicated, may hold values from -3.140625 to 3.140625
- inner_weight: float32 [64, 64], replicated, may hold values from -1.5 to 1.5
- inner_bias: float32 [64], replicated, may hold values from -3.140625 to 3.140625
- frequency: float32 [64], replicated, may hold values from 0.5 to 1.5
- filter_weight: float32 [64, 1024], P(None, 'mp'), may hold values from -0.015625 to 0.015625
- skip_scale: float32 [1024], P('mp'), may hold values from -6 to 6
- output_weight: bfloat16 [1024, 1024], P('mp'), may hold values from -0.1875 to 0.1875
- output_bias: float32 [1024], replicated, may hold values from -1.25 to 1.25
- feed_gain: float32 [1024], replicated, may hold values from 0.5 to 1.5
- feed_shift: float32 [1024], replicated, may hold values from -1.25 to 1.25
- expand_weight: bfloat16 [1024, 4096], P(None, 'mp'), may hold values from -0.1875 to 0.1875
- expand_bias: float32 [4096], P('mp'), may hold values from -1.25 to 1.25
- reduce_weight: bfloat16 [4096, 1024], P('mp'), may hold values from -0.09375 to 0.09375
- reduce_bias: float32 [1024], replicated, may hold values from -1.25 to 1.25
- cotangent: float32 [16384, 1024], P(('dp', 'mp')), may hold values from -6 to 6
Outputs:
- result: float32 [16384, 1024], P(('dp', 'mp'))
- input_grad: float32 [16384, 1024], P(('dp', 'mp'))
- mixer_gain_grad: float32 [1024], replicated
- mixer_shift_grad: float32 [1024], replicated
- input_weight_grad: float32 [1024, 3, 1024], P(None, None, 'mp')
- input_bias_grad: float32 [3, 1024], P(None, 'mp')
- conv_weight_grad: float32 [3, 3, 1024], P(None, None, 'mp')
- conv_bias_grad: float32 [3, 1024], P(None, 'mp')
- enter_weight_grad: float32 [33, 64], replicated
- enter_bias_grad: float32 [64], replicated
- middle_weight_grad: float32 [64, 64], replicated
- middle_bias_grad: float32 [64], replicated
- inner_weight_grad: float32 [64, 64], replicated
- inner_bias_grad: float32 [64], replicated
- frequency_grad: float32 [64], replicated
- filter_weight_grad: float32 [64, 1024], P(None, 'mp')
- skip_scale_grad: float32 [1024], P('mp')
- output_weight_grad: float32 [1024, 1024], P('mp')
- output_bias_grad: float32 [1024], replicated
- feed_gain_grad: float32 [1024], replicated
- feed_shift_grad: float32 [1024], replicated
- expand_weight_grad: float32 [1024, 4096], P(None, 'mp')
- expand_bias_grad: float32 [4096], P('mp')
- reduce_weight_grad: float32 [4096, 1024], P('mp')
- reduce_bias_grad: float32 [1024], replicated
Inputs may be any that keep to these rules, and one draw needn't show every extreme that they name: `lengths`: each sequence uses more than three quarters of its 2048 slots; in every draw some sequence uses all of them.
All inputs are finite; a program needn't handle non-finite values.
Results may differ from a plain program's by a relative error of at most 0.017.
Values may be sent and summed in bfloat16 or wider, within the bound.
No kernel may reach another device: no remote copies, remote signals or barrier semaphores. Data moves between devices by JAX's collectives and lax.ppermute only.
A program may use at most 192 MiB of HBM per device.

v0:
```python
import math

import jax
import jax.numpy as jnp
from jax import lax
from jax.sharding import PartitionSpec as P

HIGHEST_MODE = lax.Precision.HIGHEST
EPSILON = 1e-05
FIRST_FACTOR = 64


def layer_norm(values_in, gain, shift):
    row_mean = jnp.mean(values_in, axis=-1, keepdims=True)
    centred = values_in - row_mean
    variance = jnp.mean(centred * centred, axis=-1, keepdims=True)
    return centred * lax.rsqrt(variance + EPSILON) * gain + shift


def short_conv(projected, conv_weight, conv_bias):
    one_back = jnp.pad(projected, ((1, 0), (0, 0), (0, 0)))[:-1]
    two_back = jnp.pad(projected, ((2, 0), (0, 0), (0, 0)))[:-2]
    return (
        conv_weight[0] * projected
        + conv_weight[1] * one_back
        + conv_weight[2] * two_back
        + conv_bias
    )


def position_features(total, emb_count):
    place = jnp.arange(total, dtype=jnp.float32)
    time_grid = place / (total - 1)
    bands = (emb_count - 1) // 2
    freq_grid = 0.0001 + jnp.arange(bands, dtype=jnp.float32) * ((bands - 1 - 0.0001) / (bands - 1))
    angles = 2.0 * math.pi / total * place[:, None] * freq_grid[None, :]
    return (
        jnp.concatenate([time_grid[:, None], jnp.cos(angles), -jnp.sin(angles)], axis=1),
        time_grid,
    )


def decay_table(time_grid, channel_ids, channel_total):
    slowest = math.log(0.01) / 1.5
    fastest = math.log(0.01) / 0.3
    rates = jnp.abs(
        slowest + (fastest - slowest) * channel_ids.astype(jnp.float32) / (channel_total - 1)
    )
    return jnp.exp(-time_grid[:, None] * rates[None, :])


def filter_bank(filter_weights, features, decay_rows):
    (
        enter_weight,
        enter_bias,
        middle_weight,
        middle_bias,
        inner_weight,
        inner_bias,
        frequency,
        filter_weight,
    ) = filter_weights
    hidden = jnp.sin(
        frequency * (jnp.dot(features, enter_weight, precision=HIGHEST_MODE) + enter_bias)
    )
    hidden = jnp.sin(
        frequency * (jnp.dot(hidden, middle_weight, precision=HIGHEST_MODE) + middle_bias)
    )
    hidden = jnp.sin(
        frequency * (jnp.dot(hidden, inner_weight, precision=HIGHEST_MODE) + inner_bias)
    )
    return jnp.dot(hidden, filter_weight, precision=HIGHEST_MODE) * decay_rows


def rounded(values_in):
    return lax.optimization_barrier(values_in.astype(jnp.bfloat16)).astype(jnp.float32)


def dft_tables(count):
    grid_index = jnp.arange(count, dtype=jnp.int32)
    phase = grid_index[:, None] * grid_index[None, :] % count
    angle = phase.astype(jnp.float32) * (2.0 * math.pi / count)
    return (jnp.cos(angle), -jnp.sin(angle))


def spectral_tables(seq_len):
    total = 2 * seq_len
    rows_count = FIRST_FACTOR
    cols_count = total // rows_count
    first_re, first_im = dft_tables(rows_count)
    second_re, second_im = dft_tables(cols_count)
    grid_rows = jnp.arange(rows_count, dtype=jnp.int32)[:, None]
    grid_cols = jnp.arange(cols_count, dtype=jnp.int32)[None, :]
    phase = (grid_rows * grid_cols % total).astype(jnp.float32) * (2.0 * math.pi / total)
    return (
        first_re,
        first_im,
        second_re,
        second_im,
        jnp.cos(phase)[:, :, None],
        -jnp.sin(phase)[:, :, None],
    )


def forward_dft(tables, signal):
    first_re, first_im, second_re, second_im, twist_re, twist_im = tables
    half_rows = first_re.shape[0] // 2
    cols_count = second_re.shape[0]
    blocks = signal.reshape(half_rows, cols_count, signal.shape[1])
    section_re = jnp.einsum("kn,nmc->kmc", first_re[:, :half_rows], blocks, precision=HIGHEST_MODE)
    section_im = jnp.einsum("kn,nmc->kmc", first_im[:, :half_rows], blocks, precision=HIGHEST_MODE)
    turned_re = section_re * twist_re - section_im * twist_im
    turned_im = section_re * twist_im + section_im * twist_re
    out_re = jnp.einsum("kmc,mj->kjc", turned_re, second_re, precision=HIGHEST_MODE) - jnp.einsum(
        "kmc,mj->kjc", turned_im, second_im, precision=HIGHEST_MODE
    )
    out_im = jnp.einsum("kmc,mj->kjc", turned_re, second_im, precision=HIGHEST_MODE) + jnp.einsum(
        "kmc,mj->kjc", turned_im, second_re, precision=HIGHEST_MODE
    )
    return (out_re, out_im)


def inverse_dft(tables, spec_re, spec_im):
    first_re, first_im, second_re, second_im, twist_re, twist_im = tables
    rows_count = first_re.shape[0]
    half_rows = rows_count // 2
    cols_count = second_re.shape[0]
    back_re = jnp.einsum("kjc,jm->kmc", spec_re, second_re, precision=HIGHEST_MODE) + jnp.einsum(
        "kjc,jm->kmc", spec_im, second_im, precision=HIGHEST_MODE
    )
    back_im = jnp.einsum("kjc,jm->kmc", spec_im, second_re, precision=HIGHEST_MODE) - jnp.einsum(
        "kjc,jm->kmc", spec_re, second_im, precision=HIGHEST_MODE
    )
    turn_re = back_re * twist_re + back_im * twist_im
    turn_im = back_im * twist_re - back_re * twist_im
    values_out = jnp.einsum(
        "nk,kmc->nmc", first_re[:half_rows], turn_re, precision=HIGHEST_MODE
    ) + jnp.einsum("nk,kmc->nmc", first_im[:half_rows], turn_im, precision=HIGHEST_MODE)
    values_out = values_out / (rows_count * cols_count)
    return values_out.reshape(half_rows * cols_count, values_out.shape[2])


def contract_rows(left, right):
    return lax.dot_general(
        left, right, (((0,), (0,)), ((), ())), preferred_element_type=jnp.float32
    )


def contract_cols(left, right):
    return lax.dot_general(
        left, right, (((1,), (1,)), ((), ())), preferred_element_type=jnp.float32
    )


def per_device(
    block_input,
    lengths,
    mixer_gain,
    mixer_shift,
    input_weight,
    input_bias,
    conv_weight,
    conv_bias,
    enter_weight,
    enter_bias,
    middle_weight,
    middle_bias,
    inner_weight,
    inner_bias,
    frequency,
    filter_weight,
    skip_scale,
    output_weight,
    output_bias,
    feed_gain,
    feed_shift,
    expand_weight,
    expand_bias,
    reduce_weight,
    reduce_bias,
    cotangent,
):
    own_rows = block_input.shape[0]
    feature_count = block_input.shape[1]
    channels = input_weight.shape[2]
    seq_len = own_rows * lax.axis_size("mp")
    mixer_normed = layer_norm(block_input, mixer_gain, mixer_shift).astype(jnp.bfloat16)
    mixer_rows = lax.all_gather(mixer_normed, "mp", axis=0, tiled=True)
    enter_flat = input_weight.reshape(feature_count, 3 * channels)
    projected = (
        jnp.dot(mixer_rows, enter_flat, preferred_element_type=jnp.float32).reshape(
            seq_len, 3, channels
        )
        + input_bias
    )
    mixed_in, conv_back = jax.vjp(short_conv, projected, conv_weight, conv_bias)
    value_path = mixed_in[:, 0]
    first_gate = mixed_in[:, 1]
    second_gate = mixed_in[:, 2]
    conv_input = rounded(first_gate * value_path)
    features, time_grid = position_features(seq_len, enter_weight.shape[0])
    channel_ids = lax.axis_index("mp") * channels + jnp.arange(channels, dtype=jnp.int32)
    decay_rows = decay_table(time_grid, channel_ids, feature_count)
    filter_weights = (
        enter_weight,
        enter_bias,
        middle_weight,
        middle_bias,
        inner_weight,
        inner_bias,
        frequency,
        filter_weight,
    )

    def local_bank(weight_set):
        return filter_bank(weight_set, features, decay_rows)

    filter_taps, bank_back = jax.vjp(local_bank, filter_weights)
    tables = spectral_tables(seq_len)
    taps_re, taps_im = forward_dft(tables, rounded(filter_taps))
    input_re, input_im = forward_dft(tables, conv_input)
    long_out = inverse_dft(
        tables, input_re * taps_re - input_im * taps_im, input_re * taps_im + input_im * taps_re
    )
    conv_out = long_out + skip_scale * conv_input
    positions = jnp.arange(seq_len, dtype=jnp.int32)
    row_mask = (positions < lengths[0]).astype(jnp.float32)[:, None]
    gated = (row_mask * second_gate * conv_out).astype(jnp.bfloat16)
    mixed = lax.psum_scatter(
        jnp.dot(gated, output_weight, preferred_element_type=jnp.float32).astype(jnp.bfloat16),
        "mp",
        scatter_dimension=0,
        tiled=True,
    ).astype(jnp.float32)
    hidden_res = block_input + mixed + output_bias
    feed_normed = layer_norm(hidden_res, feed_gain, feed_shift).astype(jnp.bfloat16)
    feed_rows = lax.all_gather(feed_normed, "mp", axis=0, tiled=True)
    pre_act = jnp.dot(feed_rows, expand_weight, preferred_element_type=jnp.float32) + expand_bias
    activated = jax.nn.gelu(pre_act, approximate=True).astype(jnp.bfloat16)
    result = (
        hidden_res
        + lax.psum_scatter(
            jnp.dot(activated, reduce_weight, preferred_element_type=jnp.float32).astype(
                jnp.bfloat16
            ),
            "mp",
            scatter_dimension=0,
            tiled=True,
        ).astype(jnp.float32)
        + reduce_bias
    )
    out_low = cotangent.astype(jnp.bfloat16)
    piece = lax.all_gather(out_low, "mp", axis=0, tiled=True)
    act_grad = contract_cols(piece, reduce_weight)
    act_grad, reduce_weight_grad = (act_grad, contract_rows(activated, piece))
    reduce_bias_grad = jnp.sum(cotangent, axis=0)
    _, gelu_back = jax.vjp(lambda pre_value: jax.nn.gelu(pre_value, approximate=True), pre_act)
    pre_grad = gelu_back(act_grad)[0].astype(jnp.bfloat16)
    expand_weight_grad = contract_rows(feed_rows, pre_grad)
    expand_bias_grad = jnp.sum(pre_grad.astype(jnp.float32), axis=0)
    feed_normed_grad = lax.psum_scatter(
        contract_cols(pre_grad, expand_weight), "mp", scatter_dimension=0, tiled=True
    )
    _, feed_norm_back = jax.vjp(layer_norm, hidden_res, feed_gain, feed_shift)
    res_part, feed_gain_grad, feed_shift_grad = feed_norm_back(feed_normed_grad)
    hidden_grad = cotangent + res_part
    output_bias_grad = jnp.sum(hidden_grad, axis=0)
    mix_low = hidden_grad.astype(jnp.bfloat16)
    piece = lax.all_gather(mix_low, "mp", axis=0, tiled=True)
    gated_grad = contract_cols(piece, output_weight)
    gated_grad, output_weight_grad = (gated_grad, contract_rows(gated, piece))
    masked_grad = gated_grad * row_mask
    second_grad = masked_grad * conv_out
    conv_grad = rounded(masked_grad * second_gate)
    skip_scale_grad = jnp.sum(conv_grad * conv_input, axis=0)
    grad_re, grad_im = forward_dft(tables, conv_grad)
    conv_input_grad = inverse_dft(
        tables, grad_re * taps_re + grad_im * taps_im, grad_im * taps_re - grad_re * taps_im
    )
    conv_input_grad = conv_input_grad + skip_scale * conv_grad
    taps_grad = inverse_dft(
        tables, grad_re * input_re + grad_im * input_im, grad_im * input_re - grad_re * input_im
    )
    mixed_grad = jnp.stack(
        [conv_input_grad * first_gate, conv_input_grad * value_path, second_grad], axis=1
    )
    projected_grad, conv_weight_grad, conv_bias_grad = conv_back(mixed_grad)
    projected_low = projected_grad.astype(jnp.bfloat16).reshape(seq_len, 3 * channels)
    input_weight_grad = contract_rows(mixer_rows, projected_low).reshape(feature_count, 3, channels)
    input_bias_grad = jnp.sum(projected_low.astype(jnp.float32), axis=0).reshape(3, channels)
    (
        enter_weight_grad,
        enter_bias_grad,
        middle_weight_grad,
        middle_bias_grad,
        inner_weight_grad,
        inner_bias_grad,
        frequency_grad,
        filter_weight_grad,
    ) = bank_back(taps_grad)[0]
    mixer_normed_grad = lax.psum_scatter(
        contract_cols(projected_low, enter_flat).astype(jnp.bfloat16),
        "mp",
        scatter_dimension=0,
        tiled=True,
    ).astype(jnp.float32)
    _, mixer_norm_back = jax.vjp(layer_norm, block_input, mixer_gain, mixer_shift)
    input_part, mixer_gain_grad, mixer_shift_grad = mixer_norm_back(mixer_normed_grad)
    input_grad = hidden_grad + input_part
    (
        input_weight_grad,
        input_bias_grad,
        conv_weight_grad,
        conv_bias_grad,
        filter_weight_grad,
        skip_scale_grad,
        output_weight_grad,
        expand_weight_grad,
        expand_bias_grad,
        reduce_weight_grad,
    ) = lax.psum(
        (
            input_weight_grad,
            input_bias_grad,
            conv_weight_grad,
            conv_bias_grad,
            filter_weight_grad,
            skip_scale_grad,
            output_weight_grad,
            expand_weight_grad,
            expand_bias_grad,
            reduce_weight_grad,
        ),
        "dp",
    )
    (
        mixer_gain_grad,
        mixer_shift_grad,
        output_bias_grad,
        feed_gain_grad,
        feed_shift_grad,
        reduce_bias_grad,
        enter_weight_grad,
        enter_bias_grad,
        middle_weight_grad,
        middle_bias_grad,
        inner_weight_grad,
        inner_bias_grad,
        frequency_grad,
    ) = lax.psum(
        (
            mixer_gain_grad,
            mixer_shift_grad,
            output_bias_grad,
            feed_gain_grad,
            feed_shift_grad,
            reduce_bias_grad,
            enter_weight_grad,
            enter_bias_grad,
            middle_weight_grad,
            middle_bias_grad,
            inner_weight_grad,
            inner_bias_grad,
            frequency_grad,
        ),
        ("dp", "mp"),
    )
    return (
        result,
        input_grad,
        mixer_gain_grad,
        mixer_shift_grad,
        input_weight_grad,
        input_bias_grad,
        conv_weight_grad,
        conv_bias_grad,
        enter_weight_grad,
        enter_bias_grad,
        middle_weight_grad,
        middle_bias_grad,
        inner_weight_grad,
        inner_bias_grad,
        frequency_grad,
        filter_weight_grad,
        skip_scale_grad,
        output_weight_grad,
        output_bias_grad,
        feed_gain_grad,
        feed_shift_grad,
        expand_weight_grad,
        expand_bias_grad,
        reduce_weight_grad,
        reduce_bias_grad,
    )


def solution(mesh):
    return jax.shard_map(
        per_device,
        mesh=mesh,
        in_specs=(
            P(("dp", "mp"), None),
            P("dp"),
            P(),
            P(),
            P(None, None, "mp"),
            P(None, "mp"),
            P(None, None, "mp"),
            P(None, "mp"),
            P(),
            P(),
            P(),
            P(),
            P(),
            P(),
            P(),
            P(None, "mp"),
            P("mp"),
            P("mp", None),
            P(),
            P(),
            P(),
            P(None, "mp"),
            P("mp"),
            P("mp", None),
            P(),
            P(("dp", "mp"), None),
        ),
        out_specs=(
            P(("dp", "mp"), None),
            P(("dp", "mp"), None),
            P(),
            P(),
            P(None, None, "mp"),
            P(None, "mp"),
            P(None, None, "mp"),
            P(None, "mp"),
            P(),
            P(),
            P(),
            P(),
            P(),
            P(),
            P(),
            P(None, "mp"),
            P("mp"),
            P("mp", None),
            P(),
            P(),
            P(),
            P(None, "mp"),
            P("mp"),
            P("mp", None),
            P(),
        ),
        check_vma=False,
    )
```

profile of v0, /device:TPU:1, one launch (start us, length us, event | category | flops | bytes accessed | tf_op | source)
XLA Modules:
  0.0 1358.0 jit_solution(14256849558126379127)
XLA Ops:
  24.2 4.1 fusion.84
  32.0 3.9 fusion.135
  35.9 61.4 %all-gather.5.cloned.1.call-done = bf16[2048,1024]{1,0:T(8,128)(2,1)} async-done(((bf16[512,1024]{1,0:T(8,128)(2,1)}), bf16[2048,1024]{1,0:T(8,128)(2,1)}) %all-gather.5.cloned.1.call-update) | async-done | bytes 4194320 | tf_op jit(solution)/shard_map/all_gather | solution.py:188
  97.3 5.7 fusion.80
  105.9 3.9 fusion.139
  109.9 3.9 fusion.137
  113.8 9.7 multiply_subtract_fusion.4
  123.5 6.0 fusion.64
  129.5 6.0 fusion.66
  135.6 7.2 fusion.72
  142.8 6.3 fusion.74
  149.1 7.1 fusion.96
  156.2 7.5 fusion.93
  163.7 7.2 fusion.87
  170.9 12.6 multiply_subtract_fusion.3
  185.5 4.2 fusion.48
  189.7 6.1 fusion.50
  195.7 4.2 fusion.44
  199.9 4.2 fusion.46
  204.1 11.5 fusion.39
  215.5 11.8 add_multiply_fusion.2
  234.2 75.4 %reduce-scatter.5.cloned.1.call-done = bf16[512,1024]{1,0:T(8,128)(2,1)} async-done(((bf16[2048,1024]{1,0:T(8,128)(2,1)}), bf16[512,1024]{1,0:T(8,128)(2,1)}) %reduce-scatter.5.cloned.1.call-update) | async-done | bytes 1048592 | tf_op jit(solution)/shard_map/reduce_scatter | solution.py:229
  309.6 5.2 fusion.317
  318.4 80.6 %all-gather.7.cloned.1.call-done = bf16[2048,1024]{1,0:T(8,128)(2,1)} async-done(((bf16[512,1024]{1,0:T(8,128)(2,1)}), bf16[2048,1024]{1,0:T(8,128)(2,1)}) %all-gather.7.cloned.1.call-update) | async-done | bytes 4194320 | tf_op jit(solution)/shard_map/all_gather | solution.py:237
  399.0 11.0 fusion.319
  410.0 70.4 %all-gather.9.cloned.1.call-done = bf16[2048,1024]{1,0:T(8,128)(2,1)} async-done(((bf16[512,1024]{1,0:T(8,128)(2,1)}), bf16[2048,1024]{1,0:T(8,128)(2,1)}) %all-gather.9.cloned.1.call-update) | async-done | bytes 4194320 | tf_op jit(solution)/shard_map/all_gather | solution.py:253
  480.4 13.4 convert_reduce_fusion
  495.9 6.9 fusion.320
  503.1 11.1 convolution_convert_fusion.1
  514.3 131.5 %reduce-scatter.9.cloned.1.call-done = f32[512,1024]{1,0:T(8,128)} async-done(((f32[2048,1024]{1,0:T(8,128)}), f32[512,1024]{1,0:T(8,128)}) %reduce-scatter.9.cloned.1.call-update) | async-done | bytes 2097168 | tf_op jit(solution)/shard_map/reduce_scatter | solution.py:261
  648.7 77.0 %reduce-scatter.7.cloned.1.call-done = bf16[512,1024]{1,0:T(8,128)(2,1)} async-done(((bf16[2048,1024]{1,0:T(8,128)(2,1)}), bf16[512,1024]{1,0:T(8,128)(2,1)}) %reduce-scatter.7.cloned.1.call-update) | async-done | bytes 1048592 | tf_op jit(solution)/shard_map/reduce_scatter | solution.py:242
  725.7 4.1 fusion.316
  733.3 81.4 %all-gather.11.cloned.1.call-done = bf16[2048,1024]{1,0:T(8,128)(2,1)} async-done(((bf16[512,1024]{1,0:T(8,128)(2,1)}), bf16[2048,1024]{1,0:T(8,128)(2,1)}) %all-gather.11.cloned.1.call-update) | async-done | bytes 4194320 | tf_op jit(solution)/shard_map/all_gather | solution.py:269
  814.7 5.8 multiply_convert_fusion.1
  825.5 7.5 fusion.56
  833.1 6.0 fusion.58
  839.1 7.2 fusion.99
  846.3 20.5 %multiply_add_fusion = (f32[64,64,256]{2,0,1:T(8,128)}, f32[64,64,256]{2,0,1:T(8,128)}, f32[64,64,256]{2,0,1:T(8,128)}, f32[64,64,256]{2,0,1:T(8,128)}) fusion(f32[64,64,256]{2,0,1:T(8,128)} %get-tuple-element.110, f32[64,64,256]{2,0,1:T(8,128)} %fusion.99, f32[64,64,256]{2,0,1:T(8,128)} %fusion.87, f32[64,64,256]{2,0,1:T(8,128)} %fusion.96, ...), kind=kOutput, calls=%fused_computation.84 | convolution fusion | flops 818999296 | bytes 46137344 | tf_op jit(solution)/shard_map/kmc,mj->kjc/dot_general | solution.py:117
  866.8 6.1 fusion.30
  872.9 4.2 fusion.32
  877.1 4.2 fusion.34
  881.2 4.2 fusion.36
  885.4 11.6 fusion.25
  897.1 11.6 add_multiply_fusion.1
  913.8 7.8 multiply_reduce_fusion.2
  921.6 5.3 convert_reduce_fusion.1
  928.5 5.2 bitcast_convert_fusion
  933.8 10.2 fusion.322
  944.1 11.5 fusion.311
  955.5 4.8 copy.166
  960.3 6.1 fusion.20
  966.4 4.2 fusion.22
  970.6 4.2 fusion.16
  974.7 4.2 fusion.18
  978.9 11.4 fusion.11
  990.3 11.8 add_multiply_fusion
  1004.0 3.5 fusion.145
  1011.1 5.2 fusion.52
  1017.8 23.7 %all-reduce.8 = (f32[3,256]{1,0:T(4,128)}, f32[3,3,256]{2,1,0:T(4,128)}, f32[3,256]{1,0:T(4,128)}, f32[256]{0:T(256)}, f32[1024]{0:T(1024)}) all-reduce(f32[3,256]{1,0:T(4,128)} %get-tuple-element.67, f32[3,3,256]{2,1,0:T(4,128)} %pad_add_fusion, f32[3,256]{1,0:T(4,128)S(1)} %get-tuple-element.28, ...), channel_id=1, replica_groups=mesh['dp'=8,'mp'=4] {'dp'}, use_global_device_ids=true, to_apply=%region_18.19 | all-reduce | flops 5120 | bytes 40960 | tf_op jit(solution)/shard_map/psum | solution.py:321
  1041.5 5.0 convolution_multiply_fusion.4
  1065.4 3.6 add_add_fusion.3
  1069.0 122.9 %all-reduce.15.cloned.1.call-done = (f32[1024,3,256]{2,0,1:T(8,128)}, f32[64,256]{1,0:T(8,128)}, f32[256,1024]{1,0:T(8,128)}, f32[1024,1024]{1,0:T(8,128)}, f32[1024,1024]{1,0:T(8,128)}) async-done(((f32[1024,3,256]{2,0,1:T(8,128)}, f32[64,256]{1,0:T(8,128)}, f32[256,1024]{1,0:T(8,128)}, f32[1024,1024]{1,0:T(8,128)}, f32[1024,1024]{1,0:T(8,128)}), (f32[1024,3,256]{2,0,1:T(8,128)}, f32[64,256]{1,0:T(8,128)}, ...) | async-done | bytes 12648464 | tf_op jit(solution)/shard_map/psum | solution.py:321
  1191.9 138.9 %all-reduce.13.cloned.1.call-done = (f32[1024]{0:T(1024)}, f32[1024]{0:T(1024)}, f32[33,64]{1,0:T(8,128)}, f32[64]{0:T(128)}, f32[64,64]{1,0:T(8,128)}, /*index=...) async-done(((f32[1024]{0:T(1024)}, f32[1024]{0:T(1024)}, ...) | async-done | bytes 66832 | tf_op jit(solution)/shard_map/psum | solution.py:350
  1333.4 3.9 copy.350
  (307 shorter events, 97.3 us)
Async XLA Ops:
  7.2 473.2 %copy-start = (bf16[1024,1024]{1,0:T(8,128)(2,1)S(1)}, bf16[1024,1024]{1,0:T(8,128)(2,1)}, u32[]{:S(2)}) copy-start(bf16[1024,1024]{1,0:T(8,128)(2,1)} %param.49) | copy-start | bytes 6291460
  7.2 9.1 copy-start.92
  7.3 9.1 copy-start.73
  7.3 90.0 %all-gather.5.cloned.1.call-start = ((), (), s32[]{:S(2)}) async-start(), calls=%async_computation.4 | async-start | bytes 5242880 | tf_op jit(solution)/shard_map/all_gather | solution.py:188
  9.2 8.6 copy-start.45
  9.2 8.6 copy-start.58
  9.2 8.6 copy-start.90
  9.3 11.8 copy-start.47
  9.3 11.7 copy-start.91
  11.2 9.0 copy-start.75
  11.2 13.0 copy-start.55
  14.3 295.3 %reduce-scatter.5.cloned.1.call-start = ((), (), s32[]{:S(2)}) async-start(), calls=%async_computation.5 | async-start | bytes 5242880 | tf_op jit(solution)/shard_map/reduce_scatter | solution.py:229
  15.0 16.3 %copy-start.88 = (f32[256]{0:T(256)}, f32[256]{0:T(256)S(1)}, u32[]{:S(2)}) copy-start(f32[256]{0:T(256)S(1)} %add_abs_fusion) | copy-start | bytes 3076
  15.1 8.3 copy-start.67
  16.4 15.6 %copy-start.78 = (f32[3,3,256]{2,1,0:T(4,128)S(1)}, f32[3,3,256]{2,1,0:T(4,128)}, u32[]{:S(2)}) copy-start(f32[3,3,256]{2,1,0:T(4,128)} %param.32) | copy-start | bytes 27652
  28.4 68.9 %copy-start.96 = (f32[3,256]{1,0:T(4,128)S(1)}, f32[3,256]{1,0:T(4,128)}, u32[]{:S(2)}) copy-start(f32[3,256]{1,0:T(4,128)} %param.31) | copy-start | bytes 9220
  32.0 71.1 %copy-start.60 = (f32[3,256]{1,0:T(4,128)}, f32[3,256]{1,0:T(4,128)S(1)}, u32[]{:S(2)}) copy-start(f32[3,256]{1,0:T(4,128)S(1)} %get-tuple-element.101) | copy-start | bytes 9220
  32.0 71.1 %copy-start.62 = (f32[3,256]{1,0:T(4,128)}, f32[3,256]{1,0:T(4,128)S(1)}, u32[]{:S(2)}) copy-start(f32[3,256]{1,0:T(4,128)S(1)} %get-tuple-element.102) | copy-start | bytes 9220
  32.0 71.1 %copy-start.64 = (f32[3,256]{1,0:T(4,128)}, f32[3,256]{1,0:T(4,128)S(1)}, u32[]{:S(2)}) copy-start(f32[3,256]{1,0:T(4,128)S(1)} %get-tuple-element.103) | copy-start | bytes 9220
  35.9 67.1 %copy-start.80 = (f32[3,256]{1,0:T(4,128)S(1)}, f32[3,256]{1,0:T(4,128)}, u32[]{:S(2)}) copy-start(f32[3,256]{1,0:T(4,128)} %param.33) | copy-start | bytes 9220
  105.7 122.8 %copy-start.3 = (f32[2048,3,256]{2,0,1:T(8,128)}, f32[2048,3,256]{2,0,1:T(8,128)S(1)}, u32[]{:S(2)}) copy-start(f32[2048,3,256]{2,0,1:T(8,128)S(1)} %add_add_fusion) | copy-start | bytes 18874372
  234.1 75.5 %copy-start.81 = (f32[1024]{0:T(1024)S(1)}, f32[1024]{0:T(1024)}, u32[]{:S(2)}) copy-start(f32[1024]{0:T(1024)} %param.44) | copy-start | bytes 12292
  234.2 82.0 %copy-start.66 = (f32[1024]{0:T(1024)S(1)}, f32[1024]{0:T(1024)}, u32[]{:S(2)}) copy-start(f32[1024]{0:T(1024)} %param.45) | copy-start | bytes 12292
  234.2 82.0 %copy-start.82 = (f32[1024]{0:T(1024)S(1)}, f32[1024]{0:T(1024)}, u32[]{:S(2)}) copy-start(f32[1024]{0:T(1024)} %param.46) | copy-start | bytes 12292
  234.2 164.8 %all-gather.7.cloned.1.call-start = ((), (), s32[]{:S(2)}) async-start(), calls=%async_computation.6 | async-start | bytes 5242880 | tf_op jit(solution)/shard_map/all_gather | solution.py:237
  317.6 162.8 %all-gather.9.cloned.1.call-start = ((), (), s32[]{:S(2)}) async-start(), calls=%async_computation.8 | async-start | bytes 5242880 | tf_op jit(solution)/shard_map/all_gather | solution.py:253
  318.2 162.2 %copy-start.97 = (f32[1024]{0:T(1024)S(1)}, f32[1024]{0:T(1024)}, u32[]{:S(2)}) copy-start(f32[1024]{0:T(1024)} %param.48) | copy-start | bytes 12292
  318.2 327.6 %reduce-scatter.9.cloned.1.call-start = ((), (), s32[]{:S(2)}) async-start(), calls=%async_computation.9 | async-start | bytes 10485760 | tf_op jit(solution)/shard_map/reduce_scatter | solution.py:261
  480.4 15.4 %copy-start.95 = (bf16[1024,1024]{1,0:T(8,128)(2,1)S(1)}, bf16[1024,1024]{1,0:T(8,128)(2,1)}, u32[]{:S(2)}) copy-start(bf16[1024,1024]{1,0:T(8,128)(2,1)} %param.47) | copy-start | bytes 6291460
  502.8 222.9 %reduce-scatter.7.cloned.1.call-start = ((), (), s32[]{:S(2)}) async-start(), calls=%async_computation.7 | async-start | bytes 5242880 | tf_op jit(solution)/shard_map/reduce_scatter | solution.py:242
  514.2 131.6 %copy-start.5 = (f32[512,1024]{1,0:T(8,128)S(1)}, f32[512,1024]{1,0:T(8,128)}, u32[]{:S(2)}) copy-start(f32[512,1024]{1,0:T(8,128)} %copy-done.4) | copy-start | bytes 6291460
  514.2 211.5 %copy-start.83 = (f32[1024]{0:T(1024)S(1)}, f32[1024]{0:T(1024)}, u32[]{:S(2)}) copy-start(f32[1024]{0:T(1024)} %param.50) | copy-start | bytes 12292
  514.2 300.4 %all-gather.11.cloned.1.call-start = ((), (), s32[]{:S(2)}) async-start(), calls=%async_computation.10 | async-start | bytes 5242880 | tf_op jit(solution)/shard_map/all_gather | solution.py:269
  729.9 84.8 %copy-start.15 = (f32[32,64,256]{2,1,0:T(8,128)S(1)}, f32[32,64,256]{2,1,0:T(8,128)}, u32[]{:S(2)}) copy-start(f32[32,64,256]{2,1,0:T(8,128)} %copy-done.14) | copy-start | bytes 6291460
  733.3 326.5 %reduce-scatter.11.cloned.1.call-start = ((), (), s32[]{:S(2)}) async-start(), calls=%async_computation.11 | async-start | bytes 5242880 | tf_op jit(solution)/shard_map/reduce_scatter | solution.py:301
  825.5 13.6 copy-start.9
  885.4 24.9 %slice-start = ((s8[6291456]{0:T(1024)(128)(4,1)}), s8[4194304]{0:T(1024)(128)(4,1)S(1)}, s32[]{:S(2)}) async-start(s8[6291456]{0:T(1024)(128)(4,1)} %bitcast.281), calls=%async_computation.14 | async-start | bytes 8388608
  897.1 13.2 slice-start.1
  933.8 258.2 %all-reduce.15.cloned.1.call-start = ((), (), s32[]{:S(2)}) async-start(), calls=%async_computation.13 | async-start | bytes 25296896 | tf_op jit(solution)/shard_map/psum | solution.py:321
  933.8 10.2 copy-start.94
  1016.3 25.2 %copy-start.56 = (f32[64,256]{1,0:T(8,128)S(1)}, f32[64,256]{1,0:T(8,128)}, u32[]{:S(2)}) copy-start(f32[64,256]{1,0:T(8,128)} %param.41) | copy-start | bytes 196612
  1016.3 30.2 %copy-start.21 = (f32[2048,64]{0,1:T(8,128)S(1)}, f32[2048,64]{0,1:T(8,128)}, u32[]{:S(2)}) copy-start(f32[2048,64]{0,1:T(8,128)} %copy-done.20) | copy-start | bytes 1572868
  1016.3 30.2 %copy-start.48 = (f32[64,64]{1,0:T(8,128)S(1)}, f32[64,64]{1,0:T(8,128)}, u32[]{:S(2)}) copy-start(f32[64,64]{1,0:T(8,128)} %param.38) | copy-start | bytes 49156
  1016.3 32.5 %copy-start.27 = (f32[2048,64]{0,1:T(8,128)S(1)}, f32[2048,64]{0,1:T(8,128)}, u32[]{:S(2)}) copy-start(f32[2048,64]{0,1:T(8,128)} %copy-done.26) | copy-start | bytes 1572868
  1016.3 32.5 %copy-start.46 = (f32[64,64]{1,0:T(8,128)S(1)}, f32[64,64]{1,0:T(8,128)}, u32[]{:S(2)}) copy-start(f32[64,64]{1,0:T(8,128)} %param.36) | copy-start | bytes 49156
  1016.3 36.2 %copy-start.41 = (f32[2048,16]{0,1:T(8,128)S(1)}, f32[2048,16]{0,1:T(8,128)}, u32[]{:S(2)}) copy-start(f32[2048,16]{0,1:T(8,128)} %copy-done.40) | copy-start | bytes 393220
  1016.3 36.2 %copy-start.43 = (f32[2048,16]{0,1:T(8,128)S(1)}, f32[2048,16]{0,1:T(8,128)}, u32[]{:S(2)}) copy-start(f32[2048,16]{0,1:T(8,128)} %copy-done.42) | copy-start | bytes 393220
  1016.4 36.2 %copy-start.50 = (f32[2048,1]{0,1:T(1,128)S(1)}, f32[2048,1]{0,1:T(1,128)}, u32[]{:S(2)}) copy-start(f32[2048,1]{0,1:T(1,128)} %copy-done.49) | copy-start | bytes 24580
  1016.4 314.4 %all-reduce.13.cloned.1.call-start = ((), (), s32[]{:S(2)}) async-start(), calls=%async_computation.12 | async-start | bytes 225280 | tf_op jit(solution)/shard_map/psum | solution.py:350
  1046.5 13.3 copy-start.2
  1046.5 13.3 copy-start.52
  1046.5 13.3 copy-start.54
  1048.9 13.5 copy-start.76
  1048.9 13.5 copy-start.72
  1191.9 149.3 %copy-start.57 = (f32[64,256]{1,0:T(8,128)S(1)}, f32[64,256]{1,0:T(8,128)}, u32[]{:S(2)}) copy-start(f32[64,256]{1,0:T(8,128)} %get-tuple-element.129) | copy-start | bytes 196612
  1191.9 149.9 %copy-start.44 = (f32[256,1024]{1,0:T(8,128)S(1)}, f32[256,1024]{1,0:T(8,128)}, u32[]{:S(2)}) copy-start(f32[256,1024]{1,0:T(8,128)} %get-tuple-element.131) | copy-start | bytes 3145732
  1330.8 8.3 copy-start.100
  1330.8 8.8 copy-start.69
  1330.8 9.4 copy-start.99
  1330.8 9.9 copy-start.98
  1333.4 9.4 copy-start.87
  1333.4 10.0 copy-start.86
  1333.4 10.6 copy-start.85
  1333.4 11.2 copy-start.36
  (53 other events, 196.8 us)
Sparse Core Ops, SparseCore 0:
  14.4 82.8 all-gather.4
  234.3 75.2 reduce-scatter.4
  317.7 81.2 all-gather.6
  401.1 79.2 all-gather.8
  502.9 142.8 reduce-scatter.8
  648.0 77.6 reduce-scatter.6
  733.4 81.2 all-gather.10
  933.9 75.2 reduce-scatter.10
  1016.4 175.4 all-reduce.14
  1200.5 130.2 all-reduce.12
where the time goes:
time: 1360 us
  waiting for transfers between devices  840 us (62%)
  matrix products  375 us (28%)
  other arithmetic  54.9 us (4%)
  local copies, waits for them, and re-layouts  47.1 us (3%)
  blocking collectives  23.7 us (2%)
  between operations  16.3 us (1%)
    psum x1, waiting for transfers between devices, per_device(): lax.psum((mixer_gain_grad, mixer_shift_grad, output_bias_grad, feed_gain_...  139 us
    reduce_scatter x1, waiting for transfers between devices, per_device(): lax.psum_scatter(contract_cols(pre_grad, expand_weight), 'mp', scatter_di...  131 us
    psum x1, waiting for transfers between devices, per_device(): lax.psum((input_weight_grad, input_bias_grad, conv_weight_grad, conv_bias...  123 us
    all_gather x1, waiting for transfers between devices, per_device(): piece = lax.all_gather(mix_low, 'mp', axis=0, tiled=True)  81.4 us
    all_gather x1, waiting for transfers between devices, per_device(): feed_rows = lax.all_gather(feed_normed, 'mp', axis=0, tiled=True)  80.6 us
    reduce_scatter x1, waiting for transfers between devices, per_device(): lax.psum_scatter(jnp.dot(activated, reduce_weight, preferred_element_type...  77 us
    reduce_scatter x1, waiting for transfers between devices, per_device(): lax.psum_scatter(jnp.dot(gated, output_weight, preferred_element_type=jnp...  75.4 us
    all_gather x1, waiting for transfers between devices, per_device(): piece = lax.all_gather(out_low, 'mp', axis=0, tiled=True)  70.4 us
  transfers between devices with their start and end apart: 10, of which 9 were waited for; matrix products, arithmetic and copies ran while one was open for 11% of the time, Pallas kernels for 0%

commit v1 on v0

v1 whole, which is shorter than its diff:
```python
import functools
import math

import jax
import jax.numpy as jnp
import ml_dtypes
import numpy as np
from jax import lax
from jax.experimental import pallas as pl
from jax.experimental.pallas import tpu as pltpu
from jax.sharding import PartitionSpec as P

HIGHEST_MODE = lax.Precision.HIGHEST
EPSILON = 1e-05
FIRST_FACTOR = 64
CHUNK = 16
F32 = jnp.float32
BF16 = jnp.bfloat16
VMEM_SPEC = pl.BlockSpec(memory_space=pltpu.VMEM)


def norm_parts(values_in):
    centred = values_in - jnp.mean(values_in, axis=-1, keepdims=True)
    variance = jnp.mean(centred * centred, axis=-1, keepdims=True)
    scale = lax.rsqrt(variance + EPSILON)
    return centred * scale, scale


def norm_back(normal, scale, gain, grad):
    inner = grad * gain
    part = scale * (
        inner
        - jnp.mean(inner, axis=-1, keepdims=True)
        - normal * jnp.mean(inner * normal, axis=-1, keepdims=True)
    )
    return part, jnp.sum(grad * normal, axis=0), jnp.sum(grad, axis=0)


def delayed(values_in, count):
    if count == 0:
        return values_in
    return jnp.pad(values_in, ((count, 0), (0, 0)))[:-count]


def advanced(values_in, count):
    if count == 0:
        return values_in
    return jnp.pad(values_in, ((0, count), (0, 0)))[count:]


def position_features(total, emb_count):
    place = jnp.arange(total, dtype=F32)
    time_grid = place / (total - 1)
    bands = (emb_count - 1) // 2
    freq_grid = 0.0001 + jnp.arange(bands, dtype=F32) * ((bands - 1 - 0.0001) / (bands - 1))
    angles = 2.0 * math.pi / total * place[:, None] * freq_grid[None, :]
    return (
        jnp.concatenate([time_grid[:, None], jnp.cos(angles), -jnp.sin(angles)], axis=1),
        time_grid,
    )


def decay_table(time_grid, channel_ids, channel_total):
    slowest = math.log(0.01) / 1.5
    fastest = math.log(0.01) / 0.3
    rates = jnp.abs(slowest + (fastest - slowest) * channel_ids.astype(F32) / (channel_total - 1))
    return jnp.exp(-time_grid[:, None] * rates[None, :])


def filter_bank(filter_weights, features, decay_rows):
    (
        enter_weight,
        enter_bias,
        middle_weight,
        middle_bias,
        inner_weight,
        inner_bias,
        frequency,
        filter_weight,
    ) = filter_weights
    hidden = jnp.sin(
        frequency * (jnp.dot(features, enter_weight, precision=HIGHEST_MODE) + enter_bias)
    )
    hidden = jnp.sin(
        frequency * (jnp.dot(hidden, middle_weight, precision=HIGHEST_MODE) + middle_bias)
    )
    hidden = jnp.sin(
        frequency * (jnp.dot(hidden, inner_weight, precision=HIGHEST_MODE) + inner_bias)
    )
    return jnp.dot(hidden, filter_weight, precision=HIGHEST_MODE) * decay_rows


def spectral_tables(seq_len):
    total = 2 * seq_len
    count1 = FIRST_FACTOR
    count2 = total // count1
    half = count1 // 2
    slot = np.arange(half)
    t1 = np.arange(half)
    t2 = np.arange(count2)
    k2 = np.arange(count2)
    angle = 2 * np.pi * slot[:, None] * t1[None, :] / count1
    first = np.zeros((half, 2, half))
    first[:, 0] = np.cos(angle)
    first[:, 1] = -np.sin(angle)
    first[0, 1] = (-1.0) ** t1
    last = np.zeros((half, half, 2))
    last[:, :, 0] = np.cos(angle.T) / seq_len
    last[:, :, 1] = -np.sin(angle.T) / seq_len
    last[:, 0, 0] = 1.0 / total
    last[:, 0, 1] = (-1.0) ** t1 / total
    mid = np.zeros((half, 2, count2, 2, count2))
    back = np.zeros((half, 2, count2, 2, count2))
    for s in range(1, half):
        turn = np.exp(-2j * np.pi * t2[None, :] * (s / total + k2[:, None] / count2))
        mid[s, 0, :, 0] = turn.real
        mid[s, 0, :, 1] = -turn.imag
        mid[s, 1, :, 0] = turn.imag
        mid[s, 1, :, 1] = turn.real
        undo = np.conj(turn).T
        back[s, 0, :, 0] = undo.real
        back[s, 0, :, 1] = -undo.imag
        back[s, 1, :, 0] = undo.imag
        back[s, 1, :, 1] = undo.real
    h2 = count2 // 2
    turn = np.exp(-2j * np.pi * t2[None, :] * k2[:h2, None] / count2)
    mid[0, 0, :h2, 0] = turn.real
    mid[0, 1, :h2, 0] = turn.imag
    mid[0, 1, 0, 0] = (-1.0) ** t2
    back[0, 0, :, 0, :h2] = 2 * turn.real.T
    back[0, 0, :, 1, :h2] = 2 * turn.imag.T
    back[0, 0, :, 0, 0] = 1.0
    back[0, 0, :, 1, 0] = (-1.0) ** t2
    turn = np.exp(-2j * np.pi * t2[None, :] * (half / total + k2[:h2, None] / count2))
    mid[0, 0, h2:, 1] = turn.real
    mid[0, 1, h2:, 1] = turn.imag
    back[0, 1, :, 0, h2:] = 2 * turn.real.T
    back[0, 1, :, 1, h2:] = 2 * turn.imag.T
    unit = np.eye(CHUNK)
    tables = (
        np.kron(first.reshape(count1, half), unit),
        mid.reshape(half, 2 * count2, 2 * count2),
        back.reshape(half, 2 * count2, 2 * count2),
        np.kron(last.reshape(half, count1), unit),
    )
    return tuple(jnp.asarray(v.astype(np.float32).astype(ml_dtypes.bfloat16)) for v in tables)


def times(left, right):
    return jnp.dot(left, right, preferred_element_type=F32)


def stage_first(first_ref, x_ref, y_ref):
    count1, count2, cols = y_ref.shape
    for j in range(count2 // CHUNK):
        rows = slice(CHUNK * j, CHUNK * (j + 1))
        block = x_ref[:, rows, :].reshape(count1 // 2 * CHUNK, cols)
        y_ref[:, rows, :] = times(first_ref[...], block).reshape(count1, CHUNK, cols).astype(BF16)


def stage_last(last_ref, z_ref, out_ref):
    count1, count2, cols = z_ref.shape
    for j in range(count2 // CHUNK):
        rows = slice(CHUNK * j, CHUNK * (j + 1))
        block = z_ref[:, rows, :].reshape(count1 * CHUNK, cols)
        values = times(last_ref[...], block).reshape(count1 // 2, CHUNK, cols)
        out_ref[:, rows, :] = values.astype(out_ref.dtype)


def spectral_product(s, left_re, left_im, right_re, right_im, sign):
    both_re = left_re * right_re
    both_im = left_im * right_im
    row = lax.broadcasted_iota(jnp.int32, both_re.shape, 0)
    real_row = (row == 0) & (s == 0)
    out_re = jnp.where(real_row, both_re, both_re - sign * both_im)
    out_im = jnp.where(real_row, both_im, left_im * right_re + sign * left_re * right_im)
    return jnp.concatenate([out_re, out_im], axis=0).astype(BF16)


def conv_kernel(
    first_ref, mid_ref, back_ref, last_ref, u_ref, t_ref, out_ref, su_ref, st_ref, y_ref, z_ref
):
    count1, count2, cols = y_ref.shape
    stage_first(first_ref, u_ref, y_ref)
    stage_first(first_ref, t_ref, z_ref)

    def slot_step(s, carry):
        pair = pl.ds(2 * s, 2)
        spec_u = times(mid_ref[s], y_ref[pair].reshape(2 * count2, cols))
        spec_t = times(mid_ref[s], z_ref[pair].reshape(2 * count2, cols))
        su_ref[pair] = spec_u.astype(BF16).reshape(2, count2, cols)
        st_ref[pair] = spec_t.astype(BF16).reshape(2, count2, cols)
        product = spectral_product(
            s, spec_u[:count2], spec_u[count2:], spec_t[:count2], spec_t[count2:], 1
        )
        z_ref[pair] = times(back_ref[s], product).astype(BF16).reshape(2, count2, cols)
        return carry

    lax.fori_loop(0, count1 // 2, slot_step, 0, unroll=2)
    stage_last(last_ref, z_ref, out_ref)


def conv_back_kernel(
    first_ref, mid_ref, back_ref, last_ref, g_ref, su_ref, st_ref, du_ref, dt_ref, y_ref, z_ref
):
    count1, count2, cols = y_ref.shape
    stage_first(first_ref, g_ref, y_ref)

    def slot_step(s, carry):
        pair = pl.ds(2 * s, 2)
        spec_g = times(mid_ref[s], y_ref[pair].reshape(2 * count2, cols))
        spec_u = su_ref[pair].astype(F32)
        spec_t = st_ref[pair].astype(F32)
        product = spectral_product(s, spec_g[:count2], spec_g[count2:], spec_t[0], spec_t[1], -1)
        y_ref[pair] = times(back_ref[s], product).astype(BF16).reshape(2, count2, cols)
        product = spectral_product(s, spec_g[:count2], spec_g[count2:], spec_u[0], spec_u[1], -1)
        z_ref[pair] = times(back_ref[s], product).astype(BF16).reshape(2, count2, cols)
        return carry

    lax.fori_loop(0, count1 // 2, slot_step, 0, unroll=2)
    stage_last(last_ref, y_ref, du_ref)
    stage_last(last_ref, z_ref, dt_ref)


def long_conv(tables, signal, taps):
    seq_len, cols = signal.shape
    count1 = FIRST_FACTOR
    count2 = 2 * seq_len // count1
    timed = (count1 // 2, count2, cols)
    spectral = jax.ShapeDtypeStruct((count1, count2, cols), BF16)
    out, spec_u, spec_t = pl.pallas_call(
        conv_kernel,
        out_shape=(jax.ShapeDtypeStruct(timed, F32), spectral, spectral),
        in_specs=[VMEM_SPEC] * 6,
        out_specs=(VMEM_SPEC,) * 3,
        scratch_shapes=[pltpu.VMEM((count1, count2, cols), BF16)] * 2,
        compiler_params=pltpu.CompilerParams(vmem_limit_bytes=40 << 20),
        cost_estimate=pl.CostEstimate(
            flops=8_000_000_000, bytes_accessed=14 << 20, transcendentals=0
        ),
        name="long_conv",
    )(*tables, signal.reshape(timed), taps.reshape(timed))
    return out.reshape(seq_len, cols), spec_u, spec_t


def long_conv_back(tables, grad, spec_u, spec_t):
    seq_len, cols = grad.shape
    count1 = FIRST_FACTOR
    count2 = 2 * seq_len // count1
    timed = (count1 // 2, count2, cols)
    grad_u, grad_t = pl.pallas_call(
        conv_back_kernel,
        out_shape=(jax.ShapeDtypeStruct(timed, F32), jax.ShapeDtypeStruct(timed, F32)),
        in_specs=[VMEM_SPEC] * 7,
        out_specs=(VMEM_SPEC,) * 2,
        scratch_shapes=[pltpu.VMEM((count1, count2, cols), BF16)] * 2,
        compiler_params=pltpu.CompilerParams(vmem_limit_bytes=40 << 20),
        cost_estimate=pl.CostEstimate(
            flops=8_000_000_000, bytes_accessed=14 << 20, transcendentals=0
        ),
        name="long_conv_back",
    )(*tables, grad.reshape(timed), spec_u, spec_t)
    return grad_u.reshape(seq_len, cols), grad_t.reshape(seq_len, cols)


def shift_mp(values_in, count):
    size = lax.axis_size("mp")
    return lax.ppermute(values_in, "mp", [(i, (i + count) % size) for i in range(size)])


def swap_dp(values_in, bit):
    size = lax.axis_size("dp")
    return lax.ppermute(values_in, "dp", [(i, i ^ (1 << bit)) for i in range(size)])


def bit_orders():
    bits = lax.axis_size("dp").bit_length() - 1
    high = list(range(1, bits))
    return [0] + high, [0] + high[::-1]


def after(values_in, *others):
    return lax.optimization_barrier((values_in,) + others)[0]


def gather_blocks(block, order):
    held = {0: block}
    for bit in order[::-1]:
        for offset in list(held):
            held[offset | (1 << bit)] = swap_dp(held[offset], bit)
    return held


def by_index(stacked):
    here = lax.axis_index("dp")
    size = stacked.shape[0]
    return jnp.concatenate(
        [lax.dynamic_slice_in_dim(stacked, here ^ i, 1, 0) for i in range(size)], axis=0
    )


def gather_dp(block, order):
    held = gather_blocks(block, order)
    return by_index(jnp.stack([held[m] for m in range(len(held))]))


def place_kernel(turned, here_ref, blocks_ref, out_ref):
    count, rows, _ = blocks_ref.shape
    here = here_ref[0]
    for i in range(count):
        block = blocks_ref[here ^ i].astype(F32)
        if turned:
            out_ref[:, i * rows : (i + 1) * rows] = block.T
        else:
            out_ref[i * rows : (i + 1) * rows, :] = block


def gather_total(total, order, turned=False):
    held = gather_blocks(total.astype(BF16), order)
    stacked = jnp.stack([held[m] for m in range(len(held))])
    count, rows, cols = stacked.shape
    if rows % 128 != 0:
        full = by_index(stacked).reshape(count * rows, cols)
        return (full.T if turned else full).astype(F32)
    shape = (cols, count * rows) if turned else (count * rows, cols)
    return pl.pallas_call(
        functools.partial(place_kernel, turned),
        out_shape=jax.ShapeDtypeStruct(shape, F32),
        in_specs=[pl.BlockSpec(memory_space=pltpu.SMEM), VMEM_SPEC],
        out_specs=VMEM_SPEC,
        compiler_params=pltpu.CompilerParams(vmem_limit_bytes=24 << 20),
        cost_estimate=pl.CostEstimate(flops=0, bytes_accessed=6 << 20, transcendentals=0),
        name="place_rows",
    )(jnp.full((1,), lax.axis_index("dp"), jnp.int32), stacked)


def scatter_dp(stacked, order):
    bits = len(order)
    here = lax.axis_index("dp")
    rest = stacked.shape[1:]
    held = stacked.reshape((2,) * bits + rest)
    left = list(range(bits))[::-1]
    for bit in order:
        axis = left.index(bit)
        own = (here >> bit) & 1
        away = lax.dynamic_index_in_dim(held, 1 - own, axis, keepdims=False).astype(BF16)
        keep = lax.dynamic_index_in_dim(held, own, axis, keepdims=False)
        held = keep.astype(F32) + swap_dp(away, bit).astype(F32)
        left.remove(bit)
        if len(left) > 0:
            held = held.astype(BF16)
    return held


def sum_dp(values_in):
    for bit in range(lax.axis_size("dp").bit_length() - 1):
        values_in = values_in + swap_dp(values_in, bit)
    return values_in


def sum_mp(values_in):
    total = values_in
    for k in range(1, lax.axis_size("mp")):
        total = total + shift_mp(values_in, k)
    return total


def pack(parts):
    flat = jnp.concatenate([p.reshape(-1) for p in parts])
    fill = -flat.shape[0] % 1024
    return jnp.pad(flat, (0, fill)).reshape(-1, 128)


def unpack(packed, parts):
    flat = packed.reshape(-1)
    out, start = [], 0
    for p in parts:
        out.append(flat[start : start + p.size].reshape(p.shape))
        start += p.size
    return out


def contract_rows(left, right):
    return lax.dot_general(left, right, (((0,), (0,)), ((), ())), preferred_element_type=F32)


def contract_cols(left, right):
    return lax.dot_general(left, right, (((1,), (1,)), ((), ())), preferred_element_type=F32)


def gelu_parts(value):
    factor = math.sqrt(2.0 / math.pi)
    square = value * value
    tanh_part = jnp.tanh(factor * value * (1.0 + 0.044715 * square))
    half = 0.5 * (1.0 + tanh_part)
    slope = half + 0.5 * value * (1.0 - tanh_part * tanh_part) * (
        factor * (1.0 + 3.0 * 0.044715 * square)
    )
    return value * half, slope


JOINT = 8
ROW_STEP = 32


def middle_kernel(*refs):
    (g0, g1, g2, g3, input_ref, cot_ref, out_weight_ref, vectors_ref, bias_ref) = refs[:9]
    weights = refs[9 : 11 + 4 * JOINT]
    (
        result_ref,
        hidden_grad_ref,
        d0,
        d1,
        d2,
        d3,
        act_ref,
        pre_grad_ref,
        normed_ref,
        mix_ref,
        out_low_ref,
        bias_grad_ref,
        sums_ref,
    ) = refs[11 + 4 * JOINT : 24 + 4 * JOINT]
    weight_ref, normal_ref, scale_ref, sems = refs[24 + 4 * JOINT :]
    expand_local, reduce_local = weights[:2]
    others = weights[2:]
    rows, width = input_ref.shape
    units = weight_ref.shape[4]
    per_step = 2 * 4 * units

    for j in range(JOINT):
        for kind, local in enumerate((expand_local, reduce_local)):
            for half in range(2):
                n = (kind * 2 + half) * 2
                pltpu.make_async_copy(
                    local.at[j, half], weight_ref.at[j, kind, half, 0], sems.at[j, n]
                ).start()
                pltpu.make_async_copy(
                    others[(kind * 2 + half) * JOINT + j],
                    weight_ref.at[j, kind, half, pl.ds(1, 3)],
                    sems.at[j, n + 1],
                ).start()

    mixed = times(g0[...], out_weight_ref[0])
    for k, g in enumerate((g1, g2, g3)):
        mixed = mixed + times(g[...], out_weight_ref[k + 1])
    result_ref[...] = input_ref[...] + mixed + vectors_ref[0:1]
    sums_ref[...] = jnp.zeros_like(sums_ref)

    def norm_step(i, carry):
        part = pl.ds(i * ROW_STEP, ROW_STEP)
        values = result_ref[part, :]
        normal, scale = norm_parts(values)
        normal_ref[part, :] = normal
        scale_ref[part, :] = scale
        normed_ref[part, :] = (normal * vectors_ref[1:2] + vectors_ref[2:3]).astype(BF16)
        cot = cot_ref[part, :]
        out_low_ref[part, :] = cot.astype(BF16)
        result_ref[part, :] = values + vectors_ref[3:4]
        hidden_grad_ref[part, :] = jnp.zeros_like(cot)
        sums_ref[0:1, :] += jnp.sum(cot, axis=0, keepdims=True)
        return carry

    lax.fori_loop(0, rows // ROW_STEP, norm_step, 0)

    def hidden_step(j, carry):
        for kind in range(2):
            for half in range(2):
                n = (kind * 2 + half) * 2
                one = weight_ref.at[j, kind, half, 0]
                pltpu.make_async_copy(one, one, sems.at[j, n]).wait()
                rest = weight_ref.at[j, kind, half, pl.ds(1, 3)]
                pltpu.make_async_copy(rest, rest, sems.at[j, n + 1]).wait()
        expand = weight_ref[j, 0].reshape(per_step, width)
        reduce = weight_ref[j, 1].reshape(per_step, width)
        value, slope = gelu_parts(contract_cols(normed_ref[...], expand) + bias_ref[j])
        value = value.astype(BF16)
        columns = pl.ds(pl.multiple_of(j * per_step, per_step), per_step)
        act_ref[:, columns] = value
        result_ref[...] += times(value, reduce)
        grad = (contract_cols(out_low_ref[...], reduce) * slope).astype(BF16)
        pre_grad_ref[:, columns] = grad
        bias_grad_ref[j] = jnp.sum(grad.astype(F32), axis=0, keepdims=True)
        hidden_grad_ref[...] += times(grad, expand)
        return carry

    lax.fori_loop(0, JOINT, hidden_step, 0)

    def back_step(i, carry):
        part = pl.ds(i * ROW_STEP, ROW_STEP)
        grad = hidden_grad_ref[part, :]
        normal = normal_ref[part, :]
        res_part, gain_sum, shift_sum = norm_back(normal, scale_ref[part, :], vectors_ref[1:2], grad)
        hidden_grad = cot_ref[part, :] + res_part
        hidden_grad_ref[part, :] = hidden_grad
        mix_ref[part, :] = hidden_grad.astype(BF16)
        sums_ref[1:2, :] += gain_sum[None]
        sums_ref[2:3, :] += shift_sum[None]
        sums_ref[3:4, :] += jnp.sum(hidden_grad, axis=0, keepdims=True)
        return carry

    lax.fori_loop(0, rows // ROW_STEP, back_step, 0)
    for k, d in enumerate((d0, d1, d2, d3)):
        d[...] = contract_cols(mix_ref[...], out_weight_ref[k]).astype(BF16)


def middle(gated, block_input, cotangent, out_weight, vectors, bias, local, others):
    rows, width = block_input.shape
    groups, channels, _ = out_weight.shape
    units = others[0].shape[1]
    hidden = JOINT * 2 * groups * units
    sh = jax.ShapeDtypeStruct
    any_spec = pl.BlockSpec(memory_space=pl.ANY)
    return pl.pallas_call(
        middle_kernel,
        out_shape=(
            sh((rows, width), F32),
            sh((rows, width), F32),
            *[sh((rows, channels), BF16)] * 4,
            sh((rows, hidden), BF16),
            sh((rows, hidden), BF16),
            sh((rows, width), BF16),
            sh((rows, width), BF16),
            sh((rows, width), BF16),
            sh((JOINT, 1, hidden // JOINT), F32),
            sh((8, width), F32),
        ),
        in_specs=[VMEM_SPEC] * 9 + [any_spec] * (2 + 4 * JOINT),
        out_specs=(VMEM_SPEC,) * 13,
        scratch_shapes=[
            pltpu.VMEM((JOINT, 2, 2, groups, units, width), BF16),
            pltpu.VMEM((rows, width), F32),
            pltpu.VMEM((rows, 1), F32),
            pltpu.SemaphoreType.DMA((JOINT, 8)),
        ],
        compiler_params=pltpu.CompilerParams(vmem_limit_bytes=58 << 20),
        cost_estimate=pl.CostEstimate(
            flops=20_000_000_000, bytes_accessed=45 << 20, transcendentals=rows * hidden
        ),
        name="middle",
    )(*gated, block_input, cotangent, out_weight, vectors, bias, *local, *others)


def per_device(
    block_input,
    lengths,
    mixer_gain,
    mixer_shift,
    input_weight,
    input_bias,
    conv_weight,
    conv_bias,
    enter_weight,
    enter_bias,
    middle_weight,
    middle_bias,
    inner_weight,
    inner_bias,
    frequency,
    filter_weight,
    skip_scale,
    output_weight,
    output_bias,
    feed_gain,
    feed_shift,
    expand_weight,
    expand_bias,
    reduce_weight,
    reduce_bias,
    cotangent,
):
    own_rows, width = block_input.shape
    channels = input_weight.shape[2]
    hidden = expand_weight.shape[1]
    mp_size = lax.axis_size("mp")
    dp_size = lax.axis_size("dp")
    mp_here = lax.axis_index("mp")
    dp_here = lax.axis_index("dp")
    seq_len = own_rows * mp_size
    order_a, order_b = bit_orders()
    bits = len(order_a)

    mixer_normal, mixer_scale = norm_parts(block_input)
    mixer_normed = (mixer_normal * mixer_gain + mixer_shift).astype(BF16)
    mixer_rows = lax.all_gather(mixer_normed, "mp", axis=0, tiled=True)

    share = hidden // dp_size
    units = share // 2
    inner = dp_size // JOINT
    out_share = channels // dp_size

    def offset_of(joint, inside):
        return (joint >> 2) | ((joint & 1) << 1) | ((joint & 2) << 1) | (inside << 3)

    offsets = [offset_of(j, i) for j in range(JOINT) for i in range(inner)]
    expand_turned = expand_weight.T
    local = []
    for weight in (expand_turned, reduce_weight):
        blocks = weight.reshape(dp_size, share, width)
        blocks = jnp.concatenate(
            [lax.dynamic_slice_in_dim(blocks, dp_here ^ m, 1, 0) for m in offsets], axis=0
        )
        blocks = blocks.reshape(JOINT, inner, 2, units, width).transpose(0, 2, 1, 3, 4)
        local.append(blocks.reshape(JOINT, 2, inner * units, width))
    expand_part = lax.dynamic_slice_in_dim(expand_turned, dp_here * share, share, 0)
    reduce_part = lax.dynamic_slice_in_dim(reduce_weight, dp_here * share, share, 0)
    output_part = lax.dynamic_slice_in_dim(output_weight, dp_here * out_share, out_share, 0)

    output_part = after(output_part, mixer_rows)
    output_pieces = jnp.stack([shift_mp(output_part, k) for k in range(1, mp_size)])
    output_other = gather_dp(output_pieces, order_a)
    others = []
    for part in (expand_part, reduce_part):
        part = after(part, mixer_rows)
        pieces = jnp.stack([shift_mp(part, k) for k in range(1, mp_size)])
        for half, order in enumerate((order_a, order_b)):
            held = gather_blocks(pieces[:, half * units : (half + 1) * units], order)
            for j in range(JOINT):
                block = jnp.stack([held[offset_of(j, i)] for i in range(inner)], axis=1)
                others.append(block.reshape(mp_size - 1, inner * units, width))
    all_bias = jnp.stack([expand_bias] + [shift_mp(expand_bias, k) for k in range(1, mp_size)])
    all_bias = by_index(all_bias.reshape(mp_size, dp_size, 2, units).transpose(1, 0, 2, 3))
    all_bias = jnp.stack([all_bias[m] for m in offsets])
    all_bias = all_bias.reshape(JOINT, inner, mp_size, 2, units).transpose(0, 3, 2, 1, 4)
    all_bias = all_bias.reshape(JOINT, 1, 2 * mp_size * inner * units)

    enter_flat = input_weight.reshape(width, 3 * channels)
    projected = times(mixer_rows, enter_flat) + input_bias.reshape(3 * channels)
    taps3 = conv_weight.reshape(3, 3 * channels)
    mixed_in = (
        taps3[0] * projected
        + taps3[1] * delayed(projected, 1)
        + taps3[2] * delayed(projected, 2)
        + conv_bias.reshape(3 * channels)
    )
    value_path = mixed_in[:, :channels]
    first_gate = mixed_in[:, channels : 2 * channels]
    second_gate = mixed_in[:, 2 * channels :]
    conv_input = (first_gate * value_path).astype(BF16)

    features, time_grid = position_features(seq_len, enter_weight.shape[0])
    channel_ids = mp_here * channels + jnp.arange(channels, dtype=jnp.int32)
    decay_rows = decay_table(time_grid, channel_ids, width)
    filter_weights = (
        enter_weight,
        enter_bias,
        middle_weight,
        middle_bias,
        inner_weight,
        inner_bias,
        frequency,
        filter_weight,
    )

    def local_bank(weight_set):
        return filter_bank(weight_set, features, decay_rows)

    filter_taps, bank_back = jax.vjp(local_bank, filter_weights)
    tables = spectral_tables(seq_len)
    long_out, spec_u, spec_t = long_conv(tables, conv_input, filter_taps.astype(BF16))
    conv_out = long_out + skip_scale * conv_input.astype(F32)
    positions = jnp.arange(seq_len, dtype=jnp.int32)
    row_mask = (positions < lengths[0]).astype(F32)[:, None]
    gated = (row_mask * second_gate * conv_out).astype(BF16)

    def to_rows(values_in):
        blocks = values_in.reshape(mp_size, own_rows, channels)
        pieces = []
        for k in range(mp_size):
            piece = lax.dynamic_index_in_dim(blocks, (mp_here + k) % mp_size, 0, keepdims=False)
            pieces.append(shift_mp(piece, k) if k > 0 else piece)
        return pieces

    def to_channels(pieces):
        arrived = jnp.stack([shift_mp(pieces[k], -k) if k > 0 else pieces[k] for k in range(mp_size)])
        blocks = [
            lax.dynamic_slice_in_dim(arrived, (z - mp_here) % mp_size, 1, 0) for z in range(mp_size)
        ]
        return jnp.concatenate(blocks, axis=0).reshape(seq_len, channels)

    gated_rows = to_rows(gated)
    out_weight = output_other.transpose(1, 0, 2, 3).reshape(mp_size - 1, channels, width)
    out_weight = jnp.concatenate([output_weight[None], out_weight])
    vectors = jnp.stack([output_bias, feed_gain, feed_shift, reduce_bias] + [reduce_bias] * 4)
    (
        result,
        hidden_grad,
        *gated_grads,
        activated,
        pre_grad,
        feed_normed,
        mix_low,
        out_low,
        bias_grad,
        sums,
    ) = middle(gated_rows, block_input, cotangent, out_weight, vectors, all_bias, local, others)
    gated_grad = to_channels(gated_grads)

    def reduce_groups(left, right, turned):
        halved = 2 * mp_size * inner * units * JOINT // 2
        shape = (2, 2, 2, mp_size) + (2,) * (bits - 3) + (units, width)
        keep = contract_rows(left[:, :halved], right).astype(BF16).reshape(shape)
        away = contract_rows(left[:, halved:], right).astype(BF16).reshape(shape)
        keep = (keep.astype(F32) + swap_dp(away, 0).astype(F32)).astype(BF16)
        pieces = []
        for half, order in enumerate((order_a, order_b)):
            held = keep[:, :, half]
            names = [2, 1, "group"] + list(range(3, bits))[::-1]
            for bit in order[1:]:
                axis = names.index(bit)
                away = lax.index_in_dim(held, 1, axis, keepdims=False)
                held = lax.index_in_dim(held, 0, axis, keepdims=False)
                held = (held.astype(F32) + swap_dp(away, bit).astype(F32)).astype(BF16)
                names.remove(bit)
            pieces.append(held)
        mine = jnp.concatenate(pieces, axis=1)
        total = mine[0].astype(F32)
        for k in range(1, mp_size):
            total = total + shift_mp(mine[k], -k).astype(F32)
        return gather_total(total, order_b if turned else order_a, turned)

    reduce_weight_grad = reduce_groups(activated, out_low, False)
    expand_weight_grad = reduce_groups(pre_grad, feed_normed, True)
    output_grads = jnp.stack([contract_rows(g, mix_low).astype(BF16) for g in gated_rows], axis=0)
    output_grads = output_grads.reshape(mp_size, dp_size, out_share, width).transpose(1, 0, 2, 3)
    mine = scatter_dp(output_grads, order_a)
    total = mine[0]
    for k in range(1, mp_size):
        total = total + shift_mp(mine[k].astype(BF16), -k).astype(F32)
    output_weight_grad = gather_dp(total.astype(BF16), order_a).astype(F32).reshape(channels, width)

    masked_grad = gated_grad.astype(F32) * row_mask
    second_grad = masked_grad * conv_out
    conv_grad_low = (masked_grad * second_gate).astype(BF16)
    conv_grad = conv_grad_low.astype(F32)
    skip_scale_grad = jnp.sum(conv_grad * conv_input.astype(F32), axis=0)
    conv_input_grad, taps_grad = long_conv_back(tables, conv_grad_low, spec_u, spec_t)
    conv_input_grad = conv_input_grad + skip_scale * conv_grad
    mixed_grad = jnp.concatenate(
        [conv_input_grad * first_gate, conv_input_grad * value_path, second_grad], axis=1
    )
    conv_weight_grad = jnp.stack(
        [jnp.sum(mixed_grad * delayed(projected, k), axis=0) for k in range(3)]
    )
    conv_bias_grad = jnp.sum(mixed_grad, axis=0)
    projected_low = (
        taps3[0] * mixed_grad
        + taps3[1] * advanced(mixed_grad, 1)
        + taps3[2] * advanced(mixed_grad, 2)
    ).astype(BF16)
    mixer_normed_grad = lax.psum_scatter(
        contract_cols(projected_low, enter_flat).astype(BF16),
        "mp",
        scatter_dimension=0,
        tiled=True,
    ).astype(F32)
    input_weight_grad = contract_rows(mixer_rows, projected_low)
    input_bias_grad = jnp.sum(projected_low.astype(F32), axis=0)
    input_weight_grad = scatter_dp(input_weight_grad.reshape(dp_size, -1, 3 * channels), order_a)
    input_weight_grad = gather_total(input_weight_grad, order_a).reshape(width, 3, channels)
    bank_grads = bank_back(taps_grad)[0]
    input_part, mixer_gain_grad, mixer_shift_grad = norm_back(
        mixer_normal, mixer_scale, mixer_gain, mixer_normed_grad
    )
    input_grad = hidden_grad + input_part

    bias_grad = bias_grad.reshape(JOINT, 2, mp_size, inner, units).transpose(0, 3, 2, 1, 4)
    bias_grad = bias_grad.reshape(dp_size, mp_size, share)
    bias_grad = by_index(jnp.stack([bias_grad[offsets.index(m)] for m in range(dp_size)]))
    bias_grad = bias_grad.transpose(1, 0, 2).reshape(mp_size, hidden)
    bias_grad = jnp.concatenate(
        [lax.dynamic_slice_in_dim(bias_grad, (mp_here - z) % mp_size, 1, 0) for z in range(mp_size)]
    )

    everywhere = [sums[3], sums[1], sums[2], sums[0], *bank_grads[:7], bias_grad]
    along_dp = [input_bias_grad, conv_weight_grad, conv_bias_grad, bank_grads[7], skip_scale_grad]
    packed_all = pack(everywhere)
    summed = sum_dp(jnp.concatenate([packed_all, pack(along_dp)]))
    along_dp = unpack(summed[packed_all.shape[0] :], along_dp)
    everywhere = unpack(sum_mp(summed[: packed_all.shape[0]]), everywhere)
    norm_sums = [mixer_gain_grad, mixer_shift_grad]
    norm_sums = unpack(sum_mp(sum_dp(pack(norm_sums))), norm_sums)
    expand_bias_grad = lax.dynamic_index_in_dim(everywhere[11], mp_here, 0, keepdims=False)
    return (
        result,
        input_grad,
        norm_sums[0],
        norm_sums[1],
        input_weight_grad,
        along_dp[0].reshape(3, channels),
        along_dp[1].reshape(3, 3, channels),
        along_dp[2].reshape(3, channels),
        *everywhere[4:11],
        along_dp[3],
        along_dp[4],
        output_weight_grad,
        everywhere[0],
        everywhere[1],
        everywhere[2],
        expand_weight_grad,
        expand_bias_grad,
        reduce_weight_grad,
        everywhere[3],
    )


ROWS = P(("dp", "mp"), None)
FIRST = P("mp", None)
SECOND = P(None, "mp")
THIRD = P(None, None, "mp")


def solution(mesh):
    return jax.shard_map(
        per_device,
        mesh=mesh,
        in_specs=(
            ROWS, P("dp"), P(), P(), THIRD, SECOND, THIRD, SECOND,
            P(), P(), P(), P(), P(), P(), P(), SECOND,
            P("mp"), FIRST, P(), P(), P(), SECOND, P("mp"), FIRST, P(), ROWS,
        ),
        out_specs=(
            ROWS, ROWS, P(), P(), THIRD, SECOND, THIRD, SECOND,
            P(), P(), P(), P(), P(), P(), P(), SECOND,
            P("mp"), FIRST, P(), P(), P(), SECOND, P("mp"), FIRST, P(),
        ),
        check_vma=False,
    )
```

time: 1360 us -> 721 us (0.53)
  waiting for transfers between devices: 840 us -> 222 us
  matrix products: 375 us -> 69.3 us
  starting transfers between devices: 0.8 us -> 163 us
  Pallas kernels: 0 us -> 77.2 us
  local copies, waits for them, and re-layouts: 47.1 us -> 101 us
  blocking collectives: 23.7 us -> 0 us
    reduce_scatter x4 -> x1, waiting for transfers between devices: 284 us -> 0.02 us  [per_device(): lax.psum_scatter(contract_cols(projected_low, enter_flat).astype(BF16), '...]
    dot_general x40 -> x1, matrix products: 284 us -> 5.72 us  [times(): return jnp.dot(left, right, preferred_element_type=F32)]
    psum x2 -> x0, waiting for transfers between devices: 262 us -> none  [the longest x1 139 us: per_device(): lax.psum((mixer_gain_grad, mixer_shift_grad, output_bias_grad, feed_gain_...]
    all_gather x3 -> x0, waiting for transfers between devices: 232 us -> none  [the longest x1 81.4 us: per_device(): piece = lax.all_gather(mix_low, 'mp', axis=0, tiled=True)]
    ppermute x0 -> x118, waiting for transfers between devices: none -> 175 us  [the longest x85 141 us: swap_dp(): lax.ppermute(values_in, 'dp', [(i, i ^ 1 << bit) for i in range(size)])]
    ppermute x0 -> x118, starting transfers between devices: none -> 163 us  [the longest x85 102 us: swap_dp(): lax.ppermute(values_in, 'dp', [(i, i ^ 1 << bit) for i in range(size)])]
    pallas_call x0 -> x6, Pallas kernels: none -> 77.2 us  [the longest x1 46.4 us: middle(): pl.pallas_call(middle_kernel, out_shape=(sh((rows, width), F32), sh((rows...]
    dot_general x4 -> x1, matrix products: 31.3 us -> 4.94 us  [contract_cols(): lax.dot_general(left, right, (((1,), (1,)), ((), ())), preferred_element_...]
  transfers between devices with their start and end apart: 10 -> 120, of which waited for: 9 -> 39; matrix products, arithmetic and copies ran while one was open for 11% -> 15% of each run, Pallas kernels for 0% -> 2%
where the time goes in v1:
time: 721 us; the launch traced here: 707 us
  waiting for transfers between devices  222 us (31%)
  starting transfers between devices  163 us (23%)
  local copies, waits for them, and re-layouts  101 us (14%)
  Pallas kernels  77.2 us (11%)
  matrix products  69.3 us (10%)
  other arithmetic  57.3 us (8%)
  between operations  18.1 us (3%)
    ppermute x85, waiting for transfers between devices, swap_dp(): lax.ppermute(values_in, 'dp', [(i, i ^ 1 << bit) for i in range(size)])  141 us
    ppermute x85, starting transfers between devices, swap_dp(): lax.ppermute(values_in, 'dp', [(i, i ^ 1 << bit) for i in range(size)])  102 us
    ppermute x33, starting transfers between devices, shift_mp(): lax.ppermute(values_in, 'mp', [(i, (i + count) % size) for i in range(siz...  60.7 us
    unnamed x371, local copies, waits for them, and re-layouts  46.9 us
    all_gather x1, waiting for transfers between devices, per_device(): mixer_rows = lax.all_gather(mixer_normed, 'mp', axis=0, tiled=True)  46.5 us
    pallas_call x1, Pallas kernels, middle(): pl.pallas_call(middle_kernel, out_shape=(sh((rows, width), F32), sh((rows...  46.4 us
    ppermute x33, waiting for transfers between devices, shift_mp(): lax.ppermute(values_in, 'mp', [(i, (i + count) % size) for i in range(siz...  34.2 us
    dot_general x9, matrix products, contract_rows(): lax.dot_general(left, right, (((0,), (0,)), ((), ())), preferred_element_...  29.3 us
  transfers between devices with their start and end apart: 120, of which 39 were waited for; matrix products, arithmetic and copies ran while one was open for 15% of the time, Pallas kernels for 2%

profile of v1, /device:TPU:1, one launch (start us, length us, event | category | flops | bytes accessed | tf_op | source)
XLA Modules:
  0.0 706.8 jit_solution(2881379365368344009)
XLA Ops:
  19.7 2.9 copy.118
  37.8 4.0 fusion.10
  48.5 46.5 %all-gather.2.cloned.1.call-done = bf16[2048,1024]{1,0:T(8,128)(2,1)} async-done(((bf16[512,1024]{1,0:T(8,128)(2,1)}), bf16[2048,1024]{1,0:T(8,128)(2,1)}) %all-gather.2.cloned.1.call-update) | async-done | bytes 4194320 | tf_op jit(solution)/shard_map/all_gather | solution.py:585
  100.1 5.7 convolution_add_fusion
  113.0 12.2 %long_conv.1 = (f32[32,64,256]{2,1,0:T(8,128)S(1)}, bf16[64,64,256]{2,1,0:T(8,128)(2,1)S(1)}, bf16[64,64,256]{2,1,0:T(8,128)(2,1)S(1)}) custom-call(bf16[1024,512]{1,0:T(8,128)(2,1)S(1)} %copy-done.6, bf16[32,128,128]{2,1,0:T(8,128)(2,1)S(1)} %copy-done.8, bf16[32,128,128]{2,1,0:T(8,128)(2,1)S(1)} %copy-done.10, bf16[512,1024]{1,0:T(8,128)(2,1)S(1)} %copy-done.12, ...), custom_call_target="tpu_custom_call" | custom-call | flops 8000000000 | bytes 14680064 | tf_op jit(solution)/shard_map/long_conv/pallas_call | solution.py:231
  134.1 9.9 %collective-permute-start.6 = (bf16[3,32,1024]{2,1,0:T(8,128)(2,1)S(1)}, bf16[3,32,1024]{2,1,0:T(8,128)(2,1)S(1)}, u32[]{:S(2)}, u32[]{:S(2)}) collective-permute-start(bf16[3,32,1024]{2,1,0:T(8,128)(2,1)S(1)} %pad_maximum_fusion.12), channel_id=1, source_target_pairs={{0,4},{4,0},{8,12},{12,8},{16,20},{20,16},{24,28},{28,24},{1,5},{5... | collective-permute-start | bytes 589832 | tf_op jit(solution)/shard_map/ppermute | solution.py:273
  144.3 6.7 collective-permute-start.1
  152.1 12.4 %collective-permute-start.2 = (bf16[512,256]{1,0:T(8,128)(2,1)S(1)}, bf16[512,256]{1,0:T(8,128)(2,1)S(1)}, u32[]{:S(2)}, u32[]{:S(2)}) collective-permute-start(bf16[512,256]{1,0:T(8,128)(2,1)S(1)} %get-tuple-element.186), channel_id=1, source_target_pairs={{0,3},{1,0},{2,1},{3,2},{4,7},{5,4},{6,5},{7,6},{8,11},{9,8},{10,9... | collective-permute-start | bytes 786440 | tf_op jit(solution)/shard_map/ppermute | solution.py:268
  171.9 2.5 collective-permute-done.1.refs_2_
  174.4 5.2 collective-permute-start.8
  181.4 5.2 collective-permute-done.11
  186.6 3.1 collective-permute-start.12
  193.7 23.6 %collective-permute-done.43.refs_36_ = bf16[3,64,1024]{2,1,0:T(8,128)(2,1)S(1)} collective-permute-done((bf16[3,64,1024]{2,1,0:T(8,128)(2,1)S(1)}, bf16[3,64,1024]{2,1,0:T(8,128)(2,1)S(1)}, u32[]{:S(2)}, u32[]{:S(2)}) %collective-permute-start.43) | collective-permute-done | bytes 393248 | tf_op jit(solution)/shard_map/ppermute | solution.py:273
  222.7 6.4 collective-permute-done.21.refs_14_
  232.9 4.7 collective-permute-done.38.refs_30_
  246.7 46.4 %middle.1 = (f32[512,1024]{1,0:T(8,128)}, f32[512,1024]{1,0:T(8,128)}, bf16[512,256]{1,0:T(8,128)(2,1)}, bf16[512,256]{1,0:T(8,128)(2,1)}, bf16[512,256]{1,0:T(8...) custom-call(bf16[512,256]{1,0:T(8,128)(2,1)} %get-tuple-element.189., ...), custom_call_target="tpu_custom_call" | custom-call | flops 20000000000 | bytes 47185920 | tf_op jit(solution)/shard_map/middle/pallas_call | solution.py:514
  293.1 6.3 convolution_convert_fusion
  299.5 4.4 convolution_convert_fusion.1
  303.9 4.3 convolution_convert_fusion.3
  308.2 4.4 convolution_convert_fusion.2
  344.4 2.9 collective-permute-start.50
  347.4 4.2 collective-permute-start.51
  357.9 2.6 copy.114
  361.6 2.5 copy.111
  365.3 9.4 %collective-permute-done.51 = bf16[512,256]{1,0:T(8,128)(2,1)S(1)} collective-permute-done((bf16[512,256]{1,0:T(8,128)(2,1)}, bf16[512,256]{1,0:T(8,128)(2,1)S(1)}, u32[]{:S(2)}, u32[]{:S(2)}) %collective-permute-start.51) | collective-permute-done | bytes 262176 | tf_op jit(solution)/shard_map/ppermute | solution.py:268
  375.6 2.6 fusion.13
  379.8 13.3 %long_conv_back.1 = (f32[32,64,256]{2,1,0:T(8,128)S(1)}, f32[32,64,256]{2,1,0:T(8,128)S(1)}) custom-call(bf16[1024,512]{1,0:T(8,128)(2,1)S(1)} %copy-done.7, bf16[32,128,128]{2,1,0:T(8,128)(2,1)S(1)} %copy-done.9, bf16[32,128,128]{2,1,0:T(8,128)(2,1)S(1)} %copy-done.11, bf16[512,1024]{1,0:T(8,128)(2,1)S(1)} %copy-done.13, ...), custom_call_target="tpu_custom_call" | custom-call | flops 8000000000 | bytes 14680064 | tf_op jit(solution)/shard_map/long_conv_back/pallas_call | solution.py:251
  394.5 3.6 convolution_multiply_fusion.3
  400.5 3.2 multiply_reduce_fusion.6
  403.6 3.2 fusion.47
  406.8 3.0 fusion.48
  409.8 3.5 convolution_bitcast_fusion
  418.7 2.9 slice_multiply_fusion.1
  423.5 4.6 multiply_reduce_fusion.2
  428.3 8.3 %convert_reduce_fusion = (f32[768]{0:T(1024)S(1)}, bf16[2048,768]{1,0:T(8,128)(2,1)S(1)}) fusion(f32[2048,768]{1,0:T(8,128)} %get-tuple-element.172, f32[768]{0:T(1024)S(1)} %copy-done.80, f32[768]{0:T(1024)S(1)} %copy-done.78, f32[768]{0:T(1024)S(1)} %copy-done.76), kind=kLoop, calls=%fused_computation.17 | loop fusion | flops 12582144 | bytes 9449472 | tf_op jit(solution)/shard_map/reduce_sum | solution.py:758
  440.2 5.3 fusion.110
  446.8 4.9 convolution_convert_fusion.4
  456.2 3.3 collective-permute-start.74
  465.0 3.5 collective-permute-done.73
  476.5 8.3 %collective-permute-done.60 = bf16[2,128,768]{2,1,0:T(8,128)(2,1)S(1)} collective-permute-done((bf16[2,128,768]{2,1,0:T(8,128)(2,1)S(1)}, bf16[2,128,768]{2,1,0:T(8,128)(2,1)S(1)}, u32[]{:S(2)}, u32[]{:S(2)}) %collective-permute-start.60) | collective-permute-done | bytes 393248 | tf_op jit(solution)/shard_map/ppermute | solution.py:273
  485.0 11.0 %collective-permute-done.76 = bf16[2,4,32,1024]{3,2,1,0:T(8,128)(2,1)S(1)} collective-permute-done((bf16[2,4,32,1024]{3,2,1,0:T(8,128)(2,1)S(1)}, bf16[2,4,32,1024]{3,2,1,0:T(8,128)(2,1)S(1)}, u32[]{:S(2)}, u32[]{:S(2)}) %collective-permute-start.76) | collective-permute-done | bytes 524320 | tf_op jit(solution)/shard_map/ppermute | solution.py:273
  500.1 3.5 collective-permute-done.77
  503.7 3.3 collective-permute-start.78
  507.6 3.7 collective-permute-done.78
  512.5 6.2 collective-permute-done.79
  519.8 5.6 collective-permute-start.81
  533.1 3.1 collective-permute-done.86
  537.9 3.3 collective-permute-done.67
  544.8 4.3 fusion
  552.2 4.3 fusion.1
  558.4 15.7 %collective-permute-done.106 = bf16[2,4,64,1024]{3,2,1,0:T(8,128)(2,1)S(1)} collective-permute-done((bf16[2,4,64,1024]{3,2,1,0:T(8,128)(2,1)S(1)}, bf16[2,4,64,1024]{3,2,1,0:T(8,128)(2,1)S(1)}, u32[]{:S(2)}, u32[]{:S(2)}) %collective-permute-start.106) | collective-permute-done | bytes 1048608 | tf_op jit(solution)/shard_map/ppermute | solution.py:273
  576.5 20.0 %collective-permute-done.91 = bf16[2,4,64,1024]{3,2,1,0:T(8,128)(2,1)S(1)} collective-permute-done((bf16[2,4,64,1024]{3,2,1,0:T(8,128)(2,1)S(1)}, bf16[2,4,64,1024]{3,2,1,0:T(8,128)(2,1)S(1)}, u32[]{:S(2)}, u32[]{:S(2)}) %collective-permute-start.91) | collective-permute-done | bytes 1048608 | tf_op jit(solution)/shard_map/ppermute | solution.py:273
  599.0 9.5 %collective-permute-done.107 = bf16[4,64,1024]{2,1,0:T(8,128)(2,1)S(1)} collective-permute-done((bf16[4,64,1024]{2,1,0:T(8,128)(2,1)S(1)}, bf16[4,64,1024]{2,1,0:T(8,128)(2,1)S(1)}, u32[]{:S(2)}, u32[]{:S(2)}) %collective-permute-start.107) | collective-permute-done | bytes 524320 | tf_op jit(solution)/shard_map/ppermute | solution.py:273
  610.1 9.7 %collective-permute-done.92 = bf16[4,64,1024]{2,1,0:T(8,128)(2,1)S(1)} collective-permute-done((bf16[4,64,1024]{2,1,0:T(8,128)(2,1)S(1)}, bf16[4,64,1024]{2,1,0:T(8,128)(2,1)S(1)}, u32[]{:S(2)}, u32[]{:S(2)}) %collective-permute-start.92) | collective-permute-done | bytes 524320 | tf_op jit(solution)/shard_map/ppermute | solution.py:273
  621.1 3.3 collective-permute-start.93
  625.5 6.4 collective-permute-done.109
  633.1 5.7 collective-permute-start.111
  638.8 7.8 %collective-permute-start.112 = (bf16[128,1024]{1,0:T(8,128)(2,1)S(1)}, bf16[128,1024]{1,0:T(8,128)(2,1)}, u32[]{:S(2)}, u32[]{:S(2)}) collective-permute-start(bf16[128,1024]{1,0:T(8,128)(2,1)S(1)} %get-tuple-element.157), channel_id=1, source_target_pairs={{0,8},{4,12},{8,0},{12,4},{16,24},{20,28},{24,16},{28,20},{1,9},{5... | collective-permute-start | bytes 786440 | tf_op jit(solution)/shard_map/ppermute | solution.py:273
  651.7 3.6 copy.117
  663.5 2.5 collective-permute-done.97
  669.0 2.6 collective-permute-done.116
  677.4 3.0 fusion.18
  682.8 2.8 place_rows.4
  690.6 4.0 collective-permute-start.56
  (746 shorter events, 231.8 us)
Async XLA Ops:
  7.3 87.8 %all-gather.2.cloned.1.call-start = ((), (), s32[]{:S(2)}) async-start(), calls=%async_computation.1 | async-start | bytes 5242880 | tf_op jit(solution)/shard_map/all_gather | solution.py:585
  12.0 665.3 %reduce-scatter.2.cloned.1.call-start = ((), (), s32[]{:S(2)}) async-start(), calls=%async_computation.2 | async-start | bytes 5242880 | tf_op jit(solution)/shard_map/reduce_scatter | solution.py:751
  12.1 33.3 %collective-permute-start.13 = (f32[1024]{0:T(1024)}, f32[1024]{0:T(1024)}, u32[]{:S(2)}, u32[]{:S(2)}) collective-permute-start(f32[1024]{0:T(1024)} %param.52), channel_id=1, source_target_pairs={{0,1},{1,2},{2,3},{3,0},{4,5},{5,6},{6,7},{7,4},{8,9},{9,10},{10,1... | collective-permute-start | bytes 12296 | tf_op jit(solution)/shard_map/ppermute | solution.py:268
  14.3 31.8 %collective-permute-start.14 = (f32[1024]{0:T(1024)}, f32[1024]{0:T(1024)}, u32[]{:S(2)}, u32[]{:S(2)}) collective-permute-start(f32[1024]{0:T(1024)} %param.52), channel_id=1, source_target_pairs={{0,2},{1,3},{2,0},{3,1},{4,6},{5,7},{6,4},{7,5},{8,10},{9,11},{10,... | collective-permute-start | bytes 12296 | tf_op jit(solution)/shard_map/ppermute | solution.py:268
  16.6 30.3 %collective-permute-start.15 = (f32[1024]{0:T(1024)}, f32[1024]{0:T(1024)}, u32[]{:S(2)}, u32[]{:S(2)}) collective-permute-start(f32[1024]{0:T(1024)} %param.52), channel_id=1, source_target_pairs={{0,3},{1,0},{2,1},{3,2},{4,7},{5,4},{6,5},{7,6},{8,11},{9,8},{10,9... | collective-permute-start | bytes 12296 | tf_op jit(solution)/shard_map/ppermute | solution.py:268
  95.0 32.1 %collective-permute-start.3 = (bf16[32,1024]{1,0:T(8,128)(2,1)}, bf16[32,1024]{1,0:T(8,128)(2,1)S(1)}, u32[]{:S(2)}, u32[]{:S(2)}) collective-permute-start(bf16[32,1024]{1,0:T(8,128)(2,1)} %constant_dynamic-slice_fusion.31), channel_id=1, source_target_pairs={{0,1},{1,2},{2,3},{3,0},{4,5},{5,6},{6,7},{7,4},{8,9},{9,10},{10,1... | collective-permute-start | bytes 196616 | tf_op jit(solution)/shard_map/ppermute | solution.py:268
  95.0 35.2 %collective-permute-start.4 = (bf16[32,1024]{1,0:T(8,128)(2,1)}, bf16[32,1024]{1,0:T(8,128)(2,1)S(1)}, u32[]{:S(2)}, u32[]{:S(2)}) collective-permute-start(bf16[32,1024]{1,0:T(8,128)(2,1)} %constant_dynamic-slice_fusion.31), channel_id=1, source_target_pairs={{0,2},{1,3},{2,0},{3,1},{4,6},{5,7},{6,4},{7,5},{8,10},{9,11},{10,... | collective-permute-start | bytes 196616 | tf_op jit(solution)/shard_map/ppermute | solution.py:268
  95.8 34.4 %collective-permute-start.5 = (bf16[32,1024]{1,0:T(8,128)(2,1)}, bf16[32,1024]{1,0:T(8,128)(2,1)S(1)}, u32[]{:S(2)}, u32[]{:S(2)}) collective-permute-start(bf16[32,1024]{1,0:T(8,128)(2,1)} %constant_dynamic-slice_fusion.31), channel_id=1, source_target_pairs={{0,3},{1,0},{2,1},{3,2},{4,7},{5,4},{6,5},{7,6},{8,11},{9,8},{10,9... | collective-permute-start | bytes 196616 | tf_op jit(solution)/shard_map/ppermute | solution.py:268
  98.3 32.9 %collective-permute-start.16 = (bf16[128,1024]{1,0:T(8,128)(2,1)}, bf16[128,1024]{1,0:T(8,128)(2,1)S(1)}, u32[]{:S(2)}, u32[]{:S(2)}) collective-permute-start(bf16[128,1024]{1,0:T(8,128)(2,1)} %bitcast.42), channel_id=1, source_target_pairs={{0,1},{1,2},{2,3},{3,0},{4,5},{5,6},{6,7},{7,4},{8,9},{9,10},{10,1... | collective-permute-start | bytes 786440 | tf_op jit(solution)/shard_map/ppermute | solution.py:268
  98.9 34.7 %collective-permute-start.17 = (bf16[128,1024]{1,0:T(8,128)(2,1)}, bf16[128,1024]{1,0:T(8,128)(2,1)S(1)}, u32[]{:S(2)}, u32[]{:S(2)}) collective-permute-start(bf16[128,1024]{1,0:T(8,128)(2,1)} %bitcast.42), channel_id=1, source_target_pairs={{0,2},{1,3},{2,0},{3,1},{4,6},{5,7},{6,4},{7,5},{8,10},{9,11},{10,... | collective-permute-start | bytes 786440 | tf_op jit(solution)/shard_map/ppermute | solution.py:268
  130.2 14.1 %collective-permute-start.33 = (bf16[128,1024]{1,0:T(8,128)(2,1)S(1)}, bf16[128,1024]{1,0:T(8,128)(2,1)S(1)}, u32[]{:S(2)}, u32[]{:S(2)}) collective-permute-start(bf16[128,1024]{1,0:T(8,128)(2,1)S(1)} %copy-done.57), channel_id=1, source_target_pairs={{0,1},{1,2},{2,3},{3,0},{4,5},{5,6},{6,7},{7,4},{8,9},{9,10},{10,1... | collective-permute-start | bytes 786440 | tf_op jit(solution)/shard_map/ppermute | solution.py:268
  130.2 21.9 %collective-permute-start.34 = (bf16[128,1024]{1,0:T(8,128)(2,1)S(1)}, bf16[128,1024]{1,0:T(8,128)(2,1)S(1)}, u32[]{:S(2)}, u32[]{:S(2)}) collective-permute-start(bf16[128,1024]{1,0:T(8,128)(2,1)S(1)} %copy-done.57), channel_id=1, source_target_pairs={{0,2},{1,3},{2,0},{3,1},{4,6},{5,7},{6,4},{7,5},{8,10},{9,11},{10,... | collective-permute-start | bytes 786440 | tf_op jit(solution)/shard_map/ppermute | solution.py:268
  131.2 33.3 %collective-permute-start.35 = (bf16[128,1024]{1,0:T(8,128)(2,1)S(1)}, bf16[128,1024]{1,0:T(8,128)(2,1)S(1)}, u32[]{:S(2)}, u32[]{:S(2)}) collective-permute-start(bf16[128,1024]{1,0:T(8,128)(2,1)S(1)} %copy-done.57), channel_id=1, source_target_pairs={{0,3},{1,0},{2,1},{3,2},{4,7},{5,4},{6,5},{7,6},{8,11},{9,8},{10,9... | collective-permute-start | bytes 786440 | tf_op jit(solution)/shard_map/ppermute | solution.py:268
  133.6 37.8 %collective-permute-start = (bf16[512,256]{1,0:T(8,128)(2,1)S(1)}, bf16[512,256]{1,0:T(8,128)(2,1)S(1)}, u32[]{:S(2)}, u32[]{:S(2)}) collective-permute-start(bf16[512,256]{1,0:T(8,128)(2,1)S(1)} %get-tuple-element.188), channel_id=1, source_target_pairs={{0,1},{1,2},{2,3},{3,0},{4,5},{5,6},{6,7},{7,4},{8,9},{9,10},{10,1... | collective-permute-start | bytes 786440 | tf_op jit(solution)/shard_map/ppermute | solution.py:268
  134.1 31.7 %collective-permute-start.6 = (bf16[3,32,1024]{2,1,0:T(8,128)(2,1)S(1)}, bf16[3,32,1024]{2,1,0:T(8,128)(2,1)S(1)}, u32[]{:S(2)}, u32[]{:S(2)}) collective-permute-start(bf16[3,32,1024]{2,1,0:T(8,128)(2,1)S(1)} %pad_maximum_fusion.12), channel_id=1, source_target_pairs={{0,4},{4,0},{8,12},{12,8},{16,20},{20,16},{24,28},{28,24},{1,5},{5... | collective-permute-start | bytes 589832 | tf_op jit(solution)/shard_map/ppermute | solution.py:273
  144.3 30.1 %collective-permute-start.1 = (bf16[512,256]{1,0:T(8,128)(2,1)S(1)}, bf16[512,256]{1,0:T(8,128)(2,1)S(1)}, u32[]{:S(2)}, u32[]{:S(2)}) collective-permute-start(bf16[512,256]{1,0:T(8,128)(2,1)S(1)} %get-tuple-element.187), channel_id=1, source_target_pairs={{0,2},{1,3},{2,0},{3,1},{4,6},{5,7},{6,4},{7,5},{8,10},{9,11},{10,... | collective-permute-start | bytes 786440 | tf_op jit(solution)/shard_map/ppermute | solution.py:268
  152.1 27.5 %collective-permute-start.2 = (bf16[512,256]{1,0:T(8,128)(2,1)S(1)}, bf16[512,256]{1,0:T(8,128)(2,1)S(1)}, u32[]{:S(2)}, u32[]{:S(2)}) collective-permute-start(bf16[512,256]{1,0:T(8,128)(2,1)S(1)} %get-tuple-element.186), channel_id=1, source_target_pairs={{0,3},{1,0},{2,1},{3,2},{4,7},{5,4},{6,5},{7,6},{8,11},{9,8},{10,9... | collective-permute-start | bytes 786440 | tf_op jit(solution)/shard_map/ppermute | solution.py:268
  169.0 22.9 %collective-permute-start.20 = (bf16[3,64,1024]{2,1,0:T(8,128)(2,1)S(1)}, bf16[3,64,1024]{2,1,0:T(8,128)(2,1)S(1)}, u32[]{:S(2)}, u32[]{:S(2)}) collective-permute-start(bf16[3,64,1024]{2,1,0:T(8,128)(2,1)S(1)} %get-tuple-element.193.refs_11_), channel_id=1, source_target_pairs={{0,16},{4,20},{8,24},{12,28},{16,0},{20,4},{24,8},{28,12},{1,17},{... | collective-permute-start | bytes 1179656 | tf_op jit(solution)/shard_map/ppermute | solution.py:273
  170.4 22.1 %collective-permute-start.26 = (bf16[3,64,1024]{2,1,0:T(8,128)(2,1)S(1)}, bf16[3,64,1024]{2,1,0:T(8,128)(2,1)S(1)}, u32[]{:S(2)}, u32[]{:S(2)}) collective-permute-start(bf16[3,64,1024]{2,1,0:T(8,128)(2,1)S(1)} %get-tuple-element.192.refs_19_), channel_id=1, source_target_pairs={{0,8},{4,12},{8,0},{12,4},{16,24},{20,28},{24,16},{28,20},{1,9},{5... | collective-permute-start | bytes 1179656 | tf_op jit(solution)/shard_map/ppermute | solution.py:273
  171.4 22.0 %collective-permute-start.37 = (bf16[3,64,1024]{2,1,0:T(8,128)(2,1)S(1)}, bf16[3,64,1024]{2,1,0:T(8,128)(2,1)S(1)}, u32[]{:S(2)}, u32[]{:S(2)}) collective-permute-start(bf16[3,64,1024]{2,1,0:T(8,128)(2,1)S(1)} %get-tuple-element.191.refs_27_), channel_id=1, source_target_pairs={{0,16},{4,20},{8,24},{12,28},{16,0},{20,4},{24,8},{28,12},{1,17},{... | collective-permute-start | bytes 1179656 | tf_op jit(solution)/shard_map/ppermute | solution.py:273
  189.7 28.5 %collective-permute-start.19 = (bf16[3,64,1024]{2,1,0:T(8,128)(2,1)S(1)}, bf16[3,64,1024]{2,1,0:T(8,128)(2,1)S(1)}, u32[]{:S(2)}, u32[]{:S(2)}) collective-permute-start(bf16[3,64,1024]{2,1,0:T(8,128)(2,1)S(1)} %get-tuple-element.193.refs_11_), channel_id=1, source_target_pairs={{0,8},{4,12},{8,0},{12,4},{16,24},{20,28},{24,16},{28,20},{1,9},{5... | collective-permute-start | bytes 1179656 | tf_op jit(solution)/shard_map/ppermute | solution.py:273
  190.8 27.5 %collective-permute-start.27 = (bf16[3,64,1024]{2,1,0:T(8,128)(2,1)S(1)}, bf16[3,64,1024]{2,1,0:T(8,128)(2,1)S(1)}, u32[]{:S(2)}, u32[]{:S(2)}) collective-permute-start(bf16[3,64,1024]{2,1,0:T(8,128)(2,1)S(1)} %get-tuple-element.192.refs_19_), channel_id=1, source_target_pairs={{0,16},{4,20},{8,24},{12,28},{16,0},{20,4},{24,8},{28,12},{1,17},{... | collective-permute-start | bytes 1179656 | tf_op jit(solution)/shard_map/ppermute | solution.py:273
  192.0 26.8 %collective-permute-start.36 = (bf16[3,64,1024]{2,1,0:T(8,128)(2,1)S(1)}, bf16[3,64,1024]{2,1,0:T(8,128)(2,1)S(1)}, u32[]{:S(2)}, u32[]{:S(2)}) collective-permute-start(bf16[3,64,1024]{2,1,0:T(8,128)(2,1)S(1)} %get-tuple-element.191.refs_27_), channel_id=1, source_target_pairs={{0,8},{4,12},{8,0},{12,4},{16,24},{20,28},{24,16},{28,20},{1,9},{5... | collective-permute-start | bytes 1179656 | tf_op jit(solution)/shard_map/ppermute | solution.py:273
  192.5 24.9 %collective-permute-start.43 = (bf16[3,64,1024]{2,1,0:T(8,128)(2,1)S(1)}, bf16[3,64,1024]{2,1,0:T(8,128)(2,1)S(1)}, u32[]{:S(2)}, u32[]{:S(2)}) collective-permute-start(bf16[3,64,1024]{2,1,0:T(8,128)(2,1)S(1)} %get-tuple-element.190.refs_35_), channel_id=1, source_target_pairs={{0,8},{4,12},{8,0},{12,4},{16,24},{20,28},{24,16},{28,20},{1,9},{5... | collective-permute-start | bytes 1179656 | tf_op jit(solution)/shard_map/ppermute | solution.py:273
  193.4 25.4 %collective-permute-start.44 = (bf16[3,64,1024]{2,1,0:T(8,128)(2,1)S(1)}, bf16[3,64,1024]{2,1,0:T(8,128)(2,1)S(1)}, u32[]{:S(2)}, u32[]{:S(2)}) collective-permute-start(bf16[3,64,1024]{2,1,0:T(8,128)(2,1)S(1)} %get-tuple-element.190.refs_35_), channel_id=1, source_target_pairs={{0,16},{4,20},{8,24},{12,28},{16,0},{20,4},{24,8},{28,12},{1,17},{... | collective-permute-start | bytes 1179656 | tf_op jit(solution)/shard_map/ppermute | solution.py:273
  219.5 21.2 %collective-permute-start.24 = (bf16[3,64,1024]{2,1,0:T(8,128)(2,1)S(1)}, bf16[3,64,1024]{2,1,0:T(8,128)(2,1)S(1)}, u32[]{:S(2)}, u32[]{:S(2)}) collective-permute-start(bf16[3,64,1024]{2,1,0:T(8,128)(2,1)S(1)} %collective-permute-done.20.refs_13_), channel_id=1, source_target_pairs={{0,4},{4,0},{8,12},{12,8},{16,20},{20,16},{24,28},{28,24},{1,5},{5... | collective-permute-start | bytes 1179656 | tf_op jit(solution)/shard_map/ppermute | solution.py:273
  221.3 19.5 %collective-permute-start.30 = (bf16[3,64,1024]{2,1,0:T(8,128)(2,1)S(1)}, bf16[3,64,1024]{2,1,0:T(8,128)(2,1)S(1)}, u32[]{:S(2)}, u32[]{:S(2)}) collective-permute-start(bf16[3,64,1024]{2,1,0:T(8,128)(2,1)S(1)} %collective-permute-done.26.refs_20_), channel_id=1, source_target_pairs={{0,4},{4,0},{8,12},{12,8},{16,20},{20,16},{24,28},{28,24},{1,5},{5... | collective-permute-start | bytes 1179656 | tf_op jit(solution)/shard_map/ppermute | solution.py:273
  221.9 15.6 %collective-permute-start.38 = (bf16[3,64,1024]{2,1,0:T(8,128)(2,1)S(1)}, bf16[3,64,1024]{2,1,0:T(8,128)(2,1)S(1)}, u32[]{:S(2)}, u32[]{:S(2)}) collective-permute-start(bf16[3,64,1024]{2,1,0:T(8,128)(2,1)S(1)} %collective-permute-done.37.refs_29_), channel_id=1, source_target_pairs={{0,8},{4,12},{8,0},{12,4},{16,24},{20,28},{24,16},{28,20},{1,9},{5... | collective-permute-start | bytes 1179656 | tf_op jit(solution)/shard_map/ppermute | solution.py:273
  230.4 11.0 %collective-permute-start.41 = (bf16[3,64,1024]{2,1,0:T(8,128)(2,1)S(1)}, bf16[3,64,1024]{2,1,0:T(8,128)(2,1)S(1)}, u32[]{:S(2)}, u32[]{:S(2)}) collective-permute-start(bf16[3,64,1024]{2,1,0:T(8,128)(2,1)S(1)} %collective-permute-done.37.refs_29_), channel_id=1, source_target_pairs={{0,4},{4,0},{8,12},{12,8},{16,20},{20,16},{24,28},{28,24},{1,5},{5... | collective-permute-start | bytes 1179656 | tf_op jit(solution)/shard_map/ppermute | solution.py:273
  344.4 20.8 %collective-permute-start.50 = (bf16[512,256]{1,0:T(8,128)(2,1)}, bf16[512,256]{1,0:T(8,128)(2,1)S(1)}, u32[]{:S(2)}, u32[]{:S(2)}) collective-permute-start(bf16[512,256]{1,0:T(8,128)(2,1)} %get-tuple-element.53), channel_id=1, source_target_pairs={{0,3},{1,0},{2,1},{3,2},{4,7},{5,4},{6,5},{7,6},{8,11},{9,8},{10,9... | collective-permute-start | bytes 786440 | tf_op jit(solution)/shard_map/ppermute | solution.py:268
  347.4 27.3 %collective-permute-start.51 = (bf16[512,256]{1,0:T(8,128)(2,1)}, bf16[512,256]{1,0:T(8,128)(2,1)S(1)}, u32[]{:S(2)}, u32[]{:S(2)}) collective-permute-start(bf16[512,256]{1,0:T(8,128)(2,1)} %get-tuple-element.54), channel_id=1, source_target_pairs={{0,2},{1,3},{2,0},{3,1},{4,6},{5,7},{6,4},{7,5},{8,10},{9,11},{10,... | collective-permute-start | bytes 786440 | tf_op jit(solution)/shard_map/ppermute | solution.py:268
  351.5 23.1 %collective-permute-start.52 = (bf16[512,256]{1,0:T(8,128)(2,1)}, bf16[512,256]{1,0:T(8,128)(2,1)S(1)}, u32[]{:S(2)}, u32[]{:S(2)}) collective-permute-start(bf16[512,256]{1,0:T(8,128)(2,1)} %get-tuple-element.55), channel_id=1, source_target_pairs={{0,1},{1,2},{2,3},{3,0},{4,5},{5,6},{6,7},{7,4},{8,9},{9,10},{10,1... | collective-permute-start | bytes 786440 | tf_op jit(solution)/shard_map/ppermute | solution.py:268
  438.3 36.3 %collective-permute-start.75 = (bf16[2,2,4,32,1024]{4,3,2,0,1:T(8,128)(2,1)S(1)}, bf16[2,2,4,32,1024]{4,3,2,0,1:T(8,128)(2,1)S(1)}, u32[]{:S(2)}, u32[]{:S(2)}) collective-permute-start(bf16[2,2,4,32,1024]{4,3,2,0,1:T(8,128)(2,1)S(1)} %bitcast.444), channel_id=1, source_target_pairs={{0,4},{4,0},{8,12},{12,8},{16,20},{20,16},{24,28},{28,24},{1,5},{5... | collective-permute-start | bytes 3145736 | tf_op jit(solution)/shard_map/ppermute | solution.py:273
  454.1 17.9 %collective-permute-start.59 = (bf16[2,2,128,768]{3,2,0,1:T(8,128)(2,1)}, bf16[2,2,128,768]{3,2,0,1:T(8,128)(2,1)}, u32[]{:S(2)}, u32[]{:S(2)}) collective-permute-start(bf16[2,2,128,768]{3,2,0,1:T(8,128)(2,1)} %fusion.37), channel_id=1, source_target_pairs={{0,4},{4,0},{8,12},{12,8},{16,20},{20,16},{24,28},{28,24},{1,5},{5... | collective-permute-start | bytes 2359304 | tf_op jit(solution)/shard_map/ppermute | solution.py:273
  456.2 12.4 %collective-permute-start.73 = (f32[152,128]{1,0:T(8,128)}, f32[152,128]{1,0:T(8,128)}, u32[]{:S(2)}, u32[]{:S(2)}) collective-permute-start(f32[152,128]{1,0:T(8,128)} %slice.437), channel_id=1, source_target_pairs={{0,2},{1,3},{2,0},{3,1},{4,6},{5,7},{6,4},{7,5},{8,10},{9,11},{10,... | collective-permute-start | bytes 233480 | tf_op jit(solution)/shard_map/ppermute | solution.py:268
  456.2 14.1 %collective-permute-start.74 = (f32[152,128]{1,0:T(8,128)}, f32[152,128]{1,0:T(8,128)}, u32[]{:S(2)}, u32[]{:S(2)}) collective-permute-start(f32[152,128]{1,0:T(8,128)} %slice.437), channel_id=1, source_target_pairs={{0,3},{1,0},{2,1},{3,2},{4,7},{5,4},{6,5},{7,6},{8,11},{9,8},{10,9... | collective-permute-start | bytes 233480 | tf_op jit(solution)/shard_map/ppermute | solution.py:268
  463.6 81.3 %collective-permute-start.103 = (bf16[2,2,2,4,64,1024]{5,4,3,1,2,0:T(8,128)(2,1)}, bf16[2,2,2,4,64,1024]{5,4,3,1,2,0:T(8,128)(2,1)}, u32[]{:S(2)}, u32[]{:S(2)}) collective-permute-start(bf16[2,2,2,4,64,1024]{5,4,3,1,2,0:T(8,128)(2,1)} %copy.114), channel_id=1, source_target_pairs={{0,4},{4,0},{8,12},{12,8},{16,20},{20,16},{24,28},{28,24},{1,5},{5... | collective-permute-start | bytes 12582920 | tf_op jit(solution)/shard_map/ppermute | solution.py:273
  468.5 82.5 %collective-permute-start.88 = (bf16[2,2,2,4,64,1024]{5,4,3,1,2,0:T(8,128)(2,1)}, bf16[2,2,2,4,64,1024]{5,4,3,1,2,0:T(8,128)(2,1)}, u32[]{:S(2)}, u32[]{:S(2)}) collective-permute-start(bf16[2,2,2,4,64,1024]{5,4,3,1,2,0:T(8,128)(2,1)} %copy.111), channel_id=1, source_target_pairs={{0,4},{4,0},{8,12},{12,8},{16,20},{20,16},{24,28},{28,24},{1,5},{5... | collective-permute-start | bytes 12582920 | tf_op jit(solution)/shard_map/ppermute | solution.py:273
  475.0 20.9 %collective-permute-start.76 = (bf16[2,4,32,1024]{3,2,1,0:T(8,128)(2,1)S(1)}, bf16[2,4,32,1024]{3,2,1,0:T(8,128)(2,1)S(1)}, u32[]{:S(2)}, u32[]{:S(2)}) collective-permute-start(bf16[2,4,32,1024]{3,2,1,0:T(8,128)(2,1)S(1)} %dynamic-slice_bitcast_fusion), channel_id=1, source_target_pairs={{0,8},{4,12},{8,0},{12,4},{16,24},{20,28},{24,16},{28,20},{1,9},{5... | collective-permute-start | bytes 1572872 | tf_op jit(solution)/shard_map/ppermute | solution.py:273
  484.9 14.0 %collective-permute-start.61 = (bf16[128,768]{1,0:T(8,128)(2,1)S(1)}, bf16[128,768]{1,0:T(8,128)(2,1)S(1)}, u32[]{:S(2)}, u32[]{:S(2)}) collective-permute-start(bf16[128,768]{1,0:T(8,128)(2,1)S(1)} %dynamic-slice_bitcast_fusion.7), channel_id=1, source_target_pairs={{0,16},{4,20},{8,24},{12,28},{16,0},{20,4},{24,8},{28,12},{1,17},{... | collective-permute-start | bytes 589832 | tf_op jit(solution)/shard_map/ppermute | solution.py:273
  507.0 11.7 %collective-permute-start.79 = (bf16[32,1024]{1,0:T(8,128)(2,1)S(1)}, bf16[32,1024]{1,0:T(8,128)(2,1)S(1)}, u32[]{:S(2)}, u32[]{:S(2)}) collective-permute-start(bf16[32,1024]{1,0:T(8,128)(2,1)S(1)} %get-tuple-element.196), channel_id=1, source_target_pairs={{0,2},{1,3},{2,0},{3,1},{4,6},{5,7},{6,4},{7,5},{8,10},{9,11},{10,... | collective-permute-start | bytes 196616 | tf_op jit(solution)/shard_map/ppermute | solution.py:268
  507.0 12.7 %collective-permute-start.80 = (bf16[32,1024]{1,0:T(8,128)(2,1)S(1)}, bf16[32,1024]{1,0:T(8,128)(2,1)S(1)}, u32[]{:S(2)}, u32[]{:S(2)}) collective-permute-start(bf16[32,1024]{1,0:T(8,128)(2,1)S(1)} %get-tuple-element.195), channel_id=1, source_target_pairs={{0,1},{1,2},{2,3},{3,0},{4,5},{5,6},{6,7},{7,4},{8,9},{9,10},{10,1... | collective-permute-start | bytes 196616 | tf_op jit(solution)/shard_map/ppermute | solution.py:268
  511.3 14.0 %collective-permute-start.63 = (bf16[128,768]{1,0:T(8,128)(2,1)S(1)}, bf16[128,768]{1,0:T(8,128)(2,1)S(1)}, u32[]{:S(2)}, u32[]{:S(2)}) collective-permute-start(bf16[128,768]{1,0:T(8,128)(2,1)S(1)} %get-tuple-element.169), channel_id=1, source_target_pairs={{0,8},{4,12},{8,0},{12,4},{16,24},{20,28},{24,16},{28,20},{1,9},{5... | collective-permute-start | bytes 589832 | tf_op jit(solution)/shard_map/ppermute | solution.py:273
  518.7 11.2 %collective-permute-start.65 = (bf16[128,768]{1,0:T(8,128)(2,1)S(1)}, bf16[128,768]{1,0:T(8,128)(2,1)S(1)}, u32[]{:S(2)}, u32[]{:S(2)}) collective-permute-start(bf16[128,768]{1,0:T(8,128)(2,1)S(1)} %get-tuple-element.169), channel_id=1, source_target_pairs={{0,16},{4,20},{8,24},{12,28},{16,0},{20,4},{24,8},{28,12},{1,17},{... | collective-permute-start | bytes 589832 | tf_op jit(solution)/shard_map/ppermute | solution.py:273
  531.1 12.5 %collective-permute-start.66 = (bf16[128,768]{1,0:T(8,128)(2,1)S(1)}, bf16[128,768]{1,0:T(8,128)(2,1)S(1)}, u32[]{:S(2)}, u32[]{:S(2)}) collective-permute-start(bf16[128,768]{1,0:T(8,128)(2,1)S(1)} %collective-permute-done.65), channel_id=1, source_target_pairs={{0,4},{4,0},{8,12},{12,8},{16,20},{20,16},{24,28},{28,24},{1,5},{5... | collective-permute-start | bytes 589832 | tf_op jit(solution)/shard_map/ppermute | solution.py:273
  541.2 97.6 %collective-permute-start.68 = (bf16[128,768]{1,0:T(8,128)(2,1)}, bf16[128,768]{1,0:T(8,128)(2,1)}, u32[]{:S(2)}, u32[]{:S(2)}) collective-permute-start(bf16[128,768]{1,0:T(8,128)(2,1)} %collective-permute-done.67), channel_id=1, source_target_pairs={{0,4},{4,0},{8,12},{12,8},{16,20},{20,16},{24,28},{28,24},{1,5},{5... | collective-permute-start | bytes 589832 | tf_op jit(solution)/shard_map/ppermute | solution.py:273
  549.2 24.9 %collective-permute-start.106 = (bf16[2,4,64,1024]{3,2,1,0:T(8,128)(2,1)S(1)}, bf16[2,4,64,1024]{3,2,1,0:T(8,128)(2,1)S(1)}, u32[]{:S(2)}, u32[]{:S(2)}) collective-permute-start(bf16[2,4,64,1024]{3,2,1,0:T(8,128)(2,1)S(1)} %slice_bitcast_fusion.2), channel_id=1, source_target_pairs={{0,16},{4,20},{8,24},{12,28},{16,0},{20,4},{24,8},{28,12},{1,17},{... | collective-permute-start | bytes 3145736 | tf_op jit(solution)/shard_map/ppermute | solution.py:273
  550.3 25.0 %collective-permute-start.104 = (bf16[2,4,64,1024]{3,2,1,0:T(8,128)(2,1)S(1)}, bf16[2,4,64,1024]{3,2,1,0:T(8,128)(2,1)S(1)}, u32[]{:S(2)}, u32[]{:S(2)}) collective-permute-start(bf16[2,4,64,1024]{3,2,1,0:T(8,128)(2,1)S(1)} %slice_bitcast_fusion.4), channel_id=1, source_target_pairs={{0,8},{4,12},{8,0},{12,4},{16,24},{20,28},{24,16},{28,20},{1,9},{5... | collective-permute-start | bytes 3145736 | tf_op jit(solution)/shard_map/ppermute | solution.py:273
  556.5 40.0 %collective-permute-start.91 = (bf16[2,4,64,1024]{3,2,1,0:T(8,128)(2,1)S(1)}, bf16[2,4,64,1024]{3,2,1,0:T(8,128)(2,1)S(1)}, u32[]{:S(2)}, u32[]{:S(2)}) collective-permute-start(bf16[2,4,64,1024]{3,2,1,0:T(8,128)(2,1)S(1)} %slice_bitcast_fusion.6), channel_id=1, source_target_pairs={{0,16},{4,20},{8,24},{12,28},{16,0},{20,4},{24,8},{28,12},{1,17},{... | collective-permute-start | bytes 3145736 | tf_op jit(solution)/shard_map/ppermute | solution.py:273
  557.7 40.1 %collective-permute-start.89 = (bf16[2,4,64,1024]{3,2,1,0:T(8,128)(2,1)S(1)}, bf16[2,4,64,1024]{3,2,1,0:T(8,128)(2,1)S(1)}, u32[]{:S(2)}, u32[]{:S(2)}) collective-permute-start(bf16[2,4,64,1024]{3,2,1,0:T(8,128)(2,1)S(1)} %slice_bitcast_fusion.8), channel_id=1, source_target_pairs={{0,8},{4,12},{8,0},{12,4},{16,24},{20,28},{24,16},{28,20},{1,9},{5... | collective-permute-start | bytes 3145736 | tf_op jit(solution)/shard_map/ppermute | solution.py:273
  574.5 34.0 %collective-permute-start.107 = (bf16[4,64,1024]{2,1,0:T(8,128)(2,1)S(1)}, bf16[4,64,1024]{2,1,0:T(8,128)(2,1)S(1)}, u32[]{:S(2)}, u32[]{:S(2)}) collective-permute-start(bf16[4,64,1024]{2,1,0:T(8,128)(2,1)S(1)} %slice_bitcast_fusion.10), channel_id=1, source_target_pairs={{0,8},{4,12},{8,0},{12,4},{16,24},{20,28},{24,16},{28,20},{1,9},{5... | collective-permute-start | bytes 1572872 | tf_op jit(solution)/shard_map/ppermute | solution.py:273
  575.8 33.0 %collective-permute-start.105 = (bf16[4,64,1024]{2,1,0:T(8,128)(2,1)S(1)}, bf16[4,64,1024]{2,1,0:T(8,128)(2,1)S(1)}, u32[]{:S(2)}, u32[]{:S(2)}) collective-permute-start(bf16[4,64,1024]{2,1,0:T(8,128)(2,1)S(1)} %slice_bitcast_fusion.12), channel_id=1, source_target_pairs={{0,16},{4,20},{8,24},{12,28},{16,0},{20,4},{24,8},{28,12},{1,17},{... | collective-permute-start | bytes 1572872 | tf_op jit(solution)/shard_map/ppermute | solution.py:273
  597.0 22.8 %collective-permute-start.92 = (bf16[4,64,1024]{2,1,0:T(8,128)(2,1)S(1)}, bf16[4,64,1024]{2,1,0:T(8,128)(2,1)S(1)}, u32[]{:S(2)}, u32[]{:S(2)}) collective-permute-start(bf16[4,64,1024]{2,1,0:T(8,128)(2,1)S(1)} %slice_bitcast_fusion.14), channel_id=1, source_target_pairs={{0,8},{4,12},{8,0},{12,4},{16,24},{20,28},{24,16},{28,20},{1,9},{5... | collective-permute-start | bytes 1572872 | tf_op jit(solution)/shard_map/ppermute | solution.py:273
  598.2 21.8 %collective-permute-start.90 = (bf16[4,64,1024]{2,1,0:T(8,128)(2,1)S(1)}, bf16[4,64,1024]{2,1,0:T(8,128)(2,1)S(1)}, u32[]{:S(2)}, u32[]{:S(2)}) collective-permute-start(bf16[4,64,1024]{2,1,0:T(8,128)(2,1)S(1)} %slice_bitcast_fusion.16), channel_id=1, source_target_pairs={{0,16},{4,20},{8,24},{12,28},{16,0},{20,4},{24,8},{28,12},{1,17},{... | collective-permute-start | bytes 1572872 | tf_op jit(solution)/shard_map/ppermute | solution.py:273
  609.0 16.5 %collective-permute-start.108 = (bf16[128,1024]{1,0:T(8,128)(2,1)S(1)}, bf16[128,1024]{1,0:T(8,128)(2,1)S(1)}, u32[]{:S(2)}, u32[]{:S(2)}) collective-permute-start(bf16[128,1024]{1,0:T(8,128)(2,1)S(1)} %get-tuple-element.176), channel_id=1, source_target_pairs={{0,3},{1,0},{2,1},{3,2},{4,7},{5,4},{6,5},{7,6},{8,11},{9,8},{10,9... | collective-permute-start | bytes 786440 | tf_op jit(solution)/shard_map/ppermute | solution.py:268
  609.1 22.8 %collective-permute-start.109 = (bf16[128,1024]{1,0:T(8,128)(2,1)S(1)}, bf16[128,1024]{1,0:T(8,128)(2,1)S(1)}, u32[]{:S(2)}, u32[]{:S(2)}) collective-permute-start(bf16[128,1024]{1,0:T(8,128)(2,1)S(1)} %get-tuple-element.178), channel_id=1, source_target_pairs={{0,2},{1,3},{2,0},{3,1},{4,6},{5,7},{6,4},{7,5},{8,10},{9,11},{10,... | collective-permute-start | bytes 786440 | tf_op jit(solution)/shard_map/ppermute | solution.py:268
  619.8 12.4 %collective-permute-start.110 = (bf16[128,1024]{1,0:T(8,128)(2,1)S(1)}, bf16[128,1024]{1,0:T(8,128)(2,1)S(1)}, u32[]{:S(2)}, u32[]{:S(2)}) collective-permute-start(bf16[128,1024]{1,0:T(8,128)(2,1)S(1)} %get-tuple-element.177), channel_id=1, source_target_pairs={{0,1},{1,2},{2,3},{3,0},{4,5},{5,6},{6,7},{7,4},{8,9},{9,10},{10,1... | collective-permute-start | bytes 786440 | tf_op jit(solution)/shard_map/ppermute | solution.py:268
  621.1 25.5 %collective-permute-start.93 = (bf16[128,1024]{1,0:T(8,128)(2,1)S(1)}, bf16[128,1024]{1,0:T(8,128)(2,1)S(1)}, u32[]{:S(2)}, u32[]{:S(2)}) collective-permute-start(bf16[128,1024]{1,0:T(8,128)(2,1)S(1)} %get-tuple-element.179), channel_id=1, source_target_pairs={{0,3},{1,0},{2,1},{3,2},{4,7},{5,4},{6,5},{7,6},{8,11},{9,8},{10,9... | collective-permute-start | bytes 786440 | tf_op jit(solution)/shard_map/ppermute | solution.py:268
  625.5 29.8 %collective-permute-start.94 = (bf16[128,1024]{1,0:T(8,128)(2,1)}, bf16[128,1024]{1,0:T(8,128)(2,1)}, u32[]{:S(2)}, u32[]{:S(2)}) collective-permute-start(bf16[128,1024]{1,0:T(8,128)(2,1)} %get-tuple-element.181), channel_id=1, source_target_pairs={{0,2},{1,3},{2,0},{3,1},{4,6},{5,7},{6,4},{7,5},{8,10},{9,11},{10,... | collective-permute-start | bytes 786440 | tf_op jit(solution)/shard_map/ppermute | solution.py:268
  631.9 23.4 %collective-permute-start.95 = (bf16[128,1024]{1,0:T(8,128)(2,1)}, bf16[128,1024]{1,0:T(8,128)(2,1)}, u32[]{:S(2)}, u32[]{:S(2)}) collective-permute-start(bf16[128,1024]{1,0:T(8,128)(2,1)} %get-tuple-element.180), channel_id=1, source_target_pairs={{0,1},{1,2},{2,3},{3,0},{4,5},{5,6},{6,7},{7,4},{8,9},{9,10},{10,1... | collective-permute-start | bytes 786440 | tf_op jit(solution)/shard_map/ppermute | solution.py:268
  633.1 26.0 %collective-permute-start.111 = (bf16[128,1024]{1,0:T(8,128)(2,1)S(1)}, bf16[128,1024]{1,0:T(8,128)(2,1)}, u32[]{:S(2)}, u32[]{:S(2)}) collective-permute-start(bf16[128,1024]{1,0:T(8,128)(2,1)S(1)} %get-tuple-element.157), channel_id=1, source_target_pairs={{0,4},{4,0},{8,12},{12,8},{16,20},{20,16},{24,28},{28,24},{1,5},{5... | collective-permute-start | bytes 786440 | tf_op jit(solution)/shard_map/ppermute | solution.py:273
  638.8 21.5 %collective-permute-start.112 = (bf16[128,1024]{1,0:T(8,128)(2,1)S(1)}, bf16[128,1024]{1,0:T(8,128)(2,1)}, u32[]{:S(2)}, u32[]{:S(2)}) collective-permute-start(bf16[128,1024]{1,0:T(8,128)(2,1)S(1)} %get-tuple-element.157), channel_id=1, source_target_pairs={{0,8},{4,12},{8,0},{12,4},{16,24},{20,28},{24,16},{28,20},{1,9},{5... | collective-permute-start | bytes 786440 | tf_op jit(solution)/shard_map/ppermute | solution.py:273
  646.6 14.4 %collective-permute-start.114 = (bf16[128,1024]{1,0:T(8,128)(2,1)S(1)}, bf16[128,1024]{1,0:T(8,128)(2,1)}, u32[]{:S(2)}, u32[]{:S(2)}) collective-permute-start(bf16[128,1024]{1,0:T(8,128)(2,1)S(1)} %get-tuple-element.157), channel_id=1, source_target_pairs={{0,16},{4,20},{8,24},{12,28},{16,0},{20,4},{24,8},{28,12},{1,17},{... | collective-permute-start | bytes 786440 | tf_op jit(solution)/shard_map/ppermute | solution.py:273
  660.9 14.8 %collective-permute-start.115 = (bf16[128,1024]{1,0:T(8,128)(2,1)}, bf16[128,1024]{1,0:T(8,128)(2,1)S(1)}, u32[]{:S(2)}, u32[]{:S(2)}) collective-permute-start(bf16[128,1024]{1,0:T(8,128)(2,1)} %collective-permute-done.114), channel_id=1, source_target_pairs={{0,4},{4,0},{8,12},{12,8},{16,20},{20,16},{24,28},{28,24},{1,5},{5... | collective-permute-start | bytes 786440 | tf_op jit(solution)/shard_map/ppermute | solution.py:273
  (198 other events, 2007.6 us)
Sparse Core Ops, SparseCore 0:
  12.1 82.8 all-gather.1
  454.7 82.4 reduce-scatter.1

commit v2 on v1

v2 whole, which is shorter than its diff:
```python
import functools
import math

import jax
import jax.numpy as jnp
import ml_dtypes
import numpy as np
from jax import lax
from jax.experimental import pallas as pl
from jax.experimental.pallas import tpu as pltpu
from jax.sharding import PartitionSpec as P

HIGHEST_MODE = lax.Precision.HIGHEST
EPSILON = 1e-05
FIRST_FACTOR = 64
CHUNK = 16
F32 = jnp.float32
BF16 = jnp.bfloat16
VMEM_SPEC = pl.BlockSpec(memory_space=pltpu.VMEM)
SMEM_SPEC = pl.BlockSpec(memory_space=pltpu.SMEM)
ANY_SPEC = pl.BlockSpec(memory_space=pl.ANY)


def norm_parts(values_in):
    centred = values_in - jnp.mean(values_in, axis=-1, keepdims=True)
    variance = jnp.mean(centred * centred, axis=-1, keepdims=True)
    scale = lax.rsqrt(variance + EPSILON)
    return centred * scale, scale


def norm_back(normal, scale, gain, grad):
    inner = grad * gain
    part = scale * (
        inner
        - jnp.mean(inner, axis=-1, keepdims=True)
        - normal * jnp.mean(inner * normal, axis=-1, keepdims=True)
    )
    return part, jnp.sum(grad * normal, axis=0), jnp.sum(grad, axis=0)


FEATURE_ROWS = 40
TAP_STEP = 256


def position_features(total, emb_count):
    place = np.arange(total, dtype=np.float64)
    bands = (emb_count - 1) // 2
    freq_grid = 1e-4 + np.arange(bands) * ((bands - 1 - 1e-4) / (bands - 1))
    angles = 2.0 * math.pi / total * freq_grid[:, None] * place[None, :]
    rows = np.concatenate([place[None] / (total - 1), np.cos(angles), -np.sin(angles)])
    rows = np.pad(rows, ((0, FEATURE_ROWS - emb_count), (0, 0)))
    return jnp.asarray(rows.astype(np.float32))


def exact(left, right, left_dim, right_dim):
    dims = (((left_dim,), (right_dim,)), ((), ()))
    return lax.dot_general(
        left, right, dims, precision=HIGHEST_MODE, preferred_element_type=F32
    )


def decay_block(first_row, rows, channels, seq_len, channel_total, group):
    slowest = math.log(0.01) / 1.5
    fastest = math.log(0.01) / 0.3
    row = lax.broadcasted_iota(jnp.int32, (rows, channels), 0) + first_row
    channel = lax.broadcasted_iota(jnp.int32, (rows, channels), 1) + group * channels
    rates = jnp.abs(slowest + (fastest - slowest) * channel.astype(F32) / (channel_total - 1))
    return jnp.exp(-(row.astype(F32) / (seq_len - 1)) * rates)


def filter_kernel(
    channel_total, here_ref, features_ref, enter_ref, middle_ref, inner_ref, columns_ref, filter_ref, *outs
):
    taps_ref, value_ref, sine_ref, cosine_ref = outs
    seq_len, channels = taps_ref.shape
    frequency = columns_ref[:, 3:4]
    hidden = features_ref[...]
    for n, weight_ref in enumerate((enter_ref, middle_ref, inner_ref)):
        value = exact(weight_ref[...], hidden, 0, 0) + columns_ref[:, n : n + 1]
        value_ref[n] = value
        hidden = jnp.sin(frequency * value)
        sine_ref[n] = hidden
        cosine_ref[n] = jnp.cos(frequency * value)
    for start in range(0, seq_len, TAP_STEP):
        rows = slice(start, start + TAP_STEP)
        decay = decay_block(start, TAP_STEP, channels, seq_len, channel_total, here_ref[1])
        taps = exact(sine_ref[2, :, rows], filter_ref[...], 0, 0)
        taps_ref[rows, :] = (taps * decay).astype(BF16)


def filter_back_kernel(
    channel_total,
    here_ref,
    features_ref,
    middle_ref,
    inner_ref,
    columns_ref,
    filter_ref,
    value_ref,
    sine_ref,
    cosine_ref,
    grad_ref,
    packed_ref,
    filter_grad_ref,
    hidden_ref,
):
    seq_len, channels = grad_ref.shape
    units = filter_ref.shape[0]
    frequency = columns_ref[:, 3:4]
    filter_grad_ref[...] = jnp.zeros_like(filter_grad_ref)
    for start in range(0, seq_len, TAP_STEP):
        rows = slice(start, start + TAP_STEP)
        decay = decay_block(start, TAP_STEP, channels, seq_len, channel_total, here_ref[1])
        grad = grad_ref[rows, :] * decay
        filter_grad_ref[...] += exact(sine_ref[2, :, rows], grad, 1, 0)
        hidden_ref[:, rows] = exact(filter_ref[...], grad, 1, 1)
    packed_ref[...] = jnp.zeros_like(packed_ref)
    grad = hidden_ref[...]
    frequency_grad = jnp.zeros((units, 1), F32)
    for n in (2, 1, 0):
        inside = grad * cosine_ref[n]
        frequency_grad += jnp.sum(inside * value_ref[n], axis=1, keepdims=True)
        inside = inside * frequency
        packed_ref[:, 3 * units + n : 3 * units + n + 1] = jnp.sum(inside, axis=1, keepdims=True)
        below = features_ref[...] if n == 0 else sine_ref[n - 1]
        packed_ref[: below.shape[0], n * units : (n + 1) * units] = exact(below, inside, 1, 1)
        if n > 0:
            grad = exact((middle_ref, inner_ref)[n - 1][...], inside, 1, 0)
    packed_ref[:, 3 * units + 3 : 3 * units + 4] = frequency_grad


def spectral_tables(seq_len):
    total = 2 * seq_len
    count1 = FIRST_FACTOR
    count2 = total // count1
    half = count1 // 2
    slot = np.arange(half)
    t1 = np.arange(half)
    t2 = np.arange(count2)
    k2 = np.arange(count2)
    angle = 2 * np.pi * slot[:, None] * t1[None, :] / count1
    first = np.zeros((half, 2, half))
    first[:, 0] = np.cos(angle)
    first[:, 1] = -np.sin(angle)
    first[0, 1] = (-1.0) ** t1
    last = np.zeros((half, half, 2))
    last[:, :, 0] = np.cos(angle.T) / seq_len
    last[:, :, 1] = -np.sin(angle.T) / seq_len
    last[:, 0, 0] = 1.0 / total
    last[:, 0, 1] = (-1.0) ** t1 / total
    mid = np.zeros((half, 2, count2, 2, count2))
    back = np.zeros((half, 2, count2, 2, count2))
    for s in range(1, half):
        turn = np.exp(-2j * np.pi * t2[None, :] * (s / total + k2[:, None] / count2))
        mid[s, 0, :, 0] = turn.real
        mid[s, 0, :, 1] = -turn.imag
        mid[s, 1, :, 0] = turn.imag
        mid[s, 1, :, 1] = turn.real
        undo = np.conj(turn).T
        back[s, 0, :, 0] = undo.real
        back[s, 0, :, 1] = -undo.imag
        back[s, 1, :, 0] = undo.imag
        back[s, 1, :, 1] = undo.real
    h2 = count2 // 2
    turn = np.exp(-2j * np.pi * t2[None, :] * k2[:h2, None] / count2)
    mid[0, 0, :h2, 0] = turn.real
    mid[0, 1, :h2, 0] = turn.imag
    mid[0, 1, 0, 0] = (-1.0) ** t2
    back[0, 0, :, 0, :h2] = 2 * turn.real.T
    back[0, 0, :, 1, :h2] = 2 * turn.imag.T
    back[0, 0, :, 0, 0] = 1.0
    back[0, 0, :, 1, 0] = (-1.0) ** t2
    turn = np.exp(-2j * np.pi * t2[None, :] * (half / total + k2[:h2, None] / count2))
    mid[0, 0, h2:, 1] = turn.real
    mid[0, 1, h2:, 1] = turn.imag
    back[0, 1, :, 0, h2:] = 2 * turn.real.T
    back[0, 1, :, 1, h2:] = 2 * turn.imag.T
    unit = np.eye(CHUNK)
    tables = (
        np.kron(first.reshape(count1, half), unit),
        mid.reshape(half, 2 * count2, 2 * count2),
        back.reshape(half, 2 * count2, 2 * count2),
        np.kron(last.reshape(half, count1), unit),
    )
    return tuple(jnp.asarray(v.astype(np.float32).astype(ml_dtypes.bfloat16)) for v in tables)


def times(left, right):
    return jnp.dot(left, right, preferred_element_type=F32)


def stage_first(first_ref, x_ref, y_ref):
    count1, count2, cols = y_ref.shape
    for j in range(count2 // CHUNK):
        rows = slice(CHUNK * j, CHUNK * (j + 1))
        block = x_ref[:, rows, :].reshape(count1 // 2 * CHUNK, cols)
        y_ref[:, rows, :] = times(first_ref[...], block).reshape(count1, CHUNK, cols).astype(BF16)


def stage_last(last_ref, z_ref, out_ref):
    count1, count2, cols = z_ref.shape
    for j in range(count2 // CHUNK):
        rows = slice(CHUNK * j, CHUNK * (j + 1))
        block = z_ref[:, rows, :].reshape(count1 * CHUNK, cols)
        values = times(last_ref[...], block).reshape(count1 // 2, CHUNK, cols)
        out_ref[:, rows, :] = values.astype(out_ref.dtype)


def spectral_product(s, left_re, left_im, right_re, right_im, sign):
    both_re = left_re * right_re
    both_im = left_im * right_im
    row = lax.broadcasted_iota(jnp.int32, both_re.shape, 0)
    real_row = (row == 0) & (s == 0)
    out_re = jnp.where(real_row, both_re, both_re - sign * both_im)
    out_im = jnp.where(real_row, both_im, left_im * right_re + sign * left_re * right_im)
    return jnp.concatenate([out_re, out_im], axis=0).astype(BF16)


def conv_kernel(
    first_ref, mid_ref, back_ref, last_ref, u_ref, t_ref, out_ref, su_ref, st_ref, y_ref, z_ref
):
    count1, count2, cols = y_ref.shape
    stage_first(first_ref, u_ref, y_ref)
    stage_first(first_ref, t_ref, z_ref)

    def slot_step(s, carry):
        pair = pl.ds(2 * s, 2)
        spec_u = times(mid_ref[s], y_ref[pair].reshape(2 * count2, cols))
        spec_t = times(mid_ref[s], z_ref[pair].reshape(2 * count2, cols))
        su_ref[pair] = spec_u.astype(BF16).reshape(2, count2, cols)
        st_ref[pair] = spec_t.astype(BF16).reshape(2, count2, cols)
        product = spectral_product(
            s, spec_u[:count2], spec_u[count2:], spec_t[:count2], spec_t[count2:], 1
        )
        z_ref[pair] = times(back_ref[s], product).astype(BF16).reshape(2, count2, cols)
        return carry

    lax.fori_loop(0, count1 // 2, slot_step, 0, unroll=2)
    stage_last(last_ref, z_ref, out_ref)


def conv_back_kernel(
    first_ref, mid_ref, back_ref, last_ref, g_ref, su_ref, st_ref, *refs
):
    du_ref, dt_ref, y_ref, z_ref, x_ref = refs
    count1, count2, cols = y_ref.shape
    stage_first(first_ref, g_ref, y_ref)

    def slot_step(s, carry):
        pair = pl.ds(2 * s, 2)
        spec_g = times(mid_ref[s], y_ref[pair].reshape(2 * count2, cols))
        spec_u = su_ref[pair].astype(F32)
        spec_t = st_ref[pair].astype(F32)
        product = spectral_product(s, spec_g[:count2], spec_g[count2:], spec_t[0], spec_t[1], -1)
        y_ref[pair] = times(back_ref[s], product).astype(BF16).reshape(2, count2, cols)
        product = spectral_product(s, spec_g[:count2], spec_g[count2:], spec_u[0], spec_u[1], -1)
        z_ref[pair] = times(back_ref[s], product).astype(BF16).reshape(2, count2, cols)
        return carry

    lax.fori_loop(0, count1 // 2, slot_step, 0, unroll=2)
    stage_last(last_ref, y_ref, x_ref)
    stage_last(last_ref, z_ref, dt_ref)
    groups, rows, _ = du_ref.shape
    rows -= CHUNK
    step = count1 // 2 // groups
    for place in range(groups):
        block = x_ref[place * step : (place + 1) * step]
        du_ref[place, :rows, :] = block.reshape(rows, cols)
        du_ref[place, rows:, :] = x_ref[(place + 1) % groups * step, :CHUNK, :]


def kernel_call(kernel, name, outs, in_specs, scratch, flops, size, limit, args):
    return pl.pallas_call(
        kernel,
        out_shape=tuple(jax.ShapeDtypeStruct(shape, dtype) for shape, dtype in outs),
        in_specs=in_specs,
        out_specs=(VMEM_SPEC,) * len(outs),
        scratch_shapes=scratch,
        compiler_params=pltpu.CompilerParams(vmem_limit_bytes=limit << 20),
        cost_estimate=pl.CostEstimate(flops=flops, bytes_accessed=size << 20, transcendentals=0),
        name=name,
    )(*args)


def long_conv(tables, signal, taps):
    seq_len, cols = taps.shape
    count1 = FIRST_FACTOR
    count2 = 2 * seq_len // count1
    timed = (count1 // 2, count2, cols)
    spectral = (count1, count2, cols)
    out, spec_u, spec_t = kernel_call(
        conv_kernel,
        "long_conv",
        [(timed, BF16), (spectral, BF16), (spectral, BF16)],
        [VMEM_SPEC] * 6,
        [pltpu.VMEM(spectral, BF16)] * 2,
        9_000_000_000,
        14,
        40,
        (*tables, signal.reshape(timed), taps.reshape(timed)),
    )
    return out.reshape(signal.shape), spec_u, spec_t


def long_conv_back(tables, grad, spec_u, spec_t):
    groups, rows, cols = grad.shape
    count1 = FIRST_FACTOR
    count2 = 2 * groups * rows // count1
    timed = (count1 // 2, count2, cols)
    spectral = (count1, count2, cols)
    grad_u, grad_t = kernel_call(
        conv_back_kernel,
        "long_conv_back",
        [((groups, rows + CHUNK, cols), BF16), (timed, F32)],
        [VMEM_SPEC] * 7,
        [pltpu.VMEM(spectral, BF16)] * 2 + [pltpu.VMEM(timed, BF16)],
        9_000_000_000,
        14,
        40,
        (*tables, grad.reshape(timed), spec_u, spec_t),
    )
    return grad_u, grad_t.reshape(groups * rows, cols)


def shift_mp(values_in, count):
    size = lax.axis_size("mp")
    return lax.ppermute(values_in, "mp", [(i, (i + count) % size) for i in range(size)])


def swap_dp(values_in, bit):
    size = lax.axis_size("dp")
    return lax.ppermute(values_in, "dp", [(i, i ^ (1 << bit)) for i in range(size)])


def bit_orders():
    bits = lax.axis_size("dp").bit_length() - 1
    high = list(range(1, bits))
    return [0] + high, [0] + high[::-1]


def after(values_in, *others):
    return lax.optimization_barrier((values_in,) + others)[0]


def gather_offsets(half):
    first, second = ((4, 2), (2, 4))[half]
    return [(0, first), (second, first | second), (1, first | 1), (second | 1, first | second | 1)]


def gather_start(block, half, *beside):
    bit = bit_orders()[half][2]
    return jnp.stack([after(block, *beside) if beside else block, swap_dp(block, bit)])


def gather_rest(pair, half, *beside):
    others = swap_dp(pair, bit_orders()[half][1])
    if beside:
        others = after(others, *beside)
    return [pair, others, swap_dp(pair, 0), swap_dp(others, 0)]


def split_blocks(pieces, axis, rows, *beside):
    out = []
    for half in range(2):
        part = lax.slice_in_dim(pieces, half * rows, (half + 1) * rows, axis=axis)
        out.extend(gather_rest(gather_start(part, half), half, *beside))
    return out


def add_across(part, bit, *beside):
    keep = after(part[0], *beside) if beside else part[0]
    return (keep.astype(F32) + swap_dp(part[1], bit).astype(F32)).astype(BF16)


def sum_groups(mine):
    total = mine[0].astype(F32)
    for k in range(1, lax.axis_size("mp")):
        total = total + shift_mp(mine[k], -k).astype(F32)
    return total


def own_group(grads):
    return lax.psum(sum_groups(grads), "dp")


def each_block(here, blocks):
    for half in range(2):
        for n, offsets in enumerate(gather_offsets(half)):
            for i, offset in enumerate(offsets):
                yield blocks[4 * half + n].at[i], half, here ^ offset


def place_feed_kernel(here_ref, *refs):
    *blocks, expand_ref, reduce_ref = refs
    share = blocks[0].shape[1]
    for block, half, index in each_block(here_ref[0], blocks):
        place = pl.ds(pl.multiple_of(index * share, share), share)
        if half == 0:
            expand_ref[:, place] = block[...].astype(F32).T
        else:
            reduce_ref[place, :] = block[...].astype(F32)


def place_input_kernel(here_ref, *refs):
    *blocks, input_ref, output_ref, full_ref = refs
    rows = blocks[0].shape[2]
    parts = full_ref.shape[0]
    for block, half, index in each_block(here_ref[0], blocks):
        place = pl.ds(pl.multiple_of((index * 2 + half) * rows, rows), rows)
        full_ref[:, place, :] = block[:parts].astype(F32)
        output_ref[place, :] = block[parts].astype(F32)
    for p in range(parts):
        input_ref[p] = full_ref[p].T


def sum_dp(values_in):
    for bit in range(lax.axis_size("dp").bit_length() - 1):
        values_in = values_in + swap_dp(values_in, bit)
    return values_in


def contract_rows(left, right):
    return lax.dot_general(left, right, (((0,), (0,)), ((), ())), preferred_element_type=F32)


def contract_cols(left, right):
    return lax.dot_general(left, right, (((1,), (1,)), ((), ())), preferred_element_type=F32)


def gelu_parts(value):
    factor = math.sqrt(2.0 / math.pi)
    square = value * value
    tanh_part = jnp.tanh(factor * value * (1.0 + 0.044715 * square))
    half = 0.5 * (1.0 + tanh_part)
    slope = half + 0.5 * value * (1.0 - tanh_part * tanh_part) * (
        factor * (1.0 + 3.0 * 0.044715 * square)
    )
    return value * half, slope


ROW_STEP = 32
SMALL_ROWS = 32


def fold_rows(wide_ref, narrow_ref):
    channels = narrow_ref.shape[1]
    for i in range(wide_ref.shape[1] // channels):
        narrow_ref[8 * i : 8 * i + 8, :] = wide_ref[:, i * channels : (i + 1) * channels]


def unfold_rows(narrow):
    rows, channels = narrow.shape
    return narrow.reshape(rows // 8, 8, channels).transpose(1, 0, 2).reshape(8, -1)


def store_grad(refs, k, part, here, values):
    rows = values.shape[0] // 8
    for i in range(4):
        bit1, bit2 = (i & 1) ^ (here >> 1 & 1), (i >> 1) ^ (here >> 2)
        first, second = (bit2, bit1) if k < 2 else (bit1, bit2)
        pair = [values[(2 * i + n) * rows : (2 * i + n + 1) * rows].astype(BF16) for n in range(2)]
        even = here & 1 == 0
        refs[0][k // 2, first, second, part] = jnp.where(even, pair[0], pair[1])
        refs[1][k // 2, first, second, part] = jnp.where(even, pair[1], pair[0])


def start_input_weights(here_ref, local, blocks, weight_ref, sem):
    others = pl.ds(1, weight_ref.shape[0] - 1)
    pltpu.make_async_copy(local, weight_ref.at[0], sem).start()
    if len(blocks) == 1:
        pltpu.make_async_copy(blocks[0], weight_ref.at[others], sem).start()
        return
    rows = blocks[0].shape[3]
    for block, half, index in each_block(here_ref[0], blocks):
        start = pl.multiple_of((index * 2 + half) * rows, rows)
        pltpu.make_async_copy(block, weight_ref.at[others, :, pl.ds(start, rows)], sem).start()


def group_at(here_ref, k, groups):
    return lax.rem(here_ref[1] + (groups - k), groups)


def wait_whole(ref, sem):
    pltpu.make_async_copy(ref, ref, sem).wait()


def enter_kernel(count, here_ref, input_ref, halo_ref, vectors_ref, small_ref, local_ref, *refs):
    blocks = refs[:count]
    conv_input_ref, second_ref, gates_ref, projected_ref, normed_ref = refs[count : count + 5]
    weight_ref, rows_ref, sem = refs[count + 5 :]
    rows = input_ref.shape[0]
    groups, _, channels = conv_input_ref.shape
    start_input_weights(here_ref, local_ref, blocks, weight_ref, sem)

    def normed(values):
        return (norm_parts(values)[0] * vectors_ref[0:1] + vectors_ref[1:2]).astype(BF16)

    rows_ref[:CHUNK, :] = normed(halo_ref[...])

    def norm_step(i, carry):
        start = pl.multiple_of(i * ROW_STEP, ROW_STEP)
        values = normed(input_ref[pl.ds(start, ROW_STEP), :])
        normed_ref[pl.ds(start, ROW_STEP), :] = values
        rows_ref[pl.ds(start + CHUNK, ROW_STEP), :] = values
        return carry

    lax.fori_loop(0, rows // ROW_STEP, norm_step, 0)
    wait_whole(weight_ref, sem)
    row = lax.broadcasted_iota(jnp.int32, (rows + CHUNK, channels), 0)
    begins = (row < CHUNK) & (here_ref[1] == 0)
    for k in range(groups):
        mixed = []
        for p in range(3):
            small = small_ref[k, 8 * p : 8 * p + 8, :]
            values = contract_cols(rows_ref[...], weight_ref[k, p]) + small[0:1]
            values = jnp.where(begins, 0.0, values)
            projected_ref[k, p] = values.astype(BF16)
            mixed.append(
                small[1:2] * values[CHUNK:]
                + small[2:3] * values[CHUNK - 1 : -1]
                + small[3:4] * values[CHUNK - 2 : -2]
                + small[4:5]
            )
        conv_input_ref[group_at(here_ref, k, groups)] = (mixed[1] * mixed[0]).astype(BF16)
        gates_ref[k, 0] = mixed[0].astype(BF16)
        gates_ref[k, 1] = mixed[1].astype(BF16)
        second_ref[k] = mixed[2].astype(BF16)


def enter(here, block_input, halo, vectors, small, local, blocks):
    rows, width = block_input.shape
    parts, channels, _ = local.shape
    groups = small.shape[0]
    outs = [
        ((groups, rows, channels), BF16),
        ((groups, rows, channels), BF16),
        ((groups, 2, rows, channels), BF16),
        ((groups, parts, rows + CHUNK, channels), BF16),
        ((rows, width), BF16),
    ]
    return kernel_call(
        functools.partial(enter_kernel, len(blocks)),
        "enter",
        outs,
        [SMEM_SPEC] + [VMEM_SPEC] * 4 + [ANY_SPEC] * (1 + len(blocks)),
        [
            pltpu.VMEM((groups, parts, channels, width), BF16),
            pltpu.VMEM((rows + CHUNK, width), BF16),
            pltpu.SemaphoreType.DMA,
        ],
        2 * rows * width * parts * groups * channels,
        16,
        40,
        (here, block_input, halo, vectors, small, local, *blocks),
    )


def middle_kernel(count, sorted_units, here_ref, *refs):
    long_ref, conv_ref, second_ref, input_ref, cot_ref, vectors_ref, small_ref, bias_ref = refs[:8]
    expand_local, reduce_local, output_local = refs[8:11]
    blocks = refs[11 : 11 + count]
    (
        result_ref,
        hidden_grad_ref,
        conv_grad_ref,
        second_grad_ref,
        gated_ref,
        act_ref,
        pre_grad_ref,
        normed_ref,
        mix_ref,
        out_low_ref,
        bias_grad_ref,
        all_sums_ref,
        skip_grad_ref,
    ) = refs[11 + count : 24 + count]
    expand_ref, reduce_ref, output_ref, normal_ref, scale_ref, sums_ref, sems = refs[24 + count :]
    rows, width = input_ref.shape
    groups, hidden, _ = expand_ref.shape
    channels = output_ref.shape[1]
    others = pl.ds(1, groups - 1)
    here = here_ref[0]

    pltpu.make_async_copy(output_local, output_ref.at[0], sems.at[0]).start()
    pltpu.make_async_copy(expand_local, expand_ref.at[0], sems.at[1]).start()
    pltpu.make_async_copy(reduce_local, reduce_ref.at[0], sems.at[2]).start()
    if sorted_units:
        share = hidden // 8
        half_share = channels // 16
        for block, half, index in each_block(here, blocks):
            ref = (expand_ref, reduce_ref)[half]
            start = pl.multiple_of((index * 2 + half) * half_share, half_share)
            pltpu.make_async_copy(
                block.at[:, pl.ds(share, half_share)],
                output_ref.at[others, pl.ds(start, half_share)],
                sems.at[0],
            ).start()
            start = pl.multiple_of(index * share, share)
            pltpu.make_async_copy(
                block.at[:, pl.ds(0, share)],
                ref.at[others, pl.ds(start, share)],
                sems.at[1 + half],
            ).start()
    else:
        for n, (block, ref) in enumerate(zip(blocks, (output_ref, expand_ref, reduce_ref))):
            pltpu.make_async_copy(block, ref.at[others], sems.at[n]).start()

    position = here_ref[1] * rows + lax.broadcasted_iota(jnp.int32, (rows, channels), 0)
    mask = jnp.where(position < here_ref[2], 1.0, 0.0)

    def conv_out(k):
        skip = small_ref[k, 24:25, :]
        group = group_at(here_ref, k, groups)
        return long_ref[group].astype(F32) + skip * conv_ref[group].astype(F32)

    for k in range(groups):
        gated = mask * second_ref[k].astype(F32) * conv_out(k)
        gated_ref[:, k * channels : (k + 1) * channels] = gated.astype(BF16)
    wait_whole(output_ref, sems.at[0])
    mixed = times(gated_ref[...], output_ref[...].reshape(groups * channels, width))
    result_ref[...] = input_ref[...] + mixed + vectors_ref[0:1]
    sums_ref[...] = jnp.zeros_like(sums_ref)

    def norm_step(i, carry):
        part = pl.ds(pl.multiple_of(i * ROW_STEP, ROW_STEP), ROW_STEP)
        values = result_ref[part, :]
        normal, scale = norm_parts(values)
        normal_ref[part, :] = normal
        scale_ref[part, :] = scale
        normed_ref[part, :] = (normal * vectors_ref[1:2] + vectors_ref[2:3]).astype(BF16)
        cot = cot_ref[part, :]
        out_low_ref[part, :] = cot.astype(BF16)
        result_ref[part, :] = values + vectors_ref[3:4]
        hidden_grad_ref[part, :] = jnp.zeros_like(cot)
        sums_ref[0:1, :] += jnp.sum(cot, axis=0, keepdims=True)
        return carry

    lax.fori_loop(0, rows // ROW_STEP, norm_step, 0)
    wait_whole(expand_ref, sems.at[1])
    wait_whole(reduce_ref, sems.at[2])
    per_step = hidden // 2

    def store_units(ref, k, half, values):
        if not sorted_units:
            start = pl.multiple_of((lax.rem(k, 2) * 2 + half) * per_step, per_step)
            ref[k // 2, :, pl.ds(start, per_step)] = values
            return
        share = hidden // 8
        for i in range(4):
            bit0 = (here & 1) ^ (i & 1)
            bit1 = ((here >> 1) & 1) ^ (i >> 1)
            bit2 = ((here >> 2) & 1) ^ half
            outer = jnp.where(k < 2, bit2 * 2 + bit1, bit1 * 2 + bit2)
            start = ((k // 2 * 4 + outer) * 2 + lax.rem(k, 2)) * share
            columns = pl.ds(pl.multiple_of(start, share), share)
            ref[bit0, :, columns] = values[:, i * share : (i + 1) * share]

    def hidden_step(j, carry):
        k, half = j // 2, lax.rem(j, 2)
        units = pl.ds(pl.multiple_of(half * per_step, per_step), per_step)
        expand = expand_ref[k, units, :]
        reduce = reduce_ref[k, units, :]
        value, slope = gelu_parts(contract_cols(normed_ref[...], expand) + bias_ref[j])
        value = value.astype(BF16)
        store_units(act_ref, k, half, value)
        result_ref[...] += times(value, reduce)
        grad = (contract_cols(out_low_ref[...], reduce) * slope).astype(BF16)
        store_units(pre_grad_ref, k, half, grad)
        bias_grad_ref[j] = jnp.sum(grad.astype(F32), axis=0, keepdims=True)
        hidden_grad_ref[...] += times(grad, expand)
        return carry

    lax.fori_loop(0, 2 * groups, hidden_step, 0)

    def back_step(i, carry):
        part = pl.ds(pl.multiple_of(i * ROW_STEP, ROW_STEP), ROW_STEP)
        res_part, gain_sum, shift_sum = norm_back(
            normal_ref[part, :], scale_ref[part, :], vectors_ref[1:2], hidden_grad_ref[part, :]
        )
        hidden_grad = cot_ref[part, :] + res_part
        hidden_grad_ref[part, :] = hidden_grad
        mix_ref[part, :] = hidden_grad.astype(BF16)
        sums_ref[1:2, :] += gain_sum[None]
        sums_ref[2:3, :] += shift_sum[None]
        sums_ref[3:4, :] += jnp.sum(hidden_grad, axis=0, keepdims=True)
        return carry

    lax.fori_loop(0, rows // ROW_STEP, back_step, 0)
    fold_rows(sums_ref, all_sums_ref)
    for k in range(groups):
        group = group_at(here_ref, k, groups)
        masked_grad = contract_cols(mix_ref[...], output_ref[k]) * mask
        second_grad_ref[k] = (masked_grad * conv_out(k)).astype(BF16)
        conv_grad = (masked_grad * second_ref[k].astype(F32)).astype(BF16)
        conv_grad_ref[group] = conv_grad
        products = conv_grad.astype(F32) * conv_ref[group].astype(F32)
        skip_grad_ref[k] = jnp.sum(products, axis=0, keepdims=True)


def grad_shapes(groups, channels, width, split, parts):
    if split:
        return [((2, 2, 2, groups // 2 * parts, channels // 8, width), BF16)] * 2
    return [((groups * parts, channels, width), BF16), ((8, 128), BF16)]


def middle(
    here, long_out, conv_input, second, block_input, cotangent, vectors, small, bias, local, blocks
):
    rows, width = block_input.shape
    groups, _, channels = small.shape
    hidden = local[0].shape[0]
    grouped = ((groups, rows, channels), BF16)
    square = ((rows, width), BF16)
    wide = ((2, rows, groups * hidden // 2), BF16)
    outs = (
        [((rows, width), F32)] * 2
        + [grouped, grouped, square, wide, wide, square, square, square]
        + [((2 * groups, 1, hidden // 2), F32)]
        + [((8 * width // channels, channels), F32), ((groups, 1, channels), F32)]
    )
    return kernel_call(
        functools.partial(middle_kernel, len(blocks), len(blocks) == 8),
        "middle",
        outs,
        [SMEM_SPEC] + [VMEM_SPEC] * 8 + [ANY_SPEC] * (3 + len(blocks)),
        [
            pltpu.VMEM((groups, hidden, width), BF16),
            pltpu.VMEM((groups, hidden, width), BF16),
            pltpu.VMEM((groups, channels, width), BF16),
            pltpu.VMEM((rows, width), F32),
            pltpu.VMEM((rows, 1), F32),
            pltpu.VMEM((8, width), F32),
            pltpu.SemaphoreType.DMA((3,)),
        ],
        20_000_000_000,
        48,
        62,
        (
            here,
            long_out,
            conv_input,
            second,
            block_input,
            cotangent,
            vectors,
            small,
            bias,
            *local,
            *blocks,
        ),
    )


def leave_kernel(count, here_ref, *refs):
    (
        du_ref,
        conv_grad_ref,
        halo_gates_ref,
        halo_grads_ref,
        small_ref,
        vectors_ref,
        normed_ref,
        gated_ref,
        mix_ref,
        skip_grad_ref,
        bias_grad_ref,
        second_grad_any,
        gates_any,
        projected_any,
        input_any,
        hidden_grad_any,
        local_ref,
    ) = refs[:17]
    blocks = refs[17 : 17 + count]
    input_grad_ref, small_grad_ref, all_sums_ref, *weight_outs = refs[17 + count : 22 + count]
    low_ref, weight_ref, sums_ref, sem, *rest = refs[22 + count :]
    second_grad_ref, gates_ref, projected_ref, input_ref, hidden_grad_ref = rest[:5]
    sems, out_sems = rest[5:7]
    weight_grads = rest[7:]
    rows, width = input_ref.shape
    groups = small_ref.shape[0]
    channels = small_ref.shape[2]
    loads = [
        [
            pltpu.make_async_copy(source.at[k], target.at[k], sems.at[n, k])
            for n, (source, target) in enumerate(
                (
                    (second_grad_any, second_grad_ref),
                    (gates_any, gates_ref),
                    (projected_any, projected_ref),
                )
            )
        ]
        for k in range(groups)
    ]
    late_loads = [
        pltpu.make_async_copy(input_any, input_ref, sems.at[3, 0]),
        pltpu.make_async_copy(hidden_grad_any, hidden_grad_ref, sems.at[3, 1]),
    ]
    for copy in loads[0] + loads[1]:
        copy.start()
    start_input_weights(here_ref, local_ref, blocks, weight_ref, sem)
    for copy in loads[2] + loads[3] + late_loads:
        copy.start()
    row = lax.broadcasted_iota(jnp.int32, (rows + CHUNK, channels), 0)
    ends = (row >= rows) & (here_ref[1] == groups - 1)
    small_grad_ref[...] = jnp.zeros_like(small_grad_ref)

    def keep_grad(k, p, weight_grad):
        if count > 1:
            store_grad(weight_grads, k, k % 2 * 4 + p, here_ref[0], weight_grad)
        else:
            weight_grads[0][4 * k + p] = weight_grad.astype(BF16)

    for k in range(groups):
        nk = (k + 1) % groups
        for copy in loads[k]:
            copy.wait()

        def extended(values, halo):
            return jnp.concatenate([values, halo], axis=0).astype(F32)

        group = group_at(here_ref, k, groups)
        conv_grad = extended(conv_grad_ref[group], halo_grads_ref[0, group])
        skip = small_ref[k, 24:25, :]
        input_side = du_ref[group].astype(F32) + skip * conv_grad
        grads = (
            input_side * extended(gates_ref[k, 1], halo_gates_ref[nk, 1]),
            input_side * extended(gates_ref[k, 0], halo_gates_ref[nk, 0]),
            extended(second_grad_ref[k], halo_grads_ref[1, nk]),
        )
        for p, grad in enumerate(grads):
            grad = jnp.where(ends, 0.0, grad)
            small = small_ref[k, 8 * p : 8 * p + 8, :]
            low = (
                small[1:2] * grad[:rows]
                + small[2:3] * grad[1 : rows + 1]
                + small[3:4] * grad[2 : rows + 2]
            ).astype(BF16)
            low_ref[:, (3 * k + p) * channels : (3 * k + p + 1) * channels] = low
            keep_grad(k, p, contract_rows(low, normed_ref[...]))
            projected = projected_ref[k, p].astype(F32)
            own = grad[:rows]
            small_grad_ref[k, 8 * p : 8 * p + 1, :] = jnp.sum(
                low.astype(F32), axis=0, keepdims=True
            )
            for tap in range(3):
                delayed = projected[CHUNK - tap : rows + CHUNK - tap]
                small_grad_ref[k, 8 * p + 1 + tap : 8 * p + 2 + tap, :] = jnp.sum(
                    own * delayed, axis=0, keepdims=True
                )
            small_grad_ref[k, 8 * p + 4 : 8 * p + 5, :] = jnp.sum(own, axis=0, keepdims=True)
        gated = gated_ref[:, k * channels : (k + 1) * channels]
        keep_grad(k, 3, contract_rows(gated, mix_ref[...]))
        small_grad_ref[k, 24:25, :] = skip_grad_ref[k]
        per_half = bias_grad_ref.shape[2] // channels
        for n in range(2 * per_half):
            bias_row = bias_grad_ref[2 * k + n // per_half]
            first = n % per_half * channels
            small_grad_ref[k, 25 + n : 26 + n, :] = bias_row[:, first : first + channels]
        if count > 1 and k % 2 == 1:
            for n in range(2):
                pltpu.make_async_copy(
                    weight_grads[n].at[k // 2], weight_outs[n].at[k // 2], out_sems.at[n, k // 2]
                ).start()
    if count == 1:
        for n in range(2):
            pltpu.make_async_copy(weight_grads[n], weight_outs[n], out_sems.at[n, 0]).start()
    wait_whole(weight_ref, sem)
    input_grad_ref[...] = times(
        low_ref[...], weight_ref[...].reshape(groups * 3 * channels, width)
    )
    sums_ref[...] = jnp.zeros_like(sums_ref)
    for copy in late_loads:
        copy.wait()

    def back_step(i, carry):
        part = pl.ds(pl.multiple_of(i * ROW_STEP, ROW_STEP), ROW_STEP)
        normal, scale = norm_parts(input_ref[part, :])
        input_part, gain_sum, shift_sum = norm_back(
            normal, scale, vectors_ref[0:1], input_grad_ref[part, :]
        )
        input_grad_ref[part, :] = hidden_grad_ref[part, :] + input_part
        sums_ref[0:1, :] += gain_sum[None]
        sums_ref[1:2, :] += shift_sum[None]
        return carry

    lax.fori_loop(0, rows // ROW_STEP, back_step, 0)
    fold_rows(sums_ref, all_sums_ref)
    for n in range(2):
        if count > 1:
            for half in range(2):
                pltpu.make_async_copy(
                    weight_grads[n].at[half], weight_outs[n].at[half], out_sems.at[n, half]
                ).wait()
        else:
            pltpu.make_async_copy(weight_grads[n], weight_outs[n], out_sems.at[n, 0]).wait()


def leave(
    here,
    conv_input_grad,
    conv_grad,
    second_grad,
    gates,
    projected,
    halo_gates,
    halo_grads,
    small,
    block_input,
    hidden_grad,
    vectors,
    normed,
    gated,
    mix_low,
    skip_grad,
    bias_grad,
    local,
    blocks,
):
    rows, width = block_input.shape
    groups, _, channels = small.shape
    grads = grad_shapes(groups, channels, width, len(blocks) > 1, 4)
    outs = [
        ((rows, width), F32),
        ((groups, SMALL_ROWS, channels), F32),
        ((8 * width // channels, channels), F32),
        *grads,
    ]
    return pl.pallas_call(
        functools.partial(leave_kernel, len(blocks)),
        out_shape=tuple(jax.ShapeDtypeStruct(shape, dtype) for shape, dtype in outs),
        in_specs=[SMEM_SPEC] + [VMEM_SPEC] * 11 + [ANY_SPEC] * (6 + len(blocks)),
        out_specs=(VMEM_SPEC,) * 3 + (ANY_SPEC,) * 2,
        scratch_shapes=[
            pltpu.VMEM((rows, 3 * groups * channels), BF16),
            pltpu.VMEM((groups, 3, channels, width), BF16),
            pltpu.VMEM((8, width), F32),
            pltpu.SemaphoreType.DMA,
            *[
                pltpu.VMEM(a.shape, a.dtype)
                for a in (second_grad, gates, projected, block_input, hidden_grad)
            ],
            pltpu.SemaphoreType.DMA((4, groups)),
            pltpu.SemaphoreType.DMA((2, 2)),
            *[pltpu.VMEM(shape, dtype) for shape, dtype in grads],
        ],
        compiler_params=pltpu.CompilerParams(vmem_limit_bytes=60 << 20),
        cost_estimate=pl.CostEstimate(
            flops=16_000_000_000, bytes_accessed=34 << 20, transcendentals=0
        ),
        name="leave",
    )(
        here,
        conv_input_grad,
        conv_grad,
        halo_gates,
        halo_grads,
        small,
        vectors,
        normed,
        gated,
        mix_low,
        skip_grad,
        bias_grad,
        second_grad,
        gates,
        projected,
        block_input,
        hidden_grad,
        local,
        *blocks,
    )


def per_device(
    block_input,
    lengths,
    mixer_gain,
    mixer_shift,
    input_weight,
    input_bias,
    conv_weight,
    conv_bias,
    enter_weight,
    enter_bias,
    middle_weight,
    middle_bias,
    inner_weight,
    inner_bias,
    frequency,
    filter_weight,
    skip_scale,
    output_weight,
    output_bias,
    feed_gain,
    feed_shift,
    expand_weight,
    expand_bias,
    reduce_weight,
    reduce_bias,
    cotangent,
):
    own_rows, width = block_input.shape
    channels = input_weight.shape[2]
    hidden = expand_weight.shape[1]
    mp_size = lax.axis_size("mp")
    dp_size = lax.axis_size("dp")
    mp_here = lax.axis_index("mp")
    dp_here = lax.axis_index("dp")
    seq_len = own_rows * mp_size
    split = dp_size == 8
    share = hidden // dp_size
    out_share = channels // dp_size
    here = jnp.stack([dp_here, mp_here, lengths[0]]).astype(jnp.int32)

    small_own = jnp.concatenate(
        [
            jnp.concatenate(
                [input_bias[:, None], conv_weight.transpose(1, 0, 2), conv_bias[:, None]]
                + [jnp.zeros((3, 3, channels), F32)],
                axis=1,
            ).reshape(24, channels),
            skip_scale[None],
            expand_bias.reshape(-1, channels),
        ]
    )
    small_own = jnp.pad(small_own, ((0, SMALL_ROWS - small_own.shape[0]), (0, 0)))

    def other_groups(values):
        return jnp.stack([shift_mp(values, k) for k in range(1, mp_size)])

    def turned_groups(stacked, start, sign):
        return jnp.concatenate(
            [
                lax.dynamic_slice_in_dim(stacked, (mp_here + sign * k) % mp_size, 1, 0)
                for k in range(start, mp_size)
            ]
        )

    features = position_features(seq_len, enter_weight.shape[0])
    columns = jnp.stack([enter_bias, middle_bias, inner_bias, frequency], axis=1)
    net_units = frequency.shape[0]
    net_shape = ((3, net_units, seq_len), F32)
    taps_low, *net_values = kernel_call(
        functools.partial(filter_kernel, width),
        "filter_taps",
        [((seq_len, channels), BF16)] + [net_shape] * 3,
        [SMEM_SPEC] + [VMEM_SPEC] * 6,
        [],
        4_000_000_000,
        6,
        32,
        (
            here,
            features,
            jnp.pad(enter_weight, ((0, FEATURE_ROWS - enter_weight.shape[0]), (0, 0))),
            middle_weight,
            inner_weight,
            columns,
            filter_weight,
        ),
    )
    small = jnp.stack([small_own] + [shift_mp(small_own, k) for k in range(1, mp_size)])
    halo = shift_mp(block_input[-CHUNK:], 1)

    input_turned = input_weight.transpose(1, 2, 0)
    expand_turned = expand_weight.T
    if split:
        input_part = lax.dynamic_slice_in_dim(input_turned, dp_here * out_share, out_share, 1)
        input_pieces = after(other_groups(input_part), taps_low, small, halo)
        input_blocks = split_blocks(input_pieces, 2, out_share // 2)
    else:
        input_blocks = [other_groups(input_turned)]
    tables = spectral_tables(seq_len)

    if split:
        expand_part = lax.dynamic_slice_in_dim(expand_turned, dp_here * share, share, 0)
        reduce_part = lax.dynamic_slice_in_dim(reduce_weight, dp_here * share, share, 0)
        output_part = lax.dynamic_slice_in_dim(output_weight, dp_here * out_share, out_share, 0)
        half = out_share // 2
        feed_part = jnp.concatenate(
            [expand_part, output_part[:half], reduce_part, output_part[half:]]
        )
        feed_groups = lax.all_gather(feed_part, "mp")
    else:
        feed_blocks = [other_groups(w) for w in (output_weight, expand_turned, reduce_weight)]

    mixer_vectors = jnp.stack([mixer_gain, mixer_shift])
    conv_input, second_gate, gates, projected, mixer_normed = enter(
        here,
        block_input,
        halo,
        mixer_vectors,
        small,
        input_turned,
        input_blocks,
    )
    halo_gates = shift_mp(gates[:, :, :CHUNK], -1)

    def exchange(values):
        return lax.all_to_all(values, "mp", 0, 0)

    arrived_input = exchange(conv_input)
    if split:
        feed_pieces = turned_groups(after(feed_groups, conv_input), 1, -1)
        halves = (feed_pieces[:, : share + half], feed_pieces[:, share + half :])
        pairs = [gather_start(part, n, arrived_input) for n, part in enumerate(halves)]
        arrived_input = after(arrived_input, *pairs)
    long_out, spec_u, spec_t = long_conv(tables, arrived_input, taps_low)
    long_out = exchange(long_out)
    if split:
        feed_blocks = [
            block for n, pair in enumerate(pairs) for block in gather_rest(pair, n, long_out)
        ]
    vectors = jnp.stack([output_bias, feed_gain, feed_shift, reduce_bias])
    bias = small[:, 25 : 25 + hidden // channels].reshape(2 * mp_size, 1, hidden // 2)
    (
        result,
        hidden_grad,
        conv_grad,
        second_grad,
        gated,
        activated,
        pre_grad,
        feed_normed,
        mix_low,
        out_low,
        bias_grad,
        feed_sums,
        skip_grad,
    ) = middle(
        here,
        long_out,
        conv_input,
        second_gate,
        block_input,
        cotangent,
        vectors,
        small,
        bias,
        (expand_turned, reduce_weight, output_weight),
        feed_blocks,
    )
    halo_grads = shift_mp(jnp.stack([conv_grad[:, :CHUNK], second_grad[:, :CHUNK]]), -1)
    arrived_grad = exchange(conv_grad)

    if split:
        pairs = ((activated, out_low), (pre_grad, feed_normed))
        arrived = [
            swap_dp(contract_rows(u[1], right).astype(BF16), 0) for u, right in pairs
        ]
    else:
        def feed_grads(left, right):
            grads = [contract_rows(part, right).astype(BF16) for part in left]
            return own_group(jnp.concatenate(grads).reshape(mp_size, hidden, width))

        reduce_weight_grad = feed_grads(activated, out_low)
        expand_weight_grad = feed_grads(pre_grad, feed_normed).T

    arrived_grad = after(arrived_grad, halo_gates, halo_grads)
    conv_input_grad, taps_grad = long_conv_back(tables, arrived_grad, spec_u, spec_t)
    if split:
        pairs = [(after(u, taps_grad), right) for u, right in pairs]
        kept = [
            (contract_rows(u[0], right) + other.astype(F32)).astype(BF16)
            for (u, right), other in zip(pairs, arrived)
        ]
        held = [k.reshape(2, 2, 2, mp_size // 2, share, width) for k in kept]
        first_stages = [
            [jnp.stack([h[n, i] for h in held], axis=1) for i in range(2)] for n in range(2)
        ]
    conv_input_grad = exchange(conv_input_grad)
    if split:
        conv_input_grad = after(conv_input_grad, first_stages[0][1], first_stages[1][1])
    input_grad, small_grad, mixer_sums, grads_kept, grads_away = leave(
        here,
        conv_input_grad,
        conv_grad,
        second_grad,
        gates,
        projected,
        halo_gates,
        halo_grads,
        small,
        block_input,
        hidden_grad,
        mixer_vectors,
        mixer_normed,
        gated,
        mix_low,
        skip_grad,
        bias_grad,
        input_turned,
        input_blocks,
    )
    if split:
        stages = [add_across(part, bit, small_grad) for part, bit in zip(first_stages, (2, 1))]
        held = (grads_kept.astype(F32) + swap_dp(grads_away, 0).astype(F32)).astype(BF16)
        stages = [add_across(part, bit) for part, bit in zip(stages, (1, 2))]
        feed_grads = jnp.concatenate(stages, axis=1).transpose(1, 0, 2, 3)
        feed_grads = turned_groups(feed_grads, 0, -1).reshape(-1, width)
        feed_total = lax.psum_scatter(feed_grads, "mp", scatter_dimension=0, tiled=True)
        taps_grad = after(taps_grad, held)
    else:
        taps_grad = after(taps_grad, grads_kept)
    net_grads, filter_weight_grad = kernel_call(
        functools.partial(filter_back_kernel, width),
        "filter_back",
        [((net_units, 4 * net_units), F32), ((net_units, channels), F32)],
        [SMEM_SPEC] + [VMEM_SPEC] * 9,
        [pltpu.VMEM((net_units, seq_len), F32)],
        8_000_000_000,
        6,
        32,
        (
            here,
            features,
            middle_weight,
            inner_weight,
            columns,
            filter_weight,
            *net_values,
            taps_grad,
        ),
    )
    packed = [net_grads, feed_sums, mixer_sums, filter_weight_grad]
    packed.append(small_grad.reshape(-1, channels))
    ends = [sum(p.shape[0] for p in packed[:n]) for n in range(len(packed) + 1)]
    packed = jnp.concatenate(packed)
    def small_sums(packed):
        summed = sum_dp(packed)
        by_group = summed[ends[4] :].reshape(mp_size, SMALL_ROWS, channels)
        along_mp = [jnp.concatenate([summed[: ends[3]], by_group[k]]) for k in range(mp_size)]
        along_mp = sum_groups(along_mp)
        return summed, along_mp

    if split:
        held = [add_across(held[0], 2, net_grads), add_across(held[1], 1, net_grads)]
        packed = after(packed, *held)
        held = [add_across(held[0], 1), add_across(held[1], 2)]
        feed_total = after(feed_total, *held)
        mine = jnp.concatenate(held).reshape(mp_size, 4, out_share, width)
        input_total = sum_groups(mine)
        reduce_total, expand_total = feed_total[:share], feed_total[share:]
        summed, along_mp = small_sums(packed)
        input_total = after(input_total, summed)
        blocks = []
        for n, total in enumerate((expand_total, reduce_total)):
            blocks.extend(gather_rest(gather_start(total.astype(BF16), n), n))
        expand_weight_grad, reduce_weight_grad = kernel_call(
            place_feed_kernel,
            "place_feed",
            [((width, hidden), F32), ((hidden, width), F32)],
            [SMEM_SPEC] + [VMEM_SPEC] * len(blocks),
            [],
            0,
            14,
            32,
            (here, *blocks),
        )
        blocks = split_blocks(input_total.astype(BF16), 1, out_share // 2, expand_weight_grad, along_mp)
        input_weight_grad, output_weight_grad = kernel_call(
            place_input_kernel,
            "place_input",
            [((3, width, channels), F32), ((channels, width), F32)],
            [SMEM_SPEC] + [VMEM_SPEC] * len(blocks),
            [pltpu.VMEM((3, channels, width), F32)],
            0,
            8,
            24,
            (here, *blocks),
        )
        input_weight_grad = input_weight_grad.transpose(1, 0, 2)
    else:
        input_total = own_group(grads_kept.reshape(mp_size, 4, channels, width))
        input_weight_grad = input_total[:3].transpose(2, 0, 1)
        output_weight_grad = input_total[3]
        summed, along_mp = small_sums(packed)

    everywhere, groups_sum = along_mp[: ends[3]], along_mp[ends[3] :]
    net = everywhere[: ends[1]]
    net_bias = net[:, 3 * net_units :].T
    feed_sums = unfold_rows(everywhere[ends[1] : ends[2]])
    mixer_sums = unfold_rows(everywhere[ends[2] : ends[3]])
    parts = groups_sum[:24].reshape(3, 8, channels)
    return (
        result,
        input_grad,
        mixer_sums[0],
        mixer_sums[1],
        input_weight_grad,
        parts[:, 0],
        parts[:, 1:4].transpose(1, 0, 2),
        parts[:, 4],
        net[: enter_weight.shape[0], :net_units],
        net_bias[0],
        net[:, net_units : 2 * net_units],
        net_bias[1],
        net[:, 2 * net_units : 3 * net_units],
        net_bias[2],
        net_bias[3],
        summed[ends[3] : ends[4]],
        groups_sum[24],
        output_weight_grad,
        feed_sums[3],
        feed_sums[1],
        feed_sums[2],
        expand_weight_grad,
        groups_sum[25 : 25 + hidden // channels].reshape(hidden),
        reduce_weight_grad,
        feed_sums[0],
    )


ROWS = P(("dp", "mp"), None)
FIRST = P("mp", None)
SECOND = P(None, "mp")
THIRD = P(None, None, "mp")


def solution(mesh):
    return jax.shard_map(
        per_device,
        mesh=mesh,
        in_specs=(
            ROWS, P("dp"), P(), P(), THIRD, SECOND, THIRD, SECOND,
            P(), P(), P(), P(), P(), P(), P(), SECOND,
            P("mp"), FIRST, P(), P(), P(), SECOND, P("mp"), FIRST, P(), ROWS,
        ),
        out_specs=(
            ROWS, ROWS, P(), P(), THIRD, SECOND, THIRD, SECOND,
            P(), P(), P(), P(), P(), P(), P(), SECOND,
            P("mp"), FIRST, P(), P(), P(), SECOND, P("mp"), FIRST, P(),
        ),
        check_vma=False,
    )
```

time: 721 us -> 529 us (0.73)
  starting transfers between devices: 163 us -> 105 us
  local copies, waits for them, and re-layouts: 101 us -> 44.6 us
  Pallas kernels: 77.2 us -> 132 us
  waiting for transfers between devices: 222 us -> 171 us
  matrix products: 69.3 us -> 20.6 us
  other arithmetic: 57.3 us -> 30.5 us
    ppermute x85 -> x46, waiting for transfers between devices: 141 us -> 68.6 us  [swap_dp(): lax.ppermute(values_in, 'dp', [(i, i ^ 1 << bit) for i in range(size)])]
    all_to_all x0 -> x4, waiting for transfers between devices: none -> 57.2 us  [exchange(): return lax.all_to_all(values, 'mp', 0, 0)]
    pallas_call x6 -> x9, Pallas kernels: 77.2 us -> 132 us  [the longest x8 107 us: kernel_call(): pl.pallas_call(kernel, out_shape=tuple((jax.ShapeDtypeStruct(shape, dtype...]
    all_gather x1, waiting for transfers between devices: 46.5 us -> 0.01 us  [per_device(): feed_groups = lax.all_gather(feed_part, 'mp')]
    dot_general x13 -> x0, matrix products: 40 us -> none  [the longest x3 11.1 us: filter_bank(): return jnp.dot(hidden, filter_weight, precision=HIGHEST_MODE) * decay_rows]
    ppermute x85 -> x46, starting transfers between devices: 102 us -> 63.9 us  [swap_dp(): lax.ppermute(values_in, 'dp', [(i, i ^ 1 << bit) for i in range(size)])]
    ppermute x33 -> x15, starting transfers between devices: 60.7 us -> 24 us  [shift_mp(): lax.ppermute(values_in, 'mp', [(i, (i + count) % size) for i in range(siz...]
    unnamed x371 -> x157, local copies, waits for them, and re-layouts: 46.9 us -> 25.6 us
  transfers between devices with their start and end apart: 120 -> 67, of which waited for: 39 -> 25; matrix products, arithmetic and copies ran while one was open for 15% -> 13% of each run, Pallas kernels for 2% -> 16%
where the time goes in v2:
time: 529 us; the launch traced here: 521 us
  waiting for transfers between devices  171 us (32%)
  Pallas kernels  132 us (25%)
  starting transfers between devices  105 us (20%)
  local copies, waits for them, and re-layouts  44.6 us (8%)
  other arithmetic  30.5 us (6%)
  matrix products  20.6 us (4%)
  between operations  16 us (3%)
    pallas_call x8, Pallas kernels, kernel_call(): pl.pallas_call(kernel, out_shape=tuple((jax.ShapeDtypeStruct(shape, dtype...  107 us
    ppermute x46, waiting for transfers between devices, swap_dp(): lax.ppermute(values_in, 'dp', [(i, i ^ 1 << bit) for i in range(size)])  68.6 us
    ppermute x46, starting transfers between devices, swap_dp(): lax.ppermute(values_in, 'dp', [(i, i ^ 1 << bit) for i in range(size)])  63.9 us
    all_to_all x4, waiting for transfers between devices, exchange(): return lax.all_to_all(values, 'mp', 0, 0)  57.2 us
    ppermute x15, waiting for transfers between devices, shift_mp(): lax.ppermute(values_in, 'mp', [(i, (i + count) % size) for i in range(siz...  45.7 us
    unnamed x157, local copies, waits for them, and re-layouts  25.6 us
    pallas_call x1, Pallas kernels, leave(): pl.pallas_call(functools.partial(leave_kernel, len(blocks)), out_shape=tu...  24.9 us
    ppermute x15, starting transfers between devices, shift_mp(): lax.ppermute(values_in, 'mp', [(i, (i + count) % size) for i in range(siz...  24 us
  transfers between devices with their start and end apart: 67, of which 25 were waited for; matrix products, arithmetic and copies ran while one was open for 13% of the time, Pallas kernels for 16%

profile of v2, /device:TPU:1, one launch (start us, length us, event | category | flops | bytes accessed | tf_op | source)
XLA Modules:
  0.0 520.5 jit_solution(13496175869346485643)
XLA Ops:
  7.3 1.7 copy.87
  9.0 2.2 collective-permute-start.4
  11.2 2.3 collective-permute-start.5
  14.6 3.9 copy.90
  24.0 3.3 collective-permute-done.1
  27.3 1.9 collective-permute-start.3
  29.3 8.6 %filter_taps.1 = (bf16[2048,256]{1,0:T(8,128)(2,1)S(1)}, f32[3,64,2048]{2,1,0:T(8,128)S(1)}, f32[3,64,2048]{2,1,0:T(8,128)S(1)}, f32[3,64,2048]{2,1,0:T(8,128)S(1)}) custom-call(s32[3]{0:T(128)S(1)} %pad_add_fusion.here_ref, f32[40,2048]{1,0:T(8,128)S(1)} %copy-done.28, f32[40,64]{1,0:T(8,128)S(1)} %pad.9.enter_ref, f32[64,64]{1,0:T(8,128)S(1)} %copy-done.16, ...), custom_call_target="tpu_custom_call" | custom-call | flops 4000000000 | bytes 6291456 | tf_op jit(solution)/shard_map/filter_taps/pallas_call | solution.py:273
  40.4 5.7 %collective-permute-done.halo_ref = f32[16,1024]{1,0:T(8,128)S(1)} collective-permute-done((f32[16,1024]{1,0:T(8,128)S(1)}, f32[16,1024]{1,0:T(8,128)S(1)}, u32[]{:S(2)}, u32[]{:S(2)}) %collective-permute-start) | collective-permute-done | bytes 65568 | tf_op jit(solution)/shard_map/ppermute | solution.py:327
  48.8 3.5 collective-permute-done.11
  55.1 10.7 %collective-permute-start.13 = (bf16[2,3,3,16,1024]{4,3,2,1,0:T(8,128)(2,1)S(1)}, bf16[2,3,3,16,1024]{4,3,2,1,0:T(8,128)(2,1)S(1)}, u32[]{:S(2)}, u32[]{:S(2)}) collective-permute-start(bf16[2,3,3,16,1024]{4,3,2,1,0:T(8,128)(2,1)S(1)} %pad_maximum_fusion.10.refs_4_.refs_21_), channel_id=1, source_target_pairs={{0,4},{4,0},{8,12},{12,8},{16,20},{20,16},{24,28},{28,24},{1,5},{5... | collective-permute-start | bytes 1769480 | tf_op jit(solution)/shard_map/ppermute | solution.py:332
  65.8 6.6 %collective-permute-start.14 = (bf16[2,3,3,16,1024]{4,3,2,1,0:T(8,128)(2,1)S(1)}, bf16[2,3,3,16,1024]{4,3,2,1,0:T(8,128)(2,1)S(1)}, u32[]{:S(2)}, u32[]{:S(2)}) collective-permute-start(bf16[2,3,3,16,1024]{4,3,2,1,0:T(8,128)(2,1)S(1)} %collective-permute-done.12.refs_5_.refs_22_), channel_id=1, source_target_pairs={{0,4},{4,0},{8,12},{12,8},{16,20},{20,16},{24,28},{28,24},{1,5},{5... | collective-permute-start | bytes 1769480 | tf_op jit(solution)/shard_map/ppermute | solution.py:332
  75.5 12.2 %enter.1 = (bf16[4,512,256]{2,1,0:T(8,128)(2,1)}, bf16[4,512,256]{2,1,0:T(8,128)(2,1)S(1)}, bf16[4,2,512,256]{3,2,1,0:T(8,128)(2,1)S(1)}, bf16[4,3,528,256]{3,2,1,0:T(8,128)(2,1)}, bf16[512,1024]{1,0:T(8,128)(2,1)S(1)}) custom-call(s32[3]{0:T(128)S(1)} %pad_add_fusion.here_ref, f32[512,1024]{1,0:T(8,128)S(1)} %copy-done.7, ...), custom_call_target="tpu_custom_call" | custom-call | flops 3221225472 | bytes 16777216 | tf_op jit(solution)/shard_map/enter/pallas_call | solution.py:273
  91.1 3.9 all-to-all-start
  98.6 21.7 %all-to-all-done = bf16[4,512,256]{2,1,0:T(8,128)(2,1)S(1)} async-done(((bf16[4,512,256]{2,1,0:T(8,128)(2,1)}), bf16[4,512,256]{2,1,0:T(8,128)(2,1)S(1)}, u32[]{:S(2)}, u32[]{:S(2)}) %all-to-all-start) | async-done | bytes 1048608 | tf_op jit(solution)/shard_map/all_to_all | solution.py:1102
  120.3 2.7 pad_maximum_fusion.7.refs_15_
  124.4 2.6 pad_maximum_fusion.6.refs_11_
  127.4 13.2 %long_conv.1 = (bf16[32,64,256]{2,1,0:T(8,128)(2,1)}, bf16[64,64,256]{2,1,0:T(8,128)(2,1)S(1)}, bf16[64,64,256]{2,1,0:T(8,128)(2,1)S(1)}) custom-call(bf16[1024,512]{1,0:T(8,128)(2,1)S(1)} %copy-done.18, bf16[32,128,128]{2,1,0:T(8,128)(2,1)S(1)} %copy-done.20, bf16[32,128,128]{2,1,0:T(8,128)(2,1)S(1)} %copy-done.22, bf16[512,1024]{1,0:T(8,128)(2,1)S(1)} %copy-done.24, ...), custom_call_target="tpu_custom_call" | custom-call | flops 8999999488 | bytes 14680064 | tf_op jit(solution)/shard_map/long_conv/pallas_call | solution.py:273
  143.3 4.1 all-to-all-start.1
  147.4 2.1 collective-permute-start.21
  149.5 23.0 %all-to-all-done.1.refs_0_ = bf16[4,512,256]{2,1,0:T(8,128)(2,1)S(1)} async-done(((bf16[4,512,256]{2,1,0:T(8,128)(2,1)}), bf16[4,512,256]{2,1,0:T(8,128)(2,1)S(1)}, u32[]{:S(2)}, u32[]{:S(2)}) %all-to-all-start.1) | async-done | bytes 1048608 | tf_op jit(solution)/shard_map/all_to_all | solution.py:1102
  175.4 2.3 collective-permute-done.22.refs_18_
  177.7 2.5 collective-permute-done.19.refs_14_
  180.2 45.5 %middle.1 = (f32[512,1024]{1,0:T(8,128)}, f32[512,1024]{1,0:T(8,128)}, bf16[4,512,256]{2,1,0:T(8,128)(2,1)}, bf16[4,512,256]{2,1,0:T(8,128)(2,1)}, bf16[512,1024...) custom-call(s32[3]{0:T(128)} %copy-done.5, ...), custom_call_target="tpu_custom_call" | custom-call | flops 20000000000 | bytes 50331648 | tf_op jit(solution)/shard_map/middle/pallas_call | solution.py:273
  225.7 6.4 %convolution_convert_fusion.1 = bf16[2048,1024]{1,0:T(8,128)(2,1)} fusion(bf16[512,1024]{1,0:T(8,128)(2,1)} %get-tuple-element.106, bf16[2,512,2048]{2,1,0:T(8,128)(2,1)} %get-tuple-element.105), kind=kOutput, calls=%fused_computation.7 | convolution fusion | flops 2149580800 | bytes 7340032 | tf_op jit(solution)/shard_map/dot_general | solution.py:423
  232.5 4.4 convolution_convert_fusion
  237.0 3.5 all-to-all-start.2
  241.4 3.2 collective-permute-start.23
  245.8 13.3 %collective-permute-done.23.refs_2_ = bf16[4,2,16,256]{3,2,1,0:T(8,128)(2,1)S(1)} collective-permute-done((bf16[4,2,16,256]{3,2,1,0:T(8,128)(2,1)S(1)}, bf16[4,2,16,256]{3,2,1,0:T(8,128)(2,1)S(1)}, u32[]{:S(2)}, u32[]{:S(2)}) %collective-permute-start.23) | collective-permute-done | bytes 65568 | tf_op jit(solution)/shard_map/ppermute | solution.py:327
  260.5 5.5 %all-to-all-done.2 = bf16[4,512,256]{2,1,0:T(8,128)(2,1)S(1)} async-done(((bf16[4,512,256]{2,1,0:T(8,128)(2,1)}), bf16[4,512,256]{2,1,0:T(8,128)(2,1)S(1)}, u32[]{:S(2)}, u32[]{:S(2)}) %all-to-all-start.2) | async-done | bytes 1048608 | tf_op jit(solution)/shard_map/all_to_all | solution.py:1102
  270.9 1.6 copy-done.39
  272.5 1.6 copy-done.41
  274.1 13.6 %long_conv_back.1 = (bf16[4,528,256]{2,1,0:T(8,128)(2,1)}, f32[32,64,256]{2,1,0:T(8,128)S(1)}) custom-call(bf16[1024,512]{1,0:T(8,128)(2,1)S(1)} %copy-done.19, bf16[32,128,128]{2,1,0:T(8,128)(2,1)S(1)} %copy-done.21, bf16[32,128,128]{2,1,0:T(8,128)(2,1)S(1)} %copy-done.23, bf16[512,1024]{1,0:T(8,128)(2,1)S(1)} %copy-done.25, ...), custom_call_target="tpu_custom_call" | custom-call | flops 8999999488 | bytes 14680064 | tf_op jit(solution)/shard_map/long_conv_back/pallas_call | solution.py:273
  287.7 5.4 %all-to-all-start.3 = ((bf16[4,528,256]{2,1,0:T(8,128)(2,1)}), bf16[4,528,256]{2,1,0:T(8,128)(2,1)}, u32[]{:S(2)}, u32[]{:S(2)}) async-start(bf16[4,528,256]{2,1,0:T(8,128)(2,1)} %get-tuple-element.102), calls=%async_computation.3 | async-start | bytes 2162688 | tf_op jit(solution)/shard_map/all_to_all | solution.py:1102
  293.3 5.2 %add_convert_fusion.2 = bf16[2048,1024]{1,0:T(8,128)(2,1)S(1)} fusion(bf16[2048,1024]{1,0:T(8,128)(2,1)} %collective-permute-done.25, bf16[512,1024]{1,0:T(8,128)(2,1)S(1)} %copy-done.72, bf16[2,512,2048]{2,1,0:T(8,128)(2,1)} %get-tuple-element.105), kind=kOutput, calls=%fused_computation.2 | convolution fusion | flops 2153775104 | bytes 11534336 | tf_op jit(solution)/shard_map/dot_general | solution.py:423
  301.4 4.6 add_convert_fusion.1
  306.0 1.8 slice_bitcast_fusion.2
  312.2 7.0 %all-to-all-done.3.refs_0_ = bf16[4,528,256]{2,1,0:T(8,128)(2,1)} async-done(((bf16[4,528,256]{2,1,0:T(8,128)(2,1)}), bf16[4,528,256]{2,1,0:T(8,128)(2,1)}, u32[]{:S(2)}, u32[]{:S(2)}) %all-to-all-start.3) | async-done | bytes 1081376 | tf_op jit(solution)/shard_map/all_to_all | solution.py:1102
  319.2 24.9 %leave.1 = (f32[512,1024]{1,0:T(8,128)}, f32[4,32,256]{2,1,0:T(8,128)}, f32[32,256]{1,0:T(8,128)}, bf16[2,2,2,8,32,1024]{5,4,3,2,1,0:T(8,128)(2,1)}, bf16[2,2,2,8,32,1024]{5,4,3,2,1,0:T(8,128)(2,1)}) custom-call(s32[3]{0:T(128)} %copy-done.5, bf16[4,528,256]{2,1,0:T(8,128)(2,1)} %all-to-all-done.3.refs_0_, bf16[4,512,256]{2,1,0:T(8,128)(2,1)} %get-tuple-element.96.refs_1_, ...), custom_call_target="tpu_custom_call" | custom-call | flops 16000000000 | bytes 35651584 | tf_op jit(solution)/shard_map/leave/pallas_call | solution.py:930
  345.6 1.8 pad_maximum_fusion.3
  347.7 7.6 %collective-permute-done.45 = bf16[2,2,2,128,1024]{4,3,2,0,1:T(8,128)(2,1)} collective-permute-done((bf16[2,2,2,128,1024]{4,3,2,0,1:T(8,128)(2,1)}, bf16[2,2,2,128,1024]{4,3,2,0,1:T(8,128)(2,1)}, u32[]{:S(2)}, u32[]{:S(2)}) %collective-permute-start.45) | collective-permute-done | bytes 2097184 | tf_op jit(solution)/shard_map/ppermute | solution.py:332
  355.3 2.6 add_convert_fusion.3
  359.8 2.6 fusion
  364.5 17.1 %collective-permute-done.46 = bf16[2,2,128,1024]{3,2,1,0:T(8,128)(2,1)S(1)} collective-permute-done((bf16[2,2,128,1024]{3,2,1,0:T(8,128)(2,1)}, bf16[2,2,128,1024]{3,2,1,0:T(8,128)(2,1)S(1)}, u32[]{:S(2)}, u32[]{:S(2)}) %collective-permute-start.46) | collective-permute-done | bytes 1048608 | tf_op jit(solution)/shard_map/ppermute | solution.py:332
  381.6 1.6 fusion.1
  383.2 3.2 collective-permute-done.44
  386.4 1.6 fusion.2
  388.8 1.6 pad_maximum_fusion.4
  390.4 5.6 %add_convert_fusion = bf16[2,2,2,8,32,1024]{5,4,3,2,1,0:T(8,128)(2,1)S(1)} fusion(bf16[2,2,2,8,32,1024]{5,4,3,2,1,0:T(8,128)(2,1)} %collective-permute-done.27, bf16[2,2,2,8,32,1024]{5,4,3,2,1,0:T(8,128)(2,1)} %get-tuple-element.122), kind=kLoop, calls=%fused_computation | loop fusion | flops 8388608 | bytes 12582912 | tf_op jit(solution)/shard_map/convert_element_type | solution.py:1199
  398.5 6.2 %filter_back.1 = (f32[64,256]{1,0:T(8,128)S(1)}, f32[64,256]{1,0:T(8,128)S(1)}) custom-call(s32[3]{0:T(128)S(1)} %copy-done.6, f32[40,2048]{1,0:T(8,128)S(1)} %copy-done.29, f32[64,64]{1,0:T(8,128)S(1)} %copy-done.16, f32[64,64]{1,0:T(8,128)S(1)} %copy-done.17, f32[64,4]{1,0:T(8,128)S(1)} %copy.89.columns_ref, f32[64,256]{1,0:T(8,128)S(1)} %copy-done.15, ...), custom_call_target="tpu_custom_call" | custom-call | flops 8000000000 | bytes 6291456 | tf_op jit(solution)/shard_map/filter_back/pallas_call | solution.py:273
  404.8 13.1 %collective-permute-done.28 = bf16[2,8,32,1024]{3,2,1,0:T(8,128)(2,1)S(1)} collective-permute-done((bf16[2,8,32,1024]{3,2,1,0:T(8,128)(2,1)S(1)}, bf16[2,8,32,1024]{3,2,1,0:T(8,128)(2,1)S(1)}, u32[]{:S(2)}, u32[]{:S(2)}) %collective-permute-start.28) | collective-permute-done | bytes 1048608 | tf_op jit(solution)/shard_map/ppermute | solution.py:332
  419.2 5.6 %collective-permute-start.30 = (f32[320,256]{1,0:T(8,128)S(1)}, f32[320,256]{1,0:T(8,128)S(1)}, u32[]{:S(2)}, u32[]{:S(2)}) collective-permute-start(f32[320,256]{1,0:T(8,128)S(1)} %constant_dynamic-update-slice_fusion), channel_id=1, source_target_pairs={{0,4},{4,0},{8,12},{12,8},{16,20},{20,16},{24,28},{28,24},{1,5},{5... | collective-permute-start | bytes 983048 | tf_op jit(solution)/shard_map/ppermute | solution.py:332
  426.1 1.8 collective-permute-start.31
  427.9 2.5 collective-permute-done.36
  430.6 2.8 collective-permute-start.37
  433.4 5.1 collective-permute-done.38
  438.7 2.1 collective-permute-start.39
  443.1 14.6 %collective-permute-done.39 = bf16[4,32,1024]{2,1,0:T(8,128)(2,1)S(1)} collective-permute-done((bf16[4,32,1024]{2,1,0:T(8,128)(2,1)S(1)}, bf16[4,32,1024]{2,1,0:T(8,128)(2,1)S(1)}, u32[]{:S(2)}, u32[]{:S(2)}) %collective-permute-start.39) | collective-permute-done | bytes 262176 | tf_op jit(solution)/shard_map/ppermute | solution.py:327
  458.0 3.3 collective-permute-start.57
  462.1 3.8 collective-permute-start.34
  472.9 7.3 %collective-permute-done.34 = f32[160,256]{1,0:T(8,128)S(1)} collective-permute-done((f32[160,256]{1,0:T(8,128)S(1)}, f32[160,256]{1,0:T(8,128)S(1)}, u32[]{:S(2)}, u32[]{:S(2)}) %collective-permute-start.34) | collective-permute-done | bytes 163872 | tf_op jit(solution)/shard_map/ppermute | solution.py:327
  482.8 3.7 collective-permute-start.53
  487.1 7.2 %collective-permute-done.52.refs_5_ = bf16[2,128,1024]{2,1,0:T(8,128)(2,1)S(1)} collective-permute-done((bf16[2,128,1024]{2,1,0:T(8,128)(2,1)S(1)}, bf16[2,128,1024]{2,1,0:T(8,128)(2,1)S(1)}, u32[]{:S(2)}, u32[]{:S(2)}) %collective-permute-start.52) | collective-permute-done | bytes 524320 | tf_op jit(solution)/shard_map/ppermute | solution.py:332
  498.4 4.7 place_feed.1
  510.2 3.4 place_input.1
  (325 shorter events, 83.9 us)
Async XLA Ops:
  7.2 87.8 %all-gather.3.cloned.1.call-start = ((), (), s32[]{:S(2)}) async-start(), calls=%async_computation.6 | async-start | bytes 2949120 | tf_op jit(solution)/shard_map/all_gather | solution.py:1085
  9.0 31.3 %collective-permute-start.4 = (bf16[3,32,1024]{2,1,0:T(8,128)(2,1)S(1)}, bf16[3,32,1024]{2,1,0:T(8,128)(2,1)S(1)}, u32[]{:S(2)}, u32[]{:S(2)}) collective-permute-start(bf16[3,32,1024]{2,1,0:T(8,128)(2,1)S(1)} %dynamic-slice_bitcast_fusion.1), channel_id=1, source_target_pairs={{0,1},{1,2},{2,3},{3,0},{4,5},{5,6},{6,7},{7,4},{8,9},{9,10},{10,1... | collective-permute-start | bytes 589832 | tf_op jit(solution)/shard_map/ppermute | solution.py:327
  11.2 29.1 %collective-permute-start.5 = (bf16[3,32,1024]{2,1,0:T(8,128)(2,1)S(1)}, bf16[3,32,1024]{2,1,0:T(8,128)(2,1)S(1)}, u32[]{:S(2)}, u32[]{:S(2)}) collective-permute-start(bf16[3,32,1024]{2,1,0:T(8,128)(2,1)S(1)} %dynamic-slice_bitcast_fusion.1), channel_id=1, source_target_pairs={{0,2},{1,3},{2,0},{3,1},{4,6},{5,7},{6,4},{7,5},{8,10},{9,11},{10,... | collective-permute-start | bytes 589832 | tf_op jit(solution)/shard_map/ppermute | solution.py:327
  13.5 26.8 %collective-permute-start.6 = (bf16[3,32,1024]{2,1,0:T(8,128)(2,1)S(1)}, bf16[3,32,1024]{2,1,0:T(8,128)(2,1)S(1)}, u32[]{:S(2)}, u32[]{:S(2)}) collective-permute-start(bf16[3,32,1024]{2,1,0:T(8,128)(2,1)S(1)} %dynamic-slice_bitcast_fusion.1), channel_id=1, source_target_pairs={{0,3},{1,0},{2,1},{3,2},{4,7},{5,4},{6,5},{7,6},{8,11},{9,8},{10,9... | collective-permute-start | bytes 589832 | tf_op jit(solution)/shard_map/ppermute | solution.py:327
  22.6 4.7 collective-permute-start.1
  23.1 16.1 %collective-permute-start.2 = (f32[32,256]{1,0:T(8,128)S(1)}, f32[32,256]{1,0:T(8,128)S(1)}, u32[]{:S(2)}, u32[]{:S(2)}) collective-permute-start(f32[32,256]{1,0:T(8,128)S(1)} %get-tuple-element.203), channel_id=1, source_target_pairs={{0,2},{1,3},{2,0},{3,1},{4,6},{5,7},{6,4},{7,5},{8,10},{9,11},{10,... | collective-permute-start | bytes 98312 | tf_op jit(solution)/shard_map/ppermute | solution.py:327
  27.3 12.9 %collective-permute-start.3 = (f32[32,256]{1,0:T(8,128)S(1)}, f32[32,256]{1,0:T(8,128)S(1)}, u32[]{:S(2)}, u32[]{:S(2)}) collective-permute-start(f32[32,256]{1,0:T(8,128)S(1)} %get-tuple-element.203), channel_id=1, source_target_pairs={{0,3},{1,0},{2,1},{3,2},{4,7},{5,4},{6,5},{7,6},{8,11},{9,8},{10,9... | collective-permute-start | bytes 98312 | tf_op jit(solution)/shard_map/ppermute | solution.py:327
  39.1 7.0 %collective-permute-start = (f32[16,1024]{1,0:T(8,128)S(1)}, f32[16,1024]{1,0:T(8,128)S(1)}, u32[]{:S(2)}, u32[]{:S(2)}) collective-permute-start(f32[16,1024]{1,0:T(8,128)S(1)} %slice.262), channel_id=1, source_target_pairs={{0,1},{1,2},{2,3},{3,0},{4,5},{5,6},{6,7},{7,4},{8,9},{9,10},{10,1... | collective-permute-start | bytes 196616 | tf_op jit(solution)/shard_map/ppermute | solution.py:327
  46.3 6.0 %collective-permute-start.11 = (bf16[3,3,16,1024]{3,2,1,0:T(8,128)(2,1)S(1)}, bf16[3,3,16,1024]{3,2,1,0:T(8,128)(2,1)S(1)}, u32[]{:S(2)}, u32[]{:S(2)}) collective-permute-start(bf16[3,3,16,1024]{3,2,1,0:T(8,128)(2,1)S(1)} %get-tuple-element.170), channel_id=1, source_target_pairs={{0,8},{4,12},{8,0},{12,4},{16,24},{20,28},{24,16},{28,20},{1,9},{5... | collective-permute-start | bytes 884744 | tf_op jit(solution)/shard_map/ppermute | solution.py:332
  47.6 6.2 %collective-permute-start.7 = (bf16[3,3,16,1024]{3,2,1,0:T(8,128)(2,1)S(1)}, bf16[3,3,16,1024]{3,2,1,0:T(8,128)(2,1)S(1)}, u32[]{:S(2)}, u32[]{:S(2)}) collective-permute-start(bf16[3,3,16,1024]{3,2,1,0:T(8,128)(2,1)S(1)} %get-tuple-element.171), channel_id=1, source_target_pairs={{0,16},{4,20},{8,24},{12,28},{16,0},{20,4},{24,8},{28,12},{1,17},{... | collective-permute-start | bytes 884744 | tf_op jit(solution)/shard_map/ppermute | solution.py:332
  52.4 13.4 %collective-permute-start.12 = (bf16[2,3,3,16,1024]{4,3,2,1,0:T(8,128)(2,1)S(1)}, bf16[2,3,3,16,1024]{4,3,2,1,0:T(8,128)(2,1)S(1)}, u32[]{:S(2)}, u32[]{:S(2)}) collective-permute-start(bf16[2,3,3,16,1024]{4,3,2,1,0:T(8,128)(2,1)S(1)} %pad_maximum_fusion.10.refs_4_.refs_21_), channel_id=1, source_target_pairs={{0,16},{4,20},{8,24},{12,28},{16,0},{20,4},{24,8},{28,12},{1,17},{... | collective-permute-start | bytes 1769480 | tf_op jit(solution)/shard_map/ppermute | solution.py:332
  53.8 18.6 %collective-permute-start.8 = (bf16[2,3,3,16,1024]{4,3,2,1,0:T(8,128)(2,1)S(1)}, bf16[2,3,3,16,1024]{4,3,2,1,0:T(8,128)(2,1)S(1)}, u32[]{:S(2)}, u32[]{:S(2)}) collective-permute-start(bf16[2,3,3,16,1024]{4,3,2,1,0:T(8,128)(2,1)S(1)} %pad_maximum_fusion.9.refs_0_.refs_17_), channel_id=1, source_target_pairs={{0,8},{4,12},{8,0},{12,4},{16,24},{20,28},{24,16},{28,20},{1,9},{5... | collective-permute-start | bytes 1769480 | tf_op jit(solution)/shard_map/ppermute | solution.py:332
  55.1 18.8 %collective-permute-start.13 = (bf16[2,3,3,16,1024]{4,3,2,1,0:T(8,128)(2,1)S(1)}, bf16[2,3,3,16,1024]{4,3,2,1,0:T(8,128)(2,1)S(1)}, u32[]{:S(2)}, u32[]{:S(2)}) collective-permute-start(bf16[2,3,3,16,1024]{4,3,2,1,0:T(8,128)(2,1)S(1)} %pad_maximum_fusion.10.refs_4_.refs_21_), channel_id=1, source_target_pairs={{0,4},{4,0},{8,12},{12,8},{16,20},{20,16},{24,28},{28,24},{1,5},{5... | collective-permute-start | bytes 1769480 | tf_op jit(solution)/shard_map/ppermute | solution.py:332
  65.8 8.2 %collective-permute-start.9 = (bf16[2,3,3,16,1024]{4,3,2,1,0:T(8,128)(2,1)S(1)}, bf16[2,3,3,16,1024]{4,3,2,1,0:T(8,128)(2,1)S(1)}, u32[]{:S(2)}, u32[]{:S(2)}) collective-permute-start(bf16[2,3,3,16,1024]{4,3,2,1,0:T(8,128)(2,1)S(1)} %pad_maximum_fusion.9.refs_0_.refs_17_), channel_id=1, source_target_pairs={{0,4},{4,0},{8,12},{12,8},{16,20},{20,16},{24,28},{28,24},{1,5},{5... | collective-permute-start | bytes 1769480 | tf_op jit(solution)/shard_map/ppermute | solution.py:332
  65.8 8.2 %collective-permute-start.14 = (bf16[2,3,3,16,1024]{4,3,2,1,0:T(8,128)(2,1)S(1)}, bf16[2,3,3,16,1024]{4,3,2,1,0:T(8,128)(2,1)S(1)}, u32[]{:S(2)}, u32[]{:S(2)}) collective-permute-start(bf16[2,3,3,16,1024]{4,3,2,1,0:T(8,128)(2,1)S(1)} %collective-permute-done.12.refs_5_.refs_22_), channel_id=1, source_target_pairs={{0,4},{4,0},{8,12},{12,8},{16,20},{20,16},{24,28},{28,24},{1,5},{5... | collective-permute-start | bytes 1769480 | tf_op jit(solution)/shard_map/ppermute | solution.py:332
  91.1 29.2 %all-to-all-start = ((bf16[4,512,256]{2,1,0:T(8,128)(2,1)}), bf16[4,512,256]{2,1,0:T(8,128)(2,1)S(1)}, u32[]{:S(2)}, u32[]{:S(2)}) async-start(bf16[4,512,256]{2,1,0:T(8,128)(2,1)} %get-tuple-element.86.refs_1_), calls=%async_computation | async-start | bytes 2097152 | tf_op jit(solution)/shard_map/all_to_all | solution.py:1102
  96.9 23.4 %collective-permute-start.16 = (bf16[3,144,1024]{2,1,0:T(8,128)(2,1)S(1)}, bf16[3,144,1024]{2,1,0:T(8,128)(2,1)}, u32[]{:S(2)}, u32[]{:S(2)}) collective-permute-start(bf16[3,144,1024]{2,1,0:T(8,128)(2,1)S(1)} %get-tuple-element.89), channel_id=1, source_target_pairs={{0,8},{4,12},{8,0},{12,4},{16,24},{20,28},{24,16},{28,20},{1,9},{5... | collective-permute-start | bytes 2654216 | tf_op jit(solution)/shard_map/ppermute | solution.py:332
  98.2 26.2 %collective-permute-start.15 = (bf16[3,144,1024]{2,1,0:T(8,128)(2,1)S(1)}, bf16[3,144,1024]{2,1,0:T(8,128)(2,1)}, u32[]{:S(2)}, u32[]{:S(2)}) collective-permute-start(bf16[3,144,1024]{2,1,0:T(8,128)(2,1)S(1)} %get-tuple-element.88), channel_id=1, source_target_pairs={{0,16},{4,20},{8,24},{12,28},{16,0},{20,4},{24,8},{28,12},{1,17},{... | collective-permute-start | bytes 2654216 | tf_op jit(solution)/shard_map/ppermute | solution.py:332
  123.0 49.6 %collective-permute-start.20 = (bf16[2,3,144,1024]{3,2,1,0:T(8,128)(2,1)}, bf16[2,3,144,1024]{3,2,1,0:T(8,128)(2,1)}, u32[]{:S(2)}, u32[]{:S(2)}) collective-permute-start(bf16[2,3,144,1024]{3,2,1,0:T(8,128)(2,1)} %pad_maximum_fusion.7.refs_15_), channel_id=1, source_target_pairs={{0,16},{4,20},{8,24},{12,28},{16,0},{20,4},{24,8},{28,12},{1,17},{... | collective-permute-start | bytes 5308424 | tf_op jit(solution)/shard_map/ppermute | solution.py:332
  127.0 47.0 %collective-permute-start.17 = (bf16[2,3,144,1024]{3,2,1,0:T(8,128)(2,1)}, bf16[2,3,144,1024]{3,2,1,0:T(8,128)(2,1)}, u32[]{:S(2)}, u32[]{:S(2)}) collective-permute-start(bf16[2,3,144,1024]{3,2,1,0:T(8,128)(2,1)} %pad_maximum_fusion.6.refs_11_), channel_id=1, source_target_pairs={{0,8},{4,12},{8,0},{12,4},{16,24},{20,28},{24,16},{28,20},{1,9},{5... | collective-permute-start | bytes 5308424 | tf_op jit(solution)/shard_map/ppermute | solution.py:332
  143.3 29.3 %all-to-all-start.1 = ((bf16[4,512,256]{2,1,0:T(8,128)(2,1)}), bf16[4,512,256]{2,1,0:T(8,128)(2,1)S(1)}, u32[]{:S(2)}, u32[]{:S(2)}) async-start(bf16[4,512,256]{2,1,0:T(8,128)(2,1)} %bitcast.34), calls=%async_computation.1 | async-start | bytes 2097152 | tf_op jit(solution)/shard_map/all_to_all | solution.py:1102
  147.4 28.0 %collective-permute-start.21 = (bf16[2,3,144,1024]{3,2,1,0:T(8,128)(2,1)}, bf16[2,3,144,1024]{3,2,1,0:T(8,128)(2,1)}, u32[]{:S(2)}, u32[]{:S(2)}) collective-permute-start(bf16[2,3,144,1024]{3,2,1,0:T(8,128)(2,1)} %pad_maximum_fusion.7.refs_15_), channel_id=1, source_target_pairs={{0,4},{4,0},{8,12},{12,8},{16,20},{20,16},{24,28},{28,24},{1,5},{5... | collective-permute-start | bytes 5308424 | tf_op jit(solution)/shard_map/ppermute | solution.py:332
  149.4 26.0 %collective-permute-start.18 = (bf16[2,3,144,1024]{3,2,1,0:T(8,128)(2,1)}, bf16[2,3,144,1024]{3,2,1,0:T(8,128)(2,1)}, u32[]{:S(2)}, u32[]{:S(2)}) collective-permute-start(bf16[2,3,144,1024]{3,2,1,0:T(8,128)(2,1)} %pad_maximum_fusion.6.refs_11_), channel_id=1, source_target_pairs={{0,4},{4,0},{8,12},{12,8},{16,20},{20,16},{24,28},{28,24},{1,5},{5... | collective-permute-start | bytes 5308424 | tf_op jit(solution)/shard_map/ppermute | solution.py:332
  172.6 5.1 collective-permute-start.22
  174.0 6.2 %collective-permute-start.19 = (bf16[2,3,144,1024]{3,2,1,0:T(8,128)(2,1)}, bf16[2,3,144,1024]{3,2,1,0:T(8,128)(2,1)}, u32[]{:S(2)}, u32[]{:S(2)}) collective-permute-start(bf16[2,3,144,1024]{3,2,1,0:T(8,128)(2,1)} %collective-permute-done.17.refs_12_), channel_id=1, source_target_pairs={{0,4},{4,0},{8,12},{12,8},{16,20},{20,16},{24,28},{28,24},{1,5},{5... | collective-permute-start | bytes 5308424 | tf_op jit(solution)/shard_map/ppermute | solution.py:332
  232.1 61.2 %collective-permute-start.25 = (bf16[2048,1024]{1,0:T(8,128)(2,1)}, bf16[2048,1024]{1,0:T(8,128)(2,1)}, u32[]{:S(2)}, u32[]{:S(2)}) collective-permute-start(bf16[2048,1024]{1,0:T(8,128)(2,1)} %convolution_convert_fusion.1), channel_id=1, source_target_pairs={{0,4},{4,0},{8,12},{12,8},{16,20},{20,16},{24,28},{28,24},{1,5},{5... | collective-permute-start | bytes 12582920 | tf_op jit(solution)/shard_map/ppermute | solution.py:332
  236.9 63.1 %collective-permute-start.26 = (bf16[2048,1024]{1,0:T(8,128)(2,1)}, bf16[2048,1024]{1,0:T(8,128)(2,1)}, u32[]{:S(2)}, u32[]{:S(2)}) collective-permute-start(bf16[2048,1024]{1,0:T(8,128)(2,1)} %convolution_convert_fusion), channel_id=1, source_target_pairs={{0,4},{4,0},{8,12},{12,8},{16,20},{20,16},{24,28},{28,24},{1,5},{5... | collective-permute-start | bytes 12582920 | tf_op jit(solution)/shard_map/ppermute | solution.py:332
  237.0 29.0 %all-to-all-start.2 = ((bf16[4,512,256]{2,1,0:T(8,128)(2,1)}), bf16[4,512,256]{2,1,0:T(8,128)(2,1)S(1)}, u32[]{:S(2)}, u32[]{:S(2)}) async-start(bf16[4,512,256]{2,1,0:T(8,128)(2,1)} %get-tuple-element.96.refs_1_), calls=%async_computation.2 | async-start | bytes 2097152 | tf_op jit(solution)/shard_map/all_to_all | solution.py:1102
  241.4 17.7 %collective-permute-start.23 = (bf16[4,2,16,256]{3,2,1,0:T(8,128)(2,1)S(1)}, bf16[4,2,16,256]{3,2,1,0:T(8,128)(2,1)S(1)}, u32[]{:S(2)}, u32[]{:S(2)}) collective-permute-start(bf16[4,2,16,256]{3,2,1,0:T(8,128)(2,1)S(1)} %slice.270), channel_id=1, source_target_pairs={{0,3},{1,0},{2,1},{3,2},{4,7},{5,4},{6,5},{7,6},{8,11},{9,8},{10,9... | collective-permute-start | bytes 196616 | tf_op jit(solution)/shard_map/ppermute | solution.py:327
  245.4 15.1 %collective-permute-start.24 = (bf16[2,4,16,256]{3,2,1,0:T(8,128)(2,1)S(1)}, bf16[2,4,16,256]{3,2,1,0:T(8,128)(2,1)S(1)}, u32[]{:S(2)}, u32[]{:S(2)}) collective-permute-start(bf16[2,4,16,256]{3,2,1,0:T(8,128)(2,1)S(1)} %pad_maximum_fusion.21), channel_id=1, source_target_pairs={{0,3},{1,0},{2,1},{3,2},{4,7},{5,4},{6,5},{7,6},{8,11},{9,8},{10,9... | collective-permute-start | bytes 196616 | tf_op jit(solution)/shard_map/ppermute | solution.py:327
  287.7 31.4 %all-to-all-start.3 = ((bf16[4,528,256]{2,1,0:T(8,128)(2,1)}), bf16[4,528,256]{2,1,0:T(8,128)(2,1)}, u32[]{:S(2)}, u32[]{:S(2)}) async-start(bf16[4,528,256]{2,1,0:T(8,128)(2,1)} %get-tuple-element.102), calls=%async_computation.3 | async-start | bytes 2162688 | tf_op jit(solution)/shard_map/all_to_all | solution.py:1102
  293.1 175.8 %reduce-scatter.2.cloned.1.call-start = ((), (), s32[]{:S(2)}) async-start(), calls=%async_computation.5 | async-start | bytes 2621440 | tf_op jit(solution)/shard_map/reduce_scatter | solution.py:1203
  309.4 46.0 %collective-permute-start.45 = (bf16[2,2,2,128,1024]{4,3,2,0,1:T(8,128)(2,1)}, bf16[2,2,2,128,1024]{4,3,2,0,1:T(8,128)(2,1)}, u32[]{:S(2)}, u32[]{:S(2)}) collective-permute-start(bf16[2,2,2,128,1024]{4,3,2,0,1:T(8,128)(2,1)} %pad_maximum_fusion.1), channel_id=1, source_target_pairs={{0,8},{4,12},{8,0},{12,4},{16,24},{20,28},{24,16},{28,20},{1,9},{5... | collective-permute-start | bytes 6291464 | tf_op jit(solution)/shard_map/ppermute | solution.py:332
  312.0 47.8 %collective-permute-start.43 = (bf16[2,2,2,128,1024]{4,3,2,1,0:T(8,128)(2,1)}, bf16[2,2,2,128,1024]{4,3,2,1,0:T(8,128)(2,1)}, u32[]{:S(2)}, u32[]{:S(2)}) collective-permute-start(bf16[2,2,2,128,1024]{4,3,2,1,0:T(8,128)(2,1)} %pad_maximum_fusion), channel_id=1, source_target_pairs={{0,16},{4,20},{8,24},{12,28},{16,0},{20,4},{24,8},{28,12},{1,17},{... | collective-permute-start | bytes 6291464 | tf_op jit(solution)/shard_map/ppermute | solution.py:332
  344.1 46.3 %collective-permute-start.27 = (bf16[2,2,2,8,32,1024]{5,4,3,2,1,0:T(8,128)(2,1)}, bf16[2,2,2,8,32,1024]{5,4,3,2,1,0:T(8,128)(2,1)}, u32[]{:S(2)}, u32[]{:S(2)}) collective-permute-start(bf16[2,2,2,8,32,1024]{5,4,3,2,1,0:T(8,128)(2,1)} %get-tuple-element.123), channel_id=1, source_target_pairs={{0,4},{4,0},{8,12},{12,8},{16,20},{20,16},{24,28},{28,24},{1,5},{5... | collective-permute-start | bytes 12582920 | tf_op jit(solution)/shard_map/ppermute | solution.py:332
  359.0 22.6 %collective-permute-start.46 = (bf16[2,2,128,1024]{3,2,1,0:T(8,128)(2,1)}, bf16[2,2,128,1024]{3,2,1,0:T(8,128)(2,1)S(1)}, u32[]{:S(2)}, u32[]{:S(2)}) collective-permute-start(bf16[2,2,128,1024]{3,2,1,0:T(8,128)(2,1)} %slice_bitcast_fusion), channel_id=1, source_target_pairs={{0,16},{4,20},{8,24},{12,28},{16,0},{20,4},{24,8},{28,12},{1,17},{... | collective-permute-start | bytes 3145736 | tf_op jit(solution)/shard_map/ppermute | solution.py:332
  364.1 22.3 %collective-permute-start.44 = (bf16[2,2,128,1024]{3,2,1,0:T(8,128)(2,1)}, bf16[2,2,128,1024]{3,2,1,0:T(8,128)(2,1)}, u32[]{:S(2)}, u32[]{:S(2)}) collective-permute-start(bf16[2,2,128,1024]{3,2,1,0:T(8,128)(2,1)} %slice_bitcast_fusion.4), channel_id=1, source_target_pairs={{0,8},{4,12},{8,0},{12,4},{16,24},{20,28},{24,16},{28,20},{1,9},{5... | collective-permute-start | bytes 3145736 | tf_op jit(solution)/shard_map/ppermute | solution.py:332
  396.7 21.2 %collective-permute-start.28 = (bf16[2,8,32,1024]{3,2,1,0:T(8,128)(2,1)S(1)}, bf16[2,8,32,1024]{3,2,1,0:T(8,128)(2,1)S(1)}, u32[]{:S(2)}, u32[]{:S(2)}) collective-permute-start(bf16[2,8,32,1024]{3,2,1,0:T(8,128)(2,1)S(1)} %get-tuple-element.157), channel_id=1, source_target_pairs={{0,16},{4,20},{8,24},{12,28},{16,0},{20,4},{24,8},{28,12},{1,17},{... | collective-permute-start | bytes 3145736 | tf_op jit(solution)/shard_map/ppermute | solution.py:332
  397.4 21.4 %collective-permute-start.29 = (bf16[2,8,32,1024]{3,2,1,0:T(8,128)(2,1)S(1)}, bf16[2,8,32,1024]{3,2,1,0:T(8,128)(2,1)S(1)}, u32[]{:S(2)}, u32[]{:S(2)}) collective-permute-start(bf16[2,8,32,1024]{3,2,1,0:T(8,128)(2,1)S(1)} %get-tuple-element.156), channel_id=1, source_target_pairs={{0,8},{4,12},{8,0},{12,4},{16,24},{20,28},{24,16},{28,20},{1,9},{5... | collective-permute-start | bytes 3145736 | tf_op jit(solution)/shard_map/ppermute | solution.py:332
  418.4 12.0 %collective-permute-start.36 = (bf16[8,32,1024]{2,1,0:T(8,128)(2,1)S(1)}, bf16[8,32,1024]{2,1,0:T(8,128)(2,1)S(1)}, u32[]{:S(2)}, u32[]{:S(2)}) collective-permute-start(bf16[8,32,1024]{2,1,0:T(8,128)(2,1)S(1)} %slice_bitcast_fusion.18), channel_id=1, source_target_pairs={{0,8},{4,12},{8,0},{12,4},{16,24},{20,28},{24,16},{28,20},{1,9},{5... | collective-permute-start | bytes 1572872 | tf_op jit(solution)/shard_map/ppermute | solution.py:332
  419.2 6.8 %collective-permute-start.30 = (f32[320,256]{1,0:T(8,128)S(1)}, f32[320,256]{1,0:T(8,128)S(1)}, u32[]{:S(2)}, u32[]{:S(2)}) collective-permute-start(f32[320,256]{1,0:T(8,128)S(1)} %constant_dynamic-update-slice_fusion), channel_id=1, source_target_pairs={{0,4},{4,0},{8,12},{12,8},{16,20},{20,16},{24,28},{28,24},{1,5},{5... | collective-permute-start | bytes 983048 | tf_op jit(solution)/shard_map/ppermute | solution.py:332
  424.8 13.6 %collective-permute-start.38 = (bf16[8,32,1024]{2,1,0:T(8,128)(2,1)S(1)}, bf16[8,32,1024]{2,1,0:T(8,128)(2,1)S(1)}, u32[]{:S(2)}, u32[]{:S(2)}) collective-permute-start(bf16[8,32,1024]{2,1,0:T(8,128)(2,1)S(1)} %slice_bitcast_fusion.16), channel_id=1, source_target_pairs={{0,16},{4,20},{8,24},{12,28},{16,0},{20,4},{24,8},{28,12},{1,17},{... | collective-permute-start | bytes 1572872 | tf_op jit(solution)/shard_map/ppermute | solution.py:332
  426.1 15.9 %collective-permute-start.31 = (f32[320,256]{1,0:T(8,128)S(1)}, f32[320,256]{1,0:T(8,128)S(1)}, u32[]{:S(2)}, u32[]{:S(2)}) collective-permute-start(f32[320,256]{1,0:T(8,128)S(1)} %add.133), channel_id=1, source_target_pairs={{0,8},{4,12},{8,0},{12,4},{16,24},{20,28},{24,16},{28,20},{1,9},{5... | collective-permute-start | bytes 983048 | tf_op jit(solution)/shard_map/ppermute | solution.py:332
  430.6 12.5 %collective-permute-start.37 = (bf16[4,32,1024]{2,1,0:T(8,128)(2,1)S(1)}, bf16[4,32,1024]{2,1,0:T(8,128)(2,1)S(1)}, u32[]{:S(2)}, u32[]{:S(2)}) collective-permute-start(bf16[4,32,1024]{2,1,0:T(8,128)(2,1)S(1)} %slice.355), channel_id=1, source_target_pairs={{0,3},{1,0},{2,1},{3,2},{4,7},{5,4},{6,5},{7,6},{8,11},{9,8},{10,9... | collective-permute-start | bytes 786440 | tf_op jit(solution)/shard_map/ppermute | solution.py:327
  438.7 19.0 %collective-permute-start.39 = (bf16[4,32,1024]{2,1,0:T(8,128)(2,1)S(1)}, bf16[4,32,1024]{2,1,0:T(8,128)(2,1)S(1)}, u32[]{:S(2)}, u32[]{:S(2)}) collective-permute-start(bf16[4,32,1024]{2,1,0:T(8,128)(2,1)S(1)} %get-tuple-element.176), channel_id=1, source_target_pairs={{0,2},{1,3},{2,0},{3,1},{4,6},{5,7},{6,4},{7,5},{8,10},{9,11},{10,... | collective-permute-start | bytes 786440 | tf_op jit(solution)/shard_map/ppermute | solution.py:327
  440.8 16.9 %collective-permute-start.40 = (bf16[4,32,1024]{2,1,0:T(8,128)(2,1)S(1)}, bf16[4,32,1024]{2,1,0:T(8,128)(2,1)S(1)}, u32[]{:S(2)}, u32[]{:S(2)}) collective-permute-start(bf16[4,32,1024]{2,1,0:T(8,128)(2,1)S(1)} %get-tuple-element.177), channel_id=1, source_target_pairs={{0,1},{1,2},{2,3},{3,0},{4,5},{5,6},{6,7},{7,4},{8,9},{9,10},{10,1... | collective-permute-start | bytes 786440 | tf_op jit(solution)/shard_map/ppermute | solution.py:327
  442.1 15.8 %collective-permute-start.32 = (f32[320,256]{1,0:T(8,128)S(1)}, f32[320,256]{1,0:T(8,128)S(1)}, u32[]{:S(2)}, u32[]{:S(2)}) collective-permute-start(f32[320,256]{1,0:T(8,128)S(1)} %add.134), channel_id=1, source_target_pairs={{0,16},{4,20},{8,24},{12,28},{16,0},{20,4},{24,8},{28,12},{1,17},{... | collective-permute-start | bytes 983048 | tf_op jit(solution)/shard_map/ppermute | solution.py:332
  458.0 10.1 %collective-permute-start.57 = (bf16[4,16,1024]{2,1,0:T(8,128)(2,1)S(1)}, bf16[4,16,1024]{2,1,0:T(8,128)(2,1)S(1)}, u32[]{:S(2)}, u32[]{:S(2)}) collective-permute-start(bf16[4,16,1024]{2,1,0:T(8,128)(2,1)S(1)} %get-tuple-element.185), channel_id=1, source_target_pairs={{0,8},{4,12},{8,0},{12,4},{16,24},{20,28},{24,16},{28,20},{1,9},{5... | collective-permute-start | bytes 393224 | tf_op jit(solution)/shard_map/ppermute | solution.py:332
  462.1 9.9 %collective-permute-start.33 = (f32[160,256]{1,0:T(8,128)S(1)}, f32[160,256]{1,0:T(8,128)S(1)}, u32[]{:S(2)}, u32[]{:S(2)}) collective-permute-start(f32[160,256]{1,0:T(8,128)S(1)} %get-tuple-element.193), channel_id=1, source_target_pairs={{0,3},{1,0},{2,1},{3,2},{4,7},{5,4},{6,5},{7,6},{8,11},{9,8},{10,9... | collective-permute-start | bytes 491528 | tf_op jit(solution)/shard_map/ppermute | solution.py:327
  462.1 18.1 %collective-permute-start.34 = (f32[160,256]{1,0:T(8,128)S(1)}, f32[160,256]{1,0:T(8,128)S(1)}, u32[]{:S(2)}, u32[]{:S(2)}) collective-permute-start(f32[160,256]{1,0:T(8,128)S(1)} %get-tuple-element.194), channel_id=1, source_target_pairs={{0,2},{1,3},{2,0},{3,1},{4,6},{5,7},{6,4},{7,5},{8,10},{9,11},{10,... | collective-permute-start | bytes 491528 | tf_op jit(solution)/shard_map/ppermute | solution.py:327
  466.0 14.3 %collective-permute-start.35 = (f32[160,256]{1,0:T(8,128)S(1)}, f32[160,256]{1,0:T(8,128)S(1)}, u32[]{:S(2)}, u32[]{:S(2)}) collective-permute-start(f32[160,256]{1,0:T(8,128)S(1)} %get-tuple-element.195), channel_id=1, source_target_pairs={{0,1},{1,2},{2,3},{3,0},{4,5},{5,6},{6,7},{7,4},{8,9},{9,10},{10,1... | collective-permute-start | bytes 491528 | tf_op jit(solution)/shard_map/ppermute | solution.py:327
  468.2 34.9 %collective-permute-start.58 = (bf16[2,4,16,1024]{3,2,1,0:T(8,128)(2,1)S(1)}, bf16[2,4,16,1024]{3,2,1,0:T(8,128)(2,1)S(1)}, u32[]{:S(2)}, u32[]{:S(2)}) collective-permute-start(bf16[2,4,16,1024]{3,2,1,0:T(8,128)(2,1)S(1)} %pad_maximum_fusion.15.refs_4_), channel_id=1, source_target_pairs={{0,16},{4,20},{8,24},{12,28},{16,0},{20,4},{24,8},{28,12},{1,17},{... | collective-permute-start | bytes 786440 | tf_op jit(solution)/shard_map/ppermute | solution.py:332
  471.2 9.1 %collective-permute-start.51 = (bf16[128,1024]{1,0:T(8,128)(2,1)S(1)}, bf16[128,1024]{1,0:T(8,128)(2,1)S(1)}, u32[]{:S(2)}, u32[]{:S(2)}) collective-permute-start(bf16[128,1024]{1,0:T(8,128)(2,1)S(1)} %get-tuple-element.174), channel_id=1, source_target_pairs={{0,8},{4,12},{8,0},{12,4},{16,24},{20,28},{24,16},{28,20},{1,9},{5... | collective-permute-start | bytes 786440 | tf_op jit(solution)/shard_map/ppermute | solution.py:332
  471.9 10.0 %collective-permute-start.47 = (bf16[128,1024]{1,0:T(8,128)(2,1)S(1)}, bf16[128,1024]{1,0:T(8,128)(2,1)S(1)}, u32[]{:S(2)}, u32[]{:S(2)}) collective-permute-start(bf16[128,1024]{1,0:T(8,128)(2,1)S(1)} %get-tuple-element.175), channel_id=1, source_target_pairs={{0,16},{4,20},{8,24},{12,28},{16,0},{20,4},{24,8},{28,12},{1,17},{... | collective-permute-start | bytes 786440 | tf_op jit(solution)/shard_map/ppermute | solution.py:332
  480.4 14.0 %collective-permute-start.52 = (bf16[2,128,1024]{2,1,0:T(8,128)(2,1)S(1)}, bf16[2,128,1024]{2,1,0:T(8,128)(2,1)S(1)}, u32[]{:S(2)}, u32[]{:S(2)}) collective-permute-start(bf16[2,128,1024]{2,1,0:T(8,128)(2,1)S(1)} %pad_maximum_fusion.13.refs_4_), channel_id=1, source_target_pairs={{0,16},{4,20},{8,24},{12,28},{16,0},{20,4},{24,8},{28,12},{1,17},{... | collective-permute-start | bytes 1572872 | tf_op jit(solution)/shard_map/ppermute | solution.py:332
  482.0 13.7 %collective-permute-start.48 = (bf16[2,128,1024]{2,1,0:T(8,128)(2,1)S(1)}, bf16[2,128,1024]{2,1,0:T(8,128)(2,1)S(1)}, u32[]{:S(2)}, u32[]{:S(2)}) collective-permute-start(bf16[2,128,1024]{2,1,0:T(8,128)(2,1)S(1)} %pad_maximum_fusion.12.refs_0_), channel_id=1, source_target_pairs={{0,8},{4,12},{8,0},{12,4},{16,24},{20,28},{24,16},{28,20},{1,9},{5... | collective-permute-start | bytes 1572872 | tf_op jit(solution)/shard_map/ppermute | solution.py:332
  482.8 13.6 %collective-permute-start.53 = (bf16[2,128,1024]{2,1,0:T(8,128)(2,1)S(1)}, bf16[2,128,1024]{2,1,0:T(8,128)(2,1)S(1)}, u32[]{:S(2)}, u32[]{:S(2)}) collective-permute-start(bf16[2,128,1024]{2,1,0:T(8,128)(2,1)S(1)} %pad_maximum_fusion.13.refs_4_), channel_id=1, source_target_pairs={{0,4},{4,0},{8,12},{12,8},{16,20},{20,16},{24,28},{28,24},{1,5},{5... | collective-permute-start | bytes 1572872 | tf_op jit(solution)/shard_map/ppermute | solution.py:332
  487.1 10.8 %collective-permute-start.49 = (bf16[2,128,1024]{2,1,0:T(8,128)(2,1)S(1)}, bf16[2,128,1024]{2,1,0:T(8,128)(2,1)S(1)}, u32[]{:S(2)}, u32[]{:S(2)}) collective-permute-start(bf16[2,128,1024]{2,1,0:T(8,128)(2,1)S(1)} %pad_maximum_fusion.12.refs_0_), channel_id=1, source_target_pairs={{0,4},{4,0},{8,12},{12,8},{16,20},{20,16},{24,28},{28,24},{1,5},{5... | collective-permute-start | bytes 1572872 | tf_op jit(solution)/shard_map/ppermute | solution.py:332
  494.3 3.9 collective-permute-start.54
  496.4 8.0 %collective-permute-start.42 = (bf16[2,4,16,1024]{3,2,1,0:T(8,128)(2,1)S(1)}, bf16[2,4,16,1024]{3,2,1,0:T(8,128)(2,1)S(1)}, u32[]{:S(2)}, u32[]{:S(2)}) collective-permute-start(bf16[2,4,16,1024]{3,2,1,0:T(8,128)(2,1)S(1)} %pad_maximum_fusion.14.refs_0_), channel_id=1, source_target_pairs={{0,8},{4,12},{8,0},{12,4},{16,24},{20,28},{24,16},{28,20},{1,9},{5... | collective-permute-start | bytes 786440 | tf_op jit(solution)/shard_map/ppermute | solution.py:332
  497.9 12.2 %collective-permute-start.59 = (bf16[2,4,16,1024]{3,2,1,0:T(8,128)(2,1)S(1)}, bf16[2,4,16,1024]{3,2,1,0:T(8,128)(2,1)S(1)}, u32[]{:S(2)}, u32[]{:S(2)}) collective-permute-start(bf16[2,4,16,1024]{3,2,1,0:T(8,128)(2,1)S(1)} %pad_maximum_fusion.15.refs_4_), channel_id=1, source_target_pairs={{0,4},{4,0},{8,12},{12,8},{16,20},{20,16},{24,28},{28,24},{1,5},{5... | collective-permute-start | bytes 786440 | tf_op jit(solution)/shard_map/ppermute | solution.py:332
  498.2 11.9 %collective-permute-start.55 = (bf16[2,4,16,1024]{3,2,1,0:T(8,128)(2,1)S(1)}, bf16[2,4,16,1024]{3,2,1,0:T(8,128)(2,1)S(1)}, u32[]{:S(2)}, u32[]{:S(2)}) collective-permute-start(bf16[2,4,16,1024]{3,2,1,0:T(8,128)(2,1)S(1)} %pad_maximum_fusion.14.refs_0_), channel_id=1, source_target_pairs={{0,4},{4,0},{8,12},{12,8},{16,20},{20,16},{24,28},{28,24},{1,5},{5... | collective-permute-start | bytes 786440 | tf_op jit(solution)/shard_map/ppermute | solution.py:332
  503.1 7.0 %collective-permute-start.60 = (bf16[2,4,16,1024]{3,2,1,0:T(8,128)(2,1)S(1)}, bf16[2,4,16,1024]{3,2,1,0:T(8,128)(2,1)S(1)}, u32[]{:S(2)}, u32[]{:S(2)}) collective-permute-start(bf16[2,4,16,1024]{3,2,1,0:T(8,128)(2,1)S(1)} %collective-permute-done.58.refs_5_), channel_id=1, source_target_pairs={{0,4},{4,0},{8,12},{12,8},{16,20},{20,16},{24,28},{28,24},{1,5},{5... | collective-permute-start | bytes 786440 | tf_op jit(solution)/shard_map/ppermute | solution.py:332
  504.4 5.7 %collective-permute-start.56 = (bf16[2,4,16,1024]{3,2,1,0:T(8,128)(2,1)S(1)}, bf16[2,4,16,1024]{3,2,1,0:T(8,128)(2,1)S(1)}, u32[]{:S(2)}, u32[]{:S(2)}) collective-permute-start(bf16[2,4,16,1024]{3,2,1,0:T(8,128)(2,1)S(1)} %collective-permute-done.42.refs_1_), channel_id=1, source_target_pairs={{0,4},{4,0},{8,12},{12,8},{16,20},{20,16},{24,28},{28,24},{1,5},{5... | collective-permute-start | bytes 786440 | tf_op jit(solution)/shard_map/ppermute | solution.py:332
  (76 other events, 961.9 us)
Sparse Core Ops, SparseCore 0:
  22.5 51.4 all-gather.2
  390.5 47.3 reduce-scatter.1
